TPU v7x, 512 devices: a whole 4x4x16 slice. The times are simulated.
512 devices in a mesh: dom: 128 (over y, x_lo, z), sub: 4 (over x_hi, core).
Axes of the slice: x: 4 (x_hi: 2, x_lo: 2; x = x_hi * 2 + x_lo), y: 4, z: 16, core: 2. Of those that a mesh axis runs over, the one named last changes fastest.
Arguments:
- initial_field: float32 [64, 256, 1024], P(None, 'dom', 'sub'), may hold values from -6 to 6
- adjoint_source: float32 [64, 256, 1024], P(None, 'dom', 'sub'), may hold values from -6 to 6
- moduli: float32 [3, 64, 256, 1024], P(None, None, 'dom', 'sub'), may hold values from 0.5 to 2
- node_mass: float32 [64, 256, 1024], P(None, 'dom', 'sub'), may hold values from 1 to 4
- block_owner: int32 [256, 1024], P('dom', 'sub'), may hold values from 0 to 511
- spline_basis: float32 [64, 64], replicated, may hold values from -0.75 to 0.75
Outputs:
- forward_final: float32 [64, 256, 1024], P(None, 'dom', 'sub')
- adjoint_final: float32 [64, 256, 1024], P(None, 'dom', 'sub')
- kernel: float32 [64, 65536], P(None, ('dom', 'sub'))
Inputs may be any that keep to these rules, and one draw needn't show every extreme that they name: block_owner names a block of the element's own partition.
All inputs are finite; a program needn't handle non-finite values.
Results may differ from a plain program's by a relative error of at most 0.0001.
Values sent between devices are 32-bit elements; how exact they have to be, the bound alone decides.
No kernel may reach another device: no remote copies, remote signals or barrier semaphores. Data moves between devices by JAX's collectives and lax.ppermute only.
A program may use at most 64 MiB of HBM per device.

v0:
```python
import jax
import jax.numpy as jnp
import numpy as np
from jax import lax
from jax.sharding import PartitionSpec as P

NBLK_DEV = 128
STEPS = 4


DERIVATIVE = np.array(
    [
        [-3.0, 4.04508497187474, -1.54508497187474, 0.5],
        [-0.80901699437495, 0.0, 1.11803398874989, -0.30901699437495],
        [0.30901699437495, -1.11803398874989, 0.0, 0.80901699437495],
        [-0.5, 1.54508497187474, -4.04508497187474, 3.0],
    ]
)
IDENTITY_FOUR = np.eye(4)
GRADIENT_TABLE = np.concatenate(
    [
        np.kron(np.kron(DERIVATIVE, IDENTITY_FOUR), IDENTITY_FOUR),
        np.kron(np.kron(IDENTITY_FOUR, DERIVATIVE), IDENTITY_FOUR),
        np.kron(np.kron(IDENTITY_FOUR, IDENTITY_FOUR), DERIVATIVE),
    ],
    axis=0,
).astype(np.float32)
TIME_STEP = 0.1
KERNEL_SCALE = 0.05


def padded(block, sides, width):
    for axis, dim in sides:
        count = lax.axis_size(axis)
        forward = [(i, i + 1) for i in range(count - 1)]
        backward = [(target, source) for source, target in forward]
        low = lax.ppermute(
            lax.slice_in_dim(block, block.shape[dim] - width, None, axis=dim), axis, forward
        )
        high = lax.ppermute(lax.slice_in_dim(block, 0, width, axis=dim), axis, backward)
        block = jnp.concatenate([low, block, high], axis=dim)
    return block


def stiffness_apply(displace, moduli):
    fields = displace.shape[0]
    count = displace.shape[2] * displace.shape[3]
    flat = displace.reshape(fields, 64, count)
    gradients = jnp.einsum("gn,lnc->lgc", GRADIENT_TABLE, flat, precision=lax.Precision.HIGHEST)
    fluxes = moduli.reshape(1, 192, count) * gradients
    forces = jnp.einsum("gn,lgc->lnc", GRADIENT_TABLE, fluxes, precision=lax.Precision.HIGHEST)
    return (forces.reshape(displace.shape), gradients)


def merge_x(split_x, from_left, from_right):
    lower_face = split_x[:, 0]
    upper_face = split_x[:, 3]
    upper_prev = jnp.concatenate([from_left, upper_face[:, :, :-1]], axis=2)
    lower_next = jnp.concatenate([lower_face[:, :, 1:], from_right], axis=2)
    return jnp.concatenate(
        [(lower_face + upper_prev)[:, None], split_x[:, 1:3], (upper_face + lower_next)[:, None]],
        axis=1,
    )


def merge_y(split_y, from_below, from_above):
    lower_face = split_y[:, :, 0]
    upper_face = split_y[:, :, 3]
    upper_prev = jnp.concatenate([from_below, upper_face[..., :-1]], axis=4)
    lower_next = jnp.concatenate([lower_face[..., 1:], from_above], axis=4)
    return jnp.concatenate(
        [
            (lower_face + upper_prev)[:, :, None],
            split_y[:, :, 1:3],
            (upper_face + lower_next)[:, :, None],
        ],
        axis=2,
    )


def assemble(values):
    fields, rows_x, rows_y = (values.shape[0], values.shape[2], values.shape[3])
    split_x = values.reshape(fields, 4, 16, rows_x, rows_y)
    face_rims = jnp.concatenate(
        [split_x[:, 0][:, :, 0:1], split_x[:, 3][:, :, rows_x - 1 : rows_x]], axis=2
    )
    padded_x = padded(face_rims, (("dom", 2),), 1)
    merged = merge_x(split_x, padded_x[:, :, 0:1], padded_x[:, :, 3:4])
    split_y = merged.reshape(fields, 4, 4, 4, rows_x, rows_y)
    rims_y = jnp.concatenate(
        [split_y[:, :, 0][..., 0:1], split_y[:, :, 3][..., rows_y - 1 : rows_y]], axis=4
    )
    padded_y = padded(rims_y, (("sub", 4),), 1)
    merged_y = merge_y(split_y, padded_y[..., 0:1], padded_y[..., 3:4])
    return merged_y.reshape(fields, 64, rows_x, rows_y)


def run_steps(start, moduli, mass_total):
    displace = start
    velocity = jnp.zeros_like(start)
    saved = []
    for index_step in range(STEPS):
        forces, gradients = stiffness_apply(displace, moduli)
        saved.append(gradients)
        velocity = velocity - TIME_STEP * assemble(forces) / mass_total
        displace = displace + TIME_STEP * velocity
    return (displace, saved)


def on_device(initial_field, adjoint_source, moduli, node_mass, block_owner, spline_basis):
    rows_x, rows_y = (initial_field.shape[1], initial_field.shape[2])
    count = rows_x * rows_y
    mass_total = assemble(node_mass[None])
    forward_run, saved_fwd = run_steps(initial_field[None], moduli, mass_total)
    adjoint_run, saved_adj = run_steps(adjoint_source[None], moduli, mass_total)
    forward_final = forward_run[0]
    adjoint_final = adjoint_run[0]
    forward_saved = [grads[0] for grads in saved_fwd]
    adjoint_saved = [grads[0] for grads in saved_adj]
    last_grad = jnp.dot(
        GRADIENT_TABLE, forward_final.reshape(64, count), precision=lax.Precision.HIGHEST
    )
    partner = [last_grad] + [forward_saved[STEPS - m] for m in range(1, STEPS)]
    flat_moduli = moduli.reshape(192, count)
    density = jnp.zeros((64, count), jnp.float32)
    for m in range(STEPS):
        density = density + (flat_moduli * adjoint_saved[m] * partner[m]).reshape(3, 64, count).sum(
            axis=0
        )
    block_count = NBLK_DEV * lax.axis_size("sub")
    one_hot = (
        block_owner.reshape(count, 1) == jnp.arange(block_count, dtype=jnp.int32)[None, :]
    ).astype(jnp.float32)
    partial_sums = jnp.dot(density, one_hot, precision=lax.Precision.HIGHEST)
    projected = (
        jnp.dot(spline_basis.T, partial_sums, precision=lax.Precision.HIGHEST) * KERNEL_SCALE
    )
    kernel = lax.psum_scatter(projected, "sub", scatter_dimension=1, tiled=True)
    return (forward_final, adjoint_final, kernel)


def solution(mesh):
    in_specs = (
        P(None, "dom", "sub"),
        P(None, "dom", "sub"),
        P(None, None, "dom", "sub"),
        P(None, "dom", "sub"),
        P("dom", "sub"),
        P(),
    )
    out_specs = (P(None, "dom", "sub"), P(None, "dom", "sub"), P(None, ("dom", "sub")))
    return jax.shard_map(
        on_device, mesh=mesh, in_specs=in_specs, out_specs=out_specs, check_vma=False
    )
```

profile of v0, /device:TPU:25, one launch (start us, length us, event | category | flops | bytes accessed | tf_op | source)
XLA Modules:
  0.0 262.3 jit_solution(9852717418477235758)
XLA Ops:
  8.1 3.5 %collective-permute-start.4 = (f32[1,16,1,256]{3,2,1,0:T(1,128)S(1)}, f32[1,16,1,256]{3,2,1,0:T(1,128)S(1)}, u32[]{:S(2)}, u32[]{:S(2)}) collective-permute-start(f32[1,16,1,256]{3,2,1,0:T(1,128)S(1)} %get-tuple-element.89), channel_id=1, source_target_pairs={{0,4},{4,8},{8,12},{12,16},{16,20},{20,24},{24,28},{28,32},{32,36}... | collective-permute-start | bytes 49160 | tf_op jit(solution)/shard_map/ppermute | solution.py:37
  15.3 3.5 %collective-permute-start.20 = (f32[1,16,1,256]{3,2,1,0:T(1,128)S(1)}, f32[1,16,1,256]{3,2,1,0:T(1,128)S(1)}, u32[]{:S(2)}, u32[]{:S(2)}) collective-permute-start(f32[1,16,1,256]{3,2,1,0:T(1,128)S(1)} %get-tuple-element.69), channel_id=1, source_target_pairs={{0,4},{4,8},{8,12},{12,16},{16,20},{20,24},{24,28},{28,32},{32,36}... | collective-permute-start | bytes 49160 | tf_op jit(solution)/shard_map/ppermute | solution.py:37
  19.9 3.5 %collective-permute-start = (f32[1,16,1,256]{3,2,1,0:T(1,128)S(1)}, f32[1,16,1,256]{3,2,1,0:T(1,128)S(1)}, u32[]{:S(2)}, u32[]{:S(2)}) collective-permute-start(f32[1,16,1,256]{3,2,1,0:T(1,128)S(1)} %get-tuple-element.85), channel_id=1, source_target_pairs={{0,4},{4,8},{8,12},{12,16},{16,20},{20,24},{24,28},{28,32},{32,36}... | collective-permute-start | bytes 49160 | tf_op jit(solution)/shard_map/ppermute | solution.py:37
  23.6 7.4 %collective-permute-start.5 = (f32[1,16,1,256]{3,2,1,0:T(1,128)S(1)}, f32[1,16,1,256]{3,2,1,0:T(1,128)S(1)}, u32[]{:S(2)}, u32[]{:S(2)}) collective-permute-start(f32[1,16,1,256]{3,2,1,0:T(1,128)S(1)} %get-tuple-element.92), channel_id=1, source_target_pairs={{4,0},{8,4},{12,8},{16,12},{20,16},{24,20},{28,24},{32,28},{36,32}... | collective-permute-start | bytes 49160 | tf_op jit(solution)/shard_map/ppermute | solution.py:40
  31.0 3.4 %collective-permute-start.21 = (f32[1,16,1,256]{3,2,1,0:T(1,128)S(1)}, f32[1,16,1,256]{3,2,1,0:T(1,128)S(1)}, u32[]{:S(2)}, u32[]{:S(2)}) collective-permute-start(f32[1,16,1,256]{3,2,1,0:T(1,128)S(1)} %get-tuple-element.72), channel_id=1, source_target_pairs={{4,0},{8,4},{12,8},{16,12},{20,16},{24,20},{28,24},{32,28},{36,32}... | collective-permute-start | bytes 49160 | tf_op jit(solution)/shard_map/ppermute | solution.py:40
  34.5 3.4 %collective-permute-start.1 = (f32[1,16,1,256]{3,2,1,0:T(1,128)S(1)}, f32[1,16,1,256]{3,2,1,0:T(1,128)S(1)}, u32[]{:S(2)}, u32[]{:S(2)}) collective-permute-start(f32[1,16,1,256]{3,2,1,0:T(1,128)S(1)} %get-tuple-element.88), channel_id=1, source_target_pairs={{4,0},{8,4},{12,8},{16,12},{20,16},{24,20},{28,24},{32,28},{36,32}... | collective-permute-start | bytes 49160 | tf_op jit(solution)/shard_map/ppermute | solution.py:40
  38.3 6.3 %collective-permute-start.6 = (f32[1,4,4,2,1]{4,3,2,1,0:T(2,128)S(1)}, f32[1,4,4,2,1]{4,3,2,1,0:T(2,128)S(1)}, u32[]{:S(2)}, u32[]{:S(2)}) collective-permute-start(f32[1,4,4,2,1]{4,3,2,1,0:T(2,128)S(1)} %slice.558), channel_id=1, source_target_pairs={{0,1},{1,2},{2,3},{4,5},{5,6},{6,7},{8,9},{9,10},{10,11},{12,13},{... | collective-permute-start | bytes 392 | tf_op jit(solution)/shard_map/ppermute | solution.py:37
  63.2 5.3 %collective-permute-done.24 = f32[1,16,1,256]{3,2,1,0:T(1,128)S(1)} collective-permute-done((f32[1,16,1,256]{3,2,1,0:T(1,128)S(1)}, f32[1,16,1,256]{3,2,1,0:T(1,128)S(1)}, u32[]{:S(2)}, u32[]{:S(2)}) %collective-permute-start.24) | collective-permute-done | bytes 16416 | tf_op jit(solution)/shard_map/ppermute | solution.py:37
  73.2 4.7 %collective-permute-start.26 = (f32[1,4,4,2,1]{4,3,2,1,0:T(2,128)S(1)}, f32[1,4,4,2,1]{4,3,2,1,0:T(2,128)S(1)}, u32[]{:S(2)}, u32[]{:S(2)}) collective-permute-start(f32[1,4,4,2,1]{4,3,2,1,0:T(2,128)S(1)} %slice.613), channel_id=1, source_target_pairs={{0,1},{1,2},{2,3},{4,5},{5,6},{6,7},{8,9},{9,10},{10,11},{12,13},{... | collective-permute-start | bytes 392 | tf_op jit(solution)/shard_map/ppermute | solution.py:37
  81.2 5.1 %collective-permute-done.27 = f32[1,4,4,2,1]{4,3,2,1,0:T(2,128)S(1)} collective-permute-done((f32[1,4,4,2,1]{4,3,2,1,0:T(2,128)S(1)}, f32[1,4,4,2,1]{4,3,2,1,0:T(2,128)S(1)}, u32[]{:S(2)}, u32[]{:S(2)}) %collective-permute-start.27) | collective-permute-done | bytes 160 | tf_op jit(solution)/shard_map/ppermute | solution.py:40
  91.7 3.7 %collective-permute-done.28 = f32[1,16,1,256]{3,2,1,0:T(1,128)S(1)} collective-permute-done((f32[1,16,1,256]{3,2,1,0:T(1,128)S(1)}, f32[1,16,1,256]{3,2,1,0:T(1,128)S(1)}, u32[]{:S(2)}, u32[]{:S(2)}) %collective-permute-start.28) | collective-permute-done | bytes 16416 | tf_op jit(solution)/shard_map/ppermute | solution.py:37
  100.2 4.2 %collective-permute-start.30 = (f32[1,4,4,2,1]{4,3,2,1,0:T(2,128)S(1)}, f32[1,4,4,2,1]{4,3,2,1,0:T(2,128)S(1)}, u32[]{:S(2)}, u32[]{:S(2)}) collective-permute-start(f32[1,4,4,2,1]{4,3,2,1,0:T(2,128)S(1)} %slice.624), channel_id=1, source_target_pairs={{0,1},{1,2},{2,3},{4,5},{5,6},{6,7},{8,9},{9,10},{10,11},{12,13},{... | collective-permute-start | bytes 392 | tf_op jit(solution)/shard_map/ppermute | solution.py:37
  107.7 5.1 %collective-permute-done.31 = f32[1,4,4,2,1]{4,3,2,1,0:T(2,128)S(1)} collective-permute-done((f32[1,4,4,2,1]{4,3,2,1,0:T(2,128)S(1)}, f32[1,4,4,2,1]{4,3,2,1,0:T(2,128)S(1)}, u32[]{:S(2)}, u32[]{:S(2)}) %collective-permute-start.31) | collective-permute-done | bytes 160 | tf_op jit(solution)/shard_map/ppermute | solution.py:40
  123.9 3.5 %collective-permute-start.33 = (f32[1,16,1,256]{3,2,1,0:T(1,128)S(1)}, f32[1,16,1,256]{3,2,1,0:T(1,128)S(1)}, u32[]{:S(2)}, u32[]{:S(2)}) collective-permute-start(f32[1,16,1,256]{3,2,1,0:T(1,128)S(1)} %get-tuple-element.60), channel_id=1, source_target_pairs={{4,0},{8,4},{12,8},{16,12},{20,16},{24,20},{28,24},{32,28},{36,32}... | collective-permute-start | bytes 49160 | tf_op jit(solution)/shard_map/ppermute | solution.py:40
  127.5 3.4 %collective-permute-start.9 = (f32[1,16,1,256]{3,2,1,0:T(1,128)S(1)}, f32[1,16,1,256]{3,2,1,0:T(1,128)S(1)}, u32[]{:S(2)}, u32[]{:S(2)}) collective-permute-start(f32[1,16,1,256]{3,2,1,0:T(1,128)S(1)} %get-tuple-element.84), channel_id=1, source_target_pairs={{4,0},{8,4},{12,8},{16,12},{20,16},{24,20},{28,24},{32,28},{36,32}... | collective-permute-start | bytes 49160 | tf_op jit(solution)/shard_map/ppermute | solution.py:40
  133.7 3.4 %collective-permute-start.34 = (f32[1,4,4,2,1]{4,3,2,1,0:T(2,128)S(1)}, f32[1,4,4,2,1]{4,3,2,1,0:T(2,128)S(1)}, u32[]{:S(2)}, u32[]{:S(2)}) collective-permute-start(f32[1,4,4,2,1]{4,3,2,1,0:T(2,128)S(1)} %slice.635), channel_id=1, source_target_pairs={{0,1},{1,2},{2,3},{4,5},{5,6},{6,7},{8,9},{9,10},{10,11},{12,13},{... | collective-permute-start | bytes 392 | tf_op jit(solution)/shard_map/ppermute | solution.py:37
  150.5 3.4 %collective-permute-done.11 = f32[1,4,4,2,1]{4,3,2,1,0:T(2,128)S(1)} collective-permute-done((f32[1,4,4,2,1]{4,3,2,1,0:T(2,128)S(1)}, f32[1,4,4,2,1]{4,3,2,1,0:T(2,128)S(1)}, u32[]{:S(2)}, u32[]{:S(2)}) %collective-permute-start.11) | collective-permute-done | bytes 160 | tf_op jit(solution)/shard_map/ppermute | solution.py:40
  159.9 4.8 %collective-permute-done.12 = f32[1,16,1,256]{3,2,1,0:T(1,128)S(1)} collective-permute-done((f32[1,16,1,256]{3,2,1,0:T(1,128)S(1)}, f32[1,16,1,256]{3,2,1,0:T(1,128)S(1)}, u32[]{:S(2)}, u32[]{:S(2)}) %collective-permute-start.12) | collective-permute-done | bytes 16416 | tf_op jit(solution)/shard_map/ppermute | solution.py:37
  169.4 4.3 %collective-permute-start.14 = (f32[1,4,4,2,1]{4,3,2,1,0:T(2,128)S(1)}, f32[1,4,4,2,1]{4,3,2,1,0:T(2,128)S(1)}, u32[]{:S(2)}, u32[]{:S(2)}) collective-permute-start(f32[1,4,4,2,1]{4,3,2,1,0:T(2,128)S(1)} %slice.580), channel_id=1, source_target_pairs={{0,1},{1,2},{2,3},{4,5},{5,6},{6,7},{8,9},{9,10},{10,11},{12,13},{... | collective-permute-start | bytes 392 | tf_op jit(solution)/shard_map/ppermute | solution.py:37
  178.4 4.5 %collective-permute-done.15 = f32[1,4,4,2,1]{4,3,2,1,0:T(2,128)S(1)} collective-permute-done((f32[1,4,4,2,1]{4,3,2,1,0:T(2,128)S(1)}, f32[1,4,4,2,1]{4,3,2,1,0:T(2,128)S(1)}, u32[]{:S(2)}, u32[]{:S(2)}) %collective-permute-start.15) | collective-permute-done | bytes 160 | tf_op jit(solution)/shard_map/ppermute | solution.py:40
  194.4 3.5 %collective-permute-done.16 = f32[1,16,1,256]{3,2,1,0:T(1,128)} collective-permute-done((f32[1,16,1,256]{3,2,1,0:T(1,128)}, f32[1,16,1,256]{3,2,1,0:T(1,128)}, u32[]{:S(2)}, u32[]{:S(2)}) %collective-permute-start.16) | collective-permute-done | bytes 16416 | tf_op jit(solution)/shard_map/ppermute | solution.py:37
  203.4 4.2 %collective-permute-start.18 = (f32[1,4,4,2,1]{4,3,2,1,0:T(2,128)S(1)}, f32[1,4,4,2,1]{4,3,2,1,0:T(2,128)S(1)}, u32[]{:S(2)}, u32[]{:S(2)}) collective-permute-start(f32[1,4,4,2,1]{4,3,2,1,0:T(2,128)S(1)} %slice.591), channel_id=1, source_target_pairs={{0,1},{1,2},{2,3},{4,5},{5,6},{6,7},{8,9},{9,10},{10,11},{12,13},{... | collective-permute-start | bytes 392 | tf_op jit(solution)/shard_map/ppermute | solution.py:37
  211.0 5.1 %collective-permute-done.19 = f32[1,4,4,2,1]{4,3,2,1,0:T(2,128)S(1)} collective-permute-done((f32[1,4,4,2,1]{4,3,2,1,0:T(2,128)S(1)}, f32[1,4,4,2,1]{4,3,2,1,0:T(2,128)S(1)}, u32[]{:S(2)}, u32[]{:S(2)}) %collective-permute-start.19) | collective-permute-done | bytes 160 | tf_op jit(solution)/shard_map/ppermute | solution.py:40
  223.8 31.6 %reduce-scatter.2.cloned.1.call-done = f32[64,128]{1,0:T(8,128)} async-done(((f32[64,512]{1,0:T(8,128)}), f32[64,128]{1,0:T(8,128)}) %reduce-scatter.2.cloned.1.call-update) | async-done | bytes 32784 | tf_op jit(solution)/shard_map/reduce_scatter | solution.py:138
  (335 shorter events, 115.7 us)
Async XLA Ops:
  7.2 248.2 %reduce-scatter.2.cloned.1.call-start = ((), (), s32[]{:S(2)}) async-start(), calls=%async_computation.1 | async-start | bytes 163840 | tf_op jit(solution)/shard_map/reduce_scatter | solution.py:138
  8.1 15.4 %collective-permute-start.4 = (f32[1,16,1,256]{3,2,1,0:T(1,128)S(1)}, f32[1,16,1,256]{3,2,1,0:T(1,128)S(1)}, u32[]{:S(2)}, u32[]{:S(2)}) collective-permute-start(f32[1,16,1,256]{3,2,1,0:T(1,128)S(1)} %get-tuple-element.89), channel_id=1, source_target_pairs={{0,4},{4,8},{8,12},{12,16},{16,20},{20,24},{24,28},{28,32},{32,36}... | collective-permute-start | bytes 49160 | tf_op jit(solution)/shard_map/ppermute | solution.py:37
  15.3 15.7 %collective-permute-start.20 = (f32[1,16,1,256]{3,2,1,0:T(1,128)S(1)}, f32[1,16,1,256]{3,2,1,0:T(1,128)S(1)}, u32[]{:S(2)}, u32[]{:S(2)}) collective-permute-start(f32[1,16,1,256]{3,2,1,0:T(1,128)S(1)} %get-tuple-element.69), channel_id=1, source_target_pairs={{0,4},{4,8},{8,12},{12,16},{16,20},{20,24},{24,28},{28,32},{32,36}... | collective-permute-start | bytes 49160 | tf_op jit(solution)/shard_map/ppermute | solution.py:37
  19.9 14.5 %collective-permute-start = (f32[1,16,1,256]{3,2,1,0:T(1,128)S(1)}, f32[1,16,1,256]{3,2,1,0:T(1,128)S(1)}, u32[]{:S(2)}, u32[]{:S(2)}) collective-permute-start(f32[1,16,1,256]{3,2,1,0:T(1,128)S(1)} %get-tuple-element.85), channel_id=1, source_target_pairs={{0,4},{4,8},{8,12},{12,16},{16,20},{20,24},{24,28},{28,32},{32,36}... | collective-permute-start | bytes 49160 | tf_op jit(solution)/shard_map/ppermute | solution.py:37
  23.6 14.3 %collective-permute-start.5 = (f32[1,16,1,256]{3,2,1,0:T(1,128)S(1)}, f32[1,16,1,256]{3,2,1,0:T(1,128)S(1)}, u32[]{:S(2)}, u32[]{:S(2)}) collective-permute-start(f32[1,16,1,256]{3,2,1,0:T(1,128)S(1)} %get-tuple-element.92), channel_id=1, source_target_pairs={{4,0},{8,4},{12,8},{16,12},{20,16},{24,20},{28,24},{32,28},{36,32}... | collective-permute-start | bytes 49160 | tf_op jit(solution)/shard_map/ppermute | solution.py:40
  31.0 7.0 %collective-permute-start.21 = (f32[1,16,1,256]{3,2,1,0:T(1,128)S(1)}, f32[1,16,1,256]{3,2,1,0:T(1,128)S(1)}, u32[]{:S(2)}, u32[]{:S(2)}) collective-permute-start(f32[1,16,1,256]{3,2,1,0:T(1,128)S(1)} %get-tuple-element.72), channel_id=1, source_target_pairs={{4,0},{8,4},{12,8},{16,12},{20,16},{24,20},{28,24},{32,28},{36,32}... | collective-permute-start | bytes 49160 | tf_op jit(solution)/shard_map/ppermute | solution.py:40
  34.5 12.0 %collective-permute-start.1 = (f32[1,16,1,256]{3,2,1,0:T(1,128)S(1)}, f32[1,16,1,256]{3,2,1,0:T(1,128)S(1)}, u32[]{:S(2)}, u32[]{:S(2)}) collective-permute-start(f32[1,16,1,256]{3,2,1,0:T(1,128)S(1)} %get-tuple-element.88), channel_id=1, source_target_pairs={{4,0},{8,4},{12,8},{16,12},{20,16},{24,20},{28,24},{32,28},{36,32}... | collective-permute-start | bytes 49160 | tf_op jit(solution)/shard_map/ppermute | solution.py:40
  38.3 10.3 %collective-permute-start.6 = (f32[1,4,4,2,1]{4,3,2,1,0:T(2,128)S(1)}, f32[1,4,4,2,1]{4,3,2,1,0:T(2,128)S(1)}, u32[]{:S(2)}, u32[]{:S(2)}) collective-permute-start(f32[1,4,4,2,1]{4,3,2,1,0:T(2,128)S(1)} %slice.558), channel_id=1, source_target_pairs={{0,1},{1,2},{2,3},{4,5},{5,6},{6,7},{8,9},{9,10},{10,11},{12,13},{... | collective-permute-start | bytes 392 | tf_op jit(solution)/shard_map/ppermute | solution.py:37
  44.6 6.9 %collective-permute-start.22 = (f32[1,4,4,2,1]{4,3,2,1,0:T(2,128)S(1)}, f32[1,4,4,2,1]{4,3,2,1,0:T(2,128)S(1)}, u32[]{:S(2)}, u32[]{:S(2)}) collective-permute-start(f32[1,4,4,2,1]{4,3,2,1,0:T(2,128)S(1)} %slice.602), channel_id=1, source_target_pairs={{0,1},{1,2},{2,3},{4,5},{5,6},{6,7},{8,9},{9,10},{10,11},{12,13},{... | collective-permute-start | bytes 392 | tf_op jit(solution)/shard_map/ppermute | solution.py:37
  46.7 16.3 %collective-permute-start.2 = (f32[1,4,4,2,1]{4,3,2,1,0:T(2,128)S(1)}, f32[1,4,4,2,1]{4,3,2,1,0:T(2,128)S(1)}, u32[]{:S(2)}, u32[]{:S(2)}) collective-permute-start(f32[1,4,4,2,1]{4,3,2,1,0:T(2,128)S(1)} %slice.547), channel_id=1, source_target_pairs={{0,1},{1,2},{2,3},{4,5},{5,6},{6,7},{8,9},{9,10},{10,11},{12,13},{... | collective-permute-start | bytes 392 | tf_op jit(solution)/shard_map/ppermute | solution.py:37
  61.0 7.5 %collective-permute-start.24 = (f32[1,16,1,256]{3,2,1,0:T(1,128)S(1)}, f32[1,16,1,256]{3,2,1,0:T(1,128)S(1)}, u32[]{:S(2)}, u32[]{:S(2)}) collective-permute-start(f32[1,16,1,256]{3,2,1,0:T(1,128)S(1)} %get-tuple-element.65), channel_id=1, source_target_pairs={{0,4},{4,8},{8,12},{12,16},{16,20},{20,24},{24,28},{28,32},{32,36}... | collective-permute-start | bytes 49160 | tf_op jit(solution)/shard_map/ppermute | solution.py:37
  70.6 20.8 %collective-permute-start.3 = (f32[1,4,4,2,1]{4,3,2,1,0:T(2,128)S(1)}, f32[1,4,4,2,1]{4,3,2,1,0:T(2,128)S(1)}, u32[]{:S(2)}, u32[]{:S(2)}) collective-permute-start(f32[1,4,4,2,1]{4,3,2,1,0:T(2,128)S(1)} %slice.550), channel_id=1, source_target_pairs={{1,0},{2,1},{3,2},{5,4},{6,5},{7,6},{9,8},{10,9},{11,10},{13,12},{... | collective-permute-start | bytes 392 | tf_op jit(solution)/shard_map/ppermute | solution.py:40
  79.1 7.1 %collective-permute-start.27 = (f32[1,4,4,2,1]{4,3,2,1,0:T(2,128)S(1)}, f32[1,4,4,2,1]{4,3,2,1,0:T(2,128)S(1)}, u32[]{:S(2)}, u32[]{:S(2)}) collective-permute-start(f32[1,4,4,2,1]{4,3,2,1,0:T(2,128)S(1)} %slice.616), channel_id=1, source_target_pairs={{1,0},{2,1},{3,2},{5,4},{6,5},{7,6},{9,8},{10,9},{11,10},{13,12},{... | collective-permute-start | bytes 392 | tf_op jit(solution)/shard_map/ppermute | solution.py:40
  88.0 7.5 %collective-permute-start.28 = (f32[1,16,1,256]{3,2,1,0:T(1,128)S(1)}, f32[1,16,1,256]{3,2,1,0:T(1,128)S(1)}, u32[]{:S(2)}, u32[]{:S(2)}) collective-permute-start(f32[1,16,1,256]{3,2,1,0:T(1,128)S(1)} %get-tuple-element.61), channel_id=1, source_target_pairs={{0,4},{4,8},{8,12},{12,16},{16,20},{20,24},{24,28},{28,32},{32,36}... | collective-permute-start | bytes 49160 | tf_op jit(solution)/shard_map/ppermute | solution.py:37
  105.6 7.1 %collective-permute-start.31 = (f32[1,4,4,2,1]{4,3,2,1,0:T(2,128)S(1)}, f32[1,4,4,2,1]{4,3,2,1,0:T(2,128)S(1)}, u32[]{:S(2)}, u32[]{:S(2)}) collective-permute-start(f32[1,4,4,2,1]{4,3,2,1,0:T(2,128)S(1)} %slice.627), channel_id=1, source_target_pairs={{1,0},{2,1},{3,2},{5,4},{6,5},{7,6},{9,8},{10,9},{11,10},{13,12},{... | collective-permute-start | bytes 392 | tf_op jit(solution)/shard_map/ppermute | solution.py:40
  115.3 7.8 %collective-permute-start.32 = (f32[1,16,1,256]{3,2,1,0:T(1,128)}, f32[1,16,1,256]{3,2,1,0:T(1,128)}, u32[]{:S(2)}, u32[]{:S(2)}) collective-permute-start(f32[1,16,1,256]{3,2,1,0:T(1,128)} %get-tuple-element.57), channel_id=1, source_target_pairs={{0,4},{4,8},{8,12},{12,16},{16,20},{20,24},{24,28},{28,32},{32,36}... | collective-permute-start | bytes 49160 | tf_op jit(solution)/shard_map/ppermute | solution.py:37
  118.3 9.1 %collective-permute-start.8 = (f32[1,16,1,256]{3,2,1,0:T(1,128)S(1)}, f32[1,16,1,256]{3,2,1,0:T(1,128)S(1)}, u32[]{:S(2)}, u32[]{:S(2)}) collective-permute-start(f32[1,16,1,256]{3,2,1,0:T(1,128)S(1)} %get-tuple-element.81), channel_id=1, source_target_pairs={{0,4},{4,8},{8,12},{12,16},{16,20},{20,24},{24,28},{28,32},{32,36}... | collective-permute-start | bytes 49160 | tf_op jit(solution)/shard_map/ppermute | solution.py:37
  123.9 7.0 %collective-permute-start.33 = (f32[1,16,1,256]{3,2,1,0:T(1,128)S(1)}, f32[1,16,1,256]{3,2,1,0:T(1,128)S(1)}, u32[]{:S(2)}, u32[]{:S(2)}) collective-permute-start(f32[1,16,1,256]{3,2,1,0:T(1,128)S(1)} %get-tuple-element.60), channel_id=1, source_target_pairs={{4,0},{8,4},{12,8},{16,12},{20,16},{24,20},{28,24},{32,28},{36,32}... | collective-permute-start | bytes 49160 | tf_op jit(solution)/shard_map/ppermute | solution.py:40
  137.1 7.7 %collective-permute-start.10 = (f32[1,4,4,2,1]{4,3,2,1,0:T(2,128)}, f32[1,4,4,2,1]{4,3,2,1,0:T(2,128)}, u32[]{:S(2)}, u32[]{:S(2)}) collective-permute-start(f32[1,4,4,2,1]{4,3,2,1,0:T(2,128)} %slice.569), channel_id=1, source_target_pairs={{0,1},{1,2},{2,3},{4,5},{5,6},{6,7},{8,9},{9,10},{10,11},{12,13},{... | collective-permute-start | bytes 392 | tf_op jit(solution)/shard_map/ppermute | solution.py:37
  141.8 7.7 %collective-permute-start.35 = (f32[1,4,4,2,1]{4,3,2,1,0:T(2,128)}, f32[1,4,4,2,1]{4,3,2,1,0:T(2,128)}, u32[]{:S(2)}, u32[]{:S(2)}) collective-permute-start(f32[1,4,4,2,1]{4,3,2,1,0:T(2,128)} %slice.638), channel_id=1, source_target_pairs={{1,0},{2,1},{3,2},{5,4},{6,5},{7,6},{9,8},{10,9},{11,10},{13,12},{... | collective-permute-start | bytes 392 | tf_op jit(solution)/shard_map/ppermute | solution.py:40
  157.2 7.5 %collective-permute-start.12 = (f32[1,16,1,256]{3,2,1,0:T(1,128)S(1)}, f32[1,16,1,256]{3,2,1,0:T(1,128)S(1)}, u32[]{:S(2)}, u32[]{:S(2)}) collective-permute-start(f32[1,16,1,256]{3,2,1,0:T(1,128)S(1)} %get-tuple-element.77), channel_id=1, source_target_pairs={{0,4},{4,8},{8,12},{12,16},{16,20},{20,24},{24,28},{28,32},{32,36}... | collective-permute-start | bytes 49160 | tf_op jit(solution)/shard_map/ppermute | solution.py:37
  175.7 7.3 %collective-permute-start.15 = (f32[1,4,4,2,1]{4,3,2,1,0:T(2,128)S(1)}, f32[1,4,4,2,1]{4,3,2,1,0:T(2,128)S(1)}, u32[]{:S(2)}, u32[]{:S(2)}) collective-permute-start(f32[1,4,4,2,1]{4,3,2,1,0:T(2,128)S(1)} %slice.583), channel_id=1, source_target_pairs={{1,0},{2,1},{3,2},{5,4},{6,5},{7,6},{9,8},{10,9},{11,10},{13,12},{... | collective-permute-start | bytes 392 | tf_op jit(solution)/shard_map/ppermute | solution.py:40
  190.1 7.8 %collective-permute-start.16 = (f32[1,16,1,256]{3,2,1,0:T(1,128)}, f32[1,16,1,256]{3,2,1,0:T(1,128)}, u32[]{:S(2)}, u32[]{:S(2)}) collective-permute-start(f32[1,16,1,256]{3,2,1,0:T(1,128)} %get-tuple-element.73), channel_id=1, source_target_pairs={{0,4},{4,8},{8,12},{12,16},{16,20},{20,24},{24,28},{28,32},{32,36}... | collective-permute-start | bytes 49160 | tf_op jit(solution)/shard_map/ppermute | solution.py:37
  208.8 7.3 %collective-permute-start.19 = (f32[1,4,4,2,1]{4,3,2,1,0:T(2,128)S(1)}, f32[1,4,4,2,1]{4,3,2,1,0:T(2,128)S(1)}, u32[]{:S(2)}, u32[]{:S(2)}) collective-permute-start(f32[1,4,4,2,1]{4,3,2,1,0:T(2,128)S(1)} %slice.594), channel_id=1, source_target_pairs={{1,0},{2,1},{3,2},{5,4},{6,5},{7,6},{9,8},{10,9},{11,10},{13,12},{... | collective-permute-start | bytes 392 | tf_op jit(solution)/shard_map/ppermute | solution.py:40
  (49 other events, 378.4 us)
Sparse Core Ops, SparseCore 0:
  222.3 33.0 reduce-scatter.1
where the time goes:
time: 265 us; the launch traced here: 262 us
  starting transfers between devices  107 us (40%)
  waiting for transfers between devices  87.5 us (33%)
  local copies, waits for them, and re-layouts  29.4 us (11%)
  between operations  15.7 us (6%)
  other arithmetic  12.6 us (5%)
  matrix products  9.63 us (4%)
    ppermute x18, starting transfers between devices, padded(): lax.ppermute(lax.slice_in_dim(block, block.shape[dim] - width, None, axis...  57.2 us
    ppermute x18, starting transfers between devices, padded(): lax.ppermute(lax.slice_in_dim(block, 0, width, axis=dim), axis, backward)  50.1 us
    ppermute x18, waiting for transfers between devices, padded(): lax.ppermute(lax.slice_in_dim(block, 0, width, axis=dim), axis, backward)  32.3 us
    reduce_scatter x1, waiting for transfers between devices, on_device(): kernel = lax.psum_scatter(projected, 'sub', scatter_dimension=1, tiled=True)  31.6 us
    ppermute x18, waiting for transfers between devices, padded(): lax.ppermute(lax.slice_in_dim(block, block.shape[dim] - width, None, axis...  23.6 us
    unnamed x83, local copies, waits for them, and re-layouts  12.3 us
  transfers between devices with their start and end apart: 37, of which 21 were waited for; matrix products, arithmetic and copies ran while one was open for 9% of the time, Pallas kernels for 0%

commit v1 on v0

v1 whole, which is shorter than its diff:
```python
import jax
import jax.numpy as jnp
import numpy as np
from jax import lax
from jax.experimental import pallas as pl
from jax.experimental.pallas import tpu as pltpu
from jax.sharding import PartitionSpec as P

STEPS = 4
TIME_STEP = 0.1
KERNEL_SCALE = 0.05
PUSH = TIME_STEP * TIME_STEP

DERIVATIVE = np.array(
    [
        [-3.0, 4.04508497187474, -1.54508497187474, 0.5],
        [-0.80901699437495, 0.0, 1.11803398874989, -0.30901699437495],
        [0.30901699437495, -1.11803398874989, 0.0, 0.80901699437495],
        [-0.5, 1.54508497187474, -4.04508497187474, 3.0],
    ]
)
IDENTITY_FOUR = np.eye(4)
GRADIENT_TABLE = np.concatenate(
    [
        np.kron(np.kron(DERIVATIVE, IDENTITY_FOUR), IDENTITY_FOUR),
        np.kron(np.kron(IDENTITY_FOUR, DERIVATIVE), IDENTITY_FOUR),
        np.kron(np.kron(IDENTITY_FOUR, IDENTITY_FOUR), DERIVATIVE),
    ],
    axis=0,
).astype(np.float32)

HALF_AMB = float((DERIVATIVE[0, 1] - DERIVATIVE[0, 2]) / 2)
HALF_CME = float((DERIVATIVE[1, 0] - DERIVATIVE[1, 3]) / 2)
HALF_D = float(DERIVATIVE[1, 2] / 2)

RAW, FAR, MFAR, ZST, SFAR, SMFAR, MSG = 0, 96, 104, 112, 120, 122, 124
MSG_B = 20


def sub_iota():
    return lax.broadcasted_iota(jnp.int32, (8, 128), 0)


def lane_iota(rows=8):
    return lax.broadcasted_iota(jnp.int32, (rows, 128), 1)


def rs(x, shift):
    return pltpu.roll(x, shift, 0)


def rl(x, shift):
    return pltpu.roll(x, shift, 1)


def masks():
    s = sub_iota()
    lane = lane_iota()
    return dict(
        even=(s % 2) == 0,
        lo=s < 4,
        ct0=((s // 2) % 2) == 0,
        first=lane == 0,
        last=lane == 127,
    )


def d_line(x0, x1, x2, x3):
    p, m, q, n = x0 + x3, x0 - x3, x1 + x2, x1 - x2
    r = q - p
    s1 = -1.75 * m + HALF_AMB * n
    s2 = HALF_CME * m - HALF_D * n
    r1, r2 = 1.25 * r, HALF_D * r
    return s1 + r1, s2 + r2, s2 - r2, s1 - r1


def dt_line(x0, x1, x2, x3):
    p, m, q, n = x0 + x3, x0 - x3, x1 + x2, x1 - x2
    t = 1.25 * m + HALF_D * n
    q1 = HALF_CME * q - 1.75 * p
    q2 = HALF_AMB * p - HALF_D * q
    return q1 - t, t + q2, t - q2, -(q1 + t)


def line_nodes(direction, a, b):
    if direction == 0:
        return [16 * i + 4 * a + b for i in range(4)]
    if direction == 1:
        return [16 * a + 4 * j + b for j in range(4)]
    return [16 * a + 4 * b + k for k in range(4)]


def node_moduli(mod, h, g, mk):
    x = mod[h, g // 2]
    if g % 2 == 0:
        return jnp.where(mk["lo"], x, rs(x, 4))
    return jnp.where(mk["lo"], rs(x, 4), x)


def forces(u, f, mod, h, mk):
    for direction in (2, 1, 0):
        for a in range(4):
            for b in range(4):
                nodes = line_nodes(direction, a, b)
                g = d_line(*[u[h, n] for n in nodes])
                t = [
                    node_moduli(mod, h, 64 * direction + n, mk) * gn for n, gn in zip(nodes, g)
                ]
                out = dt_line(*t)
                for n, o in zip(nodes, out):
                    f[h, n] = o if direction == 2 else f[h, n] + o


def far_pack(f, mk):
    left, right = [], []
    for p in range(8):
        left.append(jnp.where(mk["even"], rs(f(2 * p), 7), f(2 * p + 1)))
        right.append(jnp.where(mk["even"], f(48 + 2 * p), rs(f(48 + 2 * p + 1), 1)))
    return left, right


def x_assemble(f, mk, from_right=None, from_left=None, base=0):
    even = mk["even"]
    for q in range(16):
        ao, bo, a_s, b_s = f[0, 48 + q], f[0, q], f[1, 48 + q], f[1, q]
        f[0, 48 + q] = ao + jnp.where(even, rs(bo, 7), rs(b_s, 1))
        f[0, q] = bo + jnp.where(even, rs(a_s, 7), rs(ao, 1))
        if from_right is not None:
            fr, fl = from_right[base + q // 2], from_left[base + q // 2]
            if q % 2 == 0:
                fl = rs(fl, 1)
            else:
                fr = rs(fr, 7)
            f[1, 48 + q] = a_s + jnp.where(even, fr, rs(bo, 1))
            f[1, q] = b_s + jnp.where(even, rs(ao, 7), fl)


def y_assemble(f, strip, h, mk):
    shift = 4 if h else 68
    for i in range(4):
        for k in range(4):
            na, nb = 16 * i + 12 + k, 16 * i + k
            inj_low = pltpu.roll(
                jnp.broadcast_to(strip[na : na + 1, :], (8, 128)), shift, 1, stride=8, stride_axis=0
            )
            inj_high = pltpu.roll(
                jnp.broadcast_to(strip[nb : nb + 1, :], (8, 128)), shift, 1, stride=8, stride_axis=0
            )
            a, b = f[h, na], f[h, nb]
            up, down = rl(b, 127), rl(a, 1)
            up = jnp.where(mk["last"], jnp.where(mk["ct0"], rs(up, 6), inj_high), up)
            down = jnp.where(mk["first"], jnp.where(mk["ct0"], inj_low, rs(down, 2)), down)
            f[h, na] = a + up
            f[h, nb] = b + down


def update(u, v, f, inv, h, first=False):
    for n in range(64):
        push = inv[h, n] * f[h, n]
        vel = -push if first else v[h, n] - push
        v[h, n] = vel
        u[h, n] = u[h, n] + vel


def strip_forces(us, mods, table, table_t):
    g = jnp.dot(table, us, precision=lax.Precision.HIGHEST, preferred_element_type=jnp.float32)
    return jnp.dot(
        table_t, mods * g, precision=lax.Precision.HIGHEST, preferred_element_type=jnp.float32
    )


def strip_x(f, far_right, far_left):
    lane = lane_iota(16)
    even, own = ((lane // 8) % 2) == 1, lane < 64
    b, a = f[0:16], f[48:64]
    na = a + jnp.where(even, jnp.where(own, rl(b, 8), rl(far_right, 72)), rl(b, 56))
    nb = b + jnp.where(even, rl(a, 72), jnp.where(own, rl(a, 120), rl(far_left, 56)))
    return jnp.concatenate([nb, f[16:48], na], axis=0)


def strip_y(f):
    low = sub_iota() < 4
    parts = []
    for i in range(4):
        x, y = f[16 * i : 16 * i + 8], f[16 * i + 8 : 16 * i + 16]
        parts.append(x + jnp.where(low, rs(rl(y, 1), 4), 0.0))
        parts.append(y + jnp.where(low, 0.0, rs(rl(x, 127), 4)))
    return jnp.concatenate(parts, axis=0)


def inverse_mass(m):
    return jnp.where(m > 0.5, PUSH / jnp.where(m > 0.5, m, 1.0), 0.0)


def strip_arrays(z1o, z2o, z1s, z2s):
    q = lane_iota(64) // 32

    def four(a, b, c, d):
        return jnp.where(q < 2, jnp.where(q == 0, a, b), jnp.where(q == 2, c, d))

    us = jnp.where(q < 2, z1o, rl(z1s, 64))
    m0 = four(rl(z1o, 64), rl(z1o, 96), z1s, rl(z1s, 32))
    m1 = four(rl(z1o, 32), rl(z1o, 64), rl(z1s, 96), z1s)
    m2 = four(z2o, rl(z2o, 32), rl(z2s, 64), rl(z2s, 96))
    mass = four(rl(z2o, 96), z2o, rl(z2s, 32), rl(z2s, 64))
    return us, jnp.concatenate([m0, m1, m2], axis=0), mass


def pair_expand(x, mk):
    r = rs(x, 4)
    return jnp.where(mk["lo"], x, r), jnp.where(mk["lo"], r, x)


def state_expand(xu, xw, mk):
    return jnp.where(mk["lo"], xu, rs(xw, 4)), jnp.where(mk["lo"], rs(xu, 4), xw)


def edge_kernel(u_ref, w_ref, m_ref, mass_ref, z_ref):
    lane = lane_iota(64)
    pieces = (
        (w_ref, 0, 0, 0),
        (u_ref, 0, 0, 1),
        (m_ref, 0, 0, 2),
        (m_ref, 256, 0, 3),
        (m_ref, 512, 1, 0),
        (mass_ref, 0, 1, 1),
    )
    z = [jnp.zeros((64, 128), jnp.float32), jnp.zeros((64, 128), jnp.float32)]
    for ref, base, half, slot in pieces:
        for side in range(2):
            for r in range(2):
                rows = ref[pl.ds(base + 2 * (1 - side) + r, 64, stride=4), :]
                dest = slot * 32 + (1 - side) * 16 + (1 - r) * 8 + (3 if side else 1)
                src = 0 if side else 124
                moved = rl(rows, (dest - src) % 128)
                z[half] = jnp.where((lane >= dest) & (lane < dest + 4), moved, z[half])
    z_ref[0] = z[0]
    z_ref[1] = z[1]


def first_kernel(u_ref, w_ref, mod_ref, state_ref, f_ref):
    mk = masks()
    for p in range(32):
        a, b = state_expand(u_ref[p], w_ref[p], mk)
        state_ref[0, 2 * p] = a
        state_ref[0, 2 * p + 1] = b
    forces(state_ref, f_ref, mod_ref, 0, mk)


def send_kernel(
    sub_ref, u_ref, w_ref, mod_ref, mass_ref, f_ref, z_ref, table_ref, tablet_ref,
    left_ref, right_ref, zo_ref,
):
    mk = masks()
    even = mk["even"]
    sub = sub_ref[0]
    base = 0
    for ref in (u_ref, w_ref, mod_ref, mass_ref):
        count = ref.shape[0] // 2
        for p in range(count):
            x, y = ref[2 * p], ref[2 * p + 1]
            left_ref[base + p] = jnp.where(even, x, rs(y, 1))
            right_ref[base + p] = jnp.where(even, rs(x, 7), y)
        base += count
    left, right = far_pack(lambda n: f_ref[0, n], mk)
    for p in range(8):
        left_ref[FAR + p] = left[p]
        right_ref[FAR + p] = right[p]

    def mass_node(n):
        return pair_expand(mass_ref[n // 2], mk)[n % 2]

    left, right = far_pack(mass_node, mk)
    for p in range(8):
        left_ref[MFAR + p] = left[p]
        right_ref[MFAR + p] = right[p]
    lane = lane_iota(64)
    side0 = ((lane // 16) % 2) == 1
    c = lane % 8
    below, above = jnp.maximum(sub - 1, 0), jnp.minimum(sub + 1, 3)
    zs = []
    for half in range(2):
        own = z_ref[sub, half]
        zl = jnp.where(sub > 0, z_ref[below, half], 0.0)
        zr = jnp.where(sub < 3, z_ref[above, half], 0.0)
        low = jnp.where(c == 0, 0.0, jnp.where(c <= 4, zl, rl(own, 18)))
        high = jnp.where(c <= 2, rl(own, 110), jnp.where(c == 7, 0.0, zr))
        z = jnp.where(side0, low, high)
        zo_ref[half] = z
        zs.append(z)
    zero = jnp.zeros((64, 128), jnp.float32)
    us, mods, mass = strip_arrays(zs[0], zs[1], zero, zero)
    fs = strip_forces(us, mods, table_ref[...], tablet_ref[...])
    evg = ((lane // 8) % 2) == 0
    wl = jnp.where(evg, rl(zs[1], 120), zs[0])
    wr = jnp.where(evg, zs[0], rl(zs[1], 8))
    for p in range(8):
        left_ref[ZST + p] = wl[8 * p : 8 * p + 8]
        right_ref[ZST + p] = wr[8 * p : 8 * p + 8]
    for p in range(2):
        left_ref[SFAR + p] = fs[8 * p : 8 * p + 8]
        right_ref[SFAR + p] = fs[48 + 8 * p : 56 + 8 * p]
        left_ref[SMFAR + p] = mass[8 * p : 8 * p + 8]
        right_ref[SMFAR + p] = mass[48 + 8 * p : 56 + 8 * p]


def rows16(ref, at):
    return jnp.concatenate([ref[at], ref[at + 1]], axis=0)


def middle_kernel(
    mod_ref, mass_ref, u0_ref, f0_ref, zo_ref, mr_ref, ml_ref, table_ref, tablet_ref,
    bl_ref, br_ref, mm_ref, inv_ref, u1_ref, v1_ref, f1_ref, u2_ref, v2_ref, f2_ref,
    smod_ref, sinv_ref, sstate_ref,
    u, v, f, sx,
):
    mk = masks()
    even, lo = mk["even"], mk["lo"]
    table, tablet = table_ref[...], tablet_ref[...]

    def shadow(p):
        r, l = mr_ref[p], ml_ref[p]
        return jnp.where(even, r, rs(l, 1)), jnp.where(even, rs(r, 7), l)

    for p in range(16):
        su, sw = shadow(p), shadow(16 + p)
        for e in range(2):
            u[1, 4 * p + 2 * e], u[1, 4 * p + 2 * e + 1] = state_expand(su[e], sw[e], mk)
    for p in range(48):
        mm_ref[1, 2 * p], mm_ref[1, 2 * p + 1] = shadow(32 + p)
    for p in range(96):
        mm_ref[0, p] = mod_ref[0, p]
    for p in range(16):
        sm = shadow(80 + p)
        for e in range(2):
            f[1, 4 * p + 2 * e], f[1, 4 * p + 2 * e + 1] = pair_expand(sm[e], mk)
    for p in range(32):
        f[0, 2 * p], f[0, 2 * p + 1] = pair_expand(mass_ref[p], mk)
    wr = jnp.concatenate([mr_ref[ZST + p] for p in range(8)], axis=0)
    wl = jnp.concatenate([ml_ref[ZST + p] for p in range(8)], axis=0)
    evg = ((lane_iota(64) // 8) % 2) == 0
    z1s = jnp.where(evg, wl, wr)
    z2s = jnp.where(evg, rl(wl, 120), rl(wr, 8))
    us, mods, smass = strip_arrays(zo_ref[0], zo_ref[1], z1s, z2s)
    smod_ref[...] = mods
    smass = strip_x(smass, rows16(mr_ref, SMFAR), rows16(ml_ref, SMFAR))
    sx[...] = smass
    x_assemble(f, mk, mr_ref, ml_ref, MFAR)
    for h in range(2):
        y_assemble(f, sx, h, mk)
    sinv = inverse_mass(strip_y(smass))
    sinv_ref[...] = sinv

    def invert(n, carry):
        inv_ref[0, n] = inverse_mass(f[0, n])
        inv_ref[1, n] = inverse_mass(f[1, n])
        return carry

    lax.fori_loop(0, 64, invert, 0, unroll=8)
    for n in range(64):
        f[0, n] = f0_ref[0, n]
        u[0, n] = u0_ref[0, n]
    forces(u, f, mm_ref, 1, mk)
    fs = strip_forces(us, mods, table, tablet)
    fs = strip_x(fs, rows16(mr_ref, SFAR), rows16(ml_ref, SFAR))
    sx[...] = fs
    x_assemble(f, mk, mr_ref, ml_ref, FAR)
    for h in range(2):
        y_assemble(f, sx, h, mk)
    svel = -sinv * strip_y(fs)
    us = us + svel
    for h in range(2):
        update(u, v, f, inv_ref, h, first=True)
    for n in range(64):
        for h in range(2):
            u1_ref[h, n] = u[h, n]
        v1_ref[1, n] = v[1, n]
        v1_ref[0, n] = v[0, n]
    lax.fori_loop(0, 2, lambda h, c: (forces(u, f, mm_ref, h, mk), c)[1], 0)
    fs = strip_forces(us, mods, table, tablet)
    sstate_ref[0] = us
    sstate_ref[1] = svel
    sstate_ref[2] = fs
    left, right = far_pack(lambda n: f[0, n], mk)
    for p in range(8):
        bl_ref[p] = left[p]
        br_ref[p] = right[p]
    for p in range(2):
        bl_ref[16 + p] = fs[8 * p : 8 * p + 8]
        br_ref[16 + p] = fs[48 + 8 * p : 56 + 8 * p]
    for n in range(64):
        for h in range(2):
            f1_ref[h, n] = f[h, n]
    zero = jnp.zeros((16, 128), jnp.float32)
    fs = strip_x(fs, zero, zero)
    sx[...] = fs
    x_assemble(f, mk)
    y_assemble(f, sx, 0, mk)
    svel = svel - sinv * strip_y(fs)
    us = us + svel
    update(u, v, f, inv_ref, 0)
    for n in range(64):
        u2_ref[n] = u[0, n]
        v2_ref[n] = v[0, n]
    forces(u, f, mm_ref, 0, mk)
    fs = strip_forces(us, mods, table, tablet)
    left, right = far_pack(lambda n: f[0, n], mk)
    for p in range(8):
        bl_ref[8 + p] = left[p]
        br_ref[8 + p] = right[p]
    for p in range(2):
        bl_ref[18 + p] = fs[8 * p : 8 * p + 8]
        br_ref[18 + p] = fs[48 + 8 * p : 56 + 8 * p]
    for n in range(64):
        f2_ref[n] = f[0, n]


def last_kernel(
    br_ref, bl_ref, mm_ref, inv_ref, u0_ref, u1_ref, v1_ref, f1_ref, u2_ref, v2_ref, f2_ref,
    smod_ref, sinv_ref, sstate_ref, owner_ref, table_ref, tablet_ref,
    out_u_ref, out_w_ref, sums_ref,
    u, v, f, sx, u3, dens, hot,
):
    mk = masks()
    lo = mk["lo"]
    table, tablet = table_ref[...], tablet_ref[...]
    mods, sinv = smod_ref[...], sinv_ref[...]
    us, svel, fs = sstate_ref[0], sstate_ref[1], sstate_ref[2]
    for n in range(64):
        f[0, n] = f1_ref[0, n]
        f[1, n] = f1_ref[1, n]
        u[1, n] = u1_ref[1, n]
        v[1, n] = v1_ref[1, n]
    fs = strip_x(fs, rows16(br_ref, 16), rows16(bl_ref, 16))
    sx[...] = fs
    x_assemble(f, mk, br_ref, bl_ref, 0)
    y_assemble(f, sx, 1, mk)
    svel = svel - sinv * strip_y(fs)
    us = us + svel
    update(u, v, f, inv_ref, 1)
    for n in range(64):
        f[0, n] = f2_ref[n]
        u[0, n] = u2_ref[n]
        v[0, n] = v2_ref[n]
    forces(u, f, mm_ref, 1, mk)
    fs = strip_forces(us, mods, table, tablet)
    fs = strip_x(fs, rows16(br_ref, 18), rows16(bl_ref, 18))
    sx[...] = fs
    x_assemble(f, mk, br_ref, bl_ref, 8)
    for h in range(2):
        y_assemble(f, sx, h, mk)
    svel = svel - sinv * strip_y(fs)
    us = us + svel
    for h in range(2):
        update(u, v, f, inv_ref, h)
    for n in range(64):
        u3[0, n] = u[0, n]
    lax.fori_loop(0, 2, lambda h, c: (forces(u, f, mm_ref, h, mk), c)[1], 0)
    fs = strip_forces(us, mods, table, tablet)
    zero = jnp.zeros((16, 128), jnp.float32)
    sx[...] = strip_x(fs, zero, zero)
    x_assemble(f, mk)
    y_assemble(f, sx, 0, mk)
    update(u, v, f, inv_ref, 0)
    for p in range(32):
        a, b = u[0, 2 * p], u[0, 2 * p + 1]
        out_u_ref[p] = jnp.where(lo, a, rs(b, 4))
        out_w_ref[p] = jnp.where(lo, rs(a, 4), b)
    for direction in (2, 1, 0):
        for a in range(4):
            for b in range(4):
                nodes = line_nodes(direction, a, b)
                g0 = d_line(*[u0_ref[0, n] for n in nodes])
                g1 = d_line(*[u1_ref[0, n] for n in nodes])
                g2 = d_line(*[u2_ref[n] for n in nodes])
                g3 = d_line(*[u3[0, n] for n in nodes])
                g4 = d_line(*[u[0, n] for n in nodes])
                for e, n in enumerate(nodes):
                    t = g1[e] * rs(g3[e], 4) + jnp.where(
                        lo, g2[e] * rs(g2[e], 4), g0[e] * rs(g4[e], 4)
                    )
                    t = t * node_moduli(mm_ref, 0, 64 * direction + n, mk)
                    at = pl.ds(8 * n, 8)
                    dens[at, :] = t if direction == 2 else dens[at, :] + t
    block = lax.broadcasted_iota(jnp.int32, (512, 128), 0)
    cols = []
    for s in range(4):
        cols.append(
            dens[pl.ds(s, 64, stride=8), :] + dens[pl.ds(s + 4, 64, stride=8), :]
        )
        owner = jnp.broadcast_to(owner_ref[s : s + 1, :], (512, 128))
        hot[:, 128 * s : 128 * s + 128] = (block == owner).astype(jnp.float32).astype(jnp.bfloat16)
    d = jnp.concatenate(cols, axis=1)
    hi = d.astype(jnp.bfloat16)
    rest = d - hi.astype(jnp.float32)
    mid = rest.astype(jnp.bfloat16)
    low = (rest - mid.astype(jnp.float32)).astype(jnp.bfloat16)
    split = jnp.concatenate([hi, mid, low], axis=0)
    res = lax.dot_general(
        split, hot[...], (((1,), (1,)), ((), ())), preferred_element_type=jnp.float32
    )
    sums = res[0:64] + (res[64:128] + res[128:192])
    for q in range(4):
        sums_ref[q] = sums[:, 128 * q : 128 * q + 128]


def project_kernel(x_ref, basis_ref, out_ref):
    total = (x_ref[0] + x_ref[1]) + (x_ref[2] + x_ref[3])
    out_ref[...] = KERNEL_SCALE * jnp.dot(
        basis_ref[...], total, precision=lax.Precision.HIGHEST, preferred_element_type=jnp.float32
    )


def call(kernel, outs, ins, scratch=(), smem_first=False):
    vmem = pl.BlockSpec(memory_space=pltpu.VMEM)
    specs = [vmem] * len(ins)
    if smem_first:
        specs[0] = pl.BlockSpec(memory_space=pltpu.SMEM)
    return pl.pallas_call(
        kernel,
        out_shape=[jax.ShapeDtypeStruct(s, jnp.float32) for s in outs],
        in_specs=specs,
        out_specs=[vmem] * len(outs),
        scratch_shapes=[pltpu.VMEM(s, t) for s, t in scratch],
        compiler_params=pltpu.CompilerParams(vmem_limit_bytes=28 * 1024 * 1024),
    )(*ins)


def raw_tiles(x):
    lead = int(np.prod(x.shape[:-2]))
    return x.reshape(lead, 2, 2, 128).transpose(0, 2, 1, 3).reshape(lead * 4, 128)


def from_tiles(x):
    return x.reshape(64, 2, 2, 128).transpose(0, 2, 1, 3).reshape(64, 2, 256)


def on_device(initial_field, adjoint_source, moduli, node_mass, block_owner, spline_basis):
    count = lax.axis_size("dom")
    to_right = [(i, i + 1) for i in range(count - 1)]
    to_left = [(b, a) for a, b in to_right]
    table = jnp.asarray(GRADIENT_TABLE)
    tablet = jnp.asarray(np.ascontiguousarray(GRADIENT_TABLE.T))
    sub = lax.axis_index("sub").astype(jnp.int32).reshape(1)
    u2d, w2d, m2d, mass2d = map(raw_tiles, (initial_field, adjoint_source, moduli, node_mass))
    owner = raw_tiles(block_owner[None])
    u, w, mass = (x.reshape(32, 8, 128) for x in (u2d, w2d, mass2d))
    mod = m2d.reshape(1, 96, 8, 128)
    tile = (64, 8, 128)
    one, two = (1,) + tile, (2,) + tile

    (edges,) = call(edge_kernel, [(2, 64, 128)], [u2d, w2d, m2d, mass2d])
    edges = lax.all_gather(edges, "sub")
    u0, f0 = call(first_kernel, [one, one], [u, w, mod])
    left, right, zo = call(
        send_kernel,
        [(MSG, 8, 128), (MSG, 8, 128), (2, 64, 128)],
        [sub, u, w, mod[0], mass, f0, edges, table, tablet],
        smem_first=True,
    )
    from_right = lax.ppermute(left, "dom", to_left)
    from_left = lax.ppermute(right, "dom", to_right)
    f32 = jnp.float32
    bl, br, mm, inv, u1, v1, f1, u2, v2, f2, smod, sinv, sstate = call(
        middle_kernel,
        [
            (MSG_B, 8, 128), (MSG_B, 8, 128), (2, 96, 8, 128), two, two, two, two,
            tile, tile, tile, (192, 128), (64, 128), (3, 64, 128),
        ],
        [mod, mass, u0, f0, zo, from_right, from_left, table, tablet],
        [(two, f32)] * 3 + [((64, 128), f32)],
    )
    from_right = lax.ppermute(bl, "dom", to_left)
    from_left = lax.ppermute(br, "dom", to_right)
    out_u, out_w, sums = call(
        last_kernel,
        [(32, 8, 128), (32, 8, 128), (4, 64, 128)],
        [
            from_right, from_left, mm, inv, u0, u1, v1, f1, u2, v2, f2, smod, sinv, sstate,
            owner, table, tablet,
        ],
        [(two, f32)] * 3
        + [((64, 128), f32), (one, f32), ((512, 128), f32), ((512, 512), jnp.bfloat16)],
    )
    sums = lax.all_to_all(sums, "sub", 0, 0)
    (kernel,) = call(project_kernel, [(64, 128)], [sums, spline_basis.T])
    return from_tiles(out_u), from_tiles(out_w), kernel


def solution(mesh):
    in_specs = (
        P(None, "dom", "sub"),
        P(None, "dom", "sub"),
        P(None, None, "dom", "sub"),
        P(None, "dom", "sub"),
        P("dom", "sub"),
        P(),
    )
    out_specs = (P(None, "dom", "sub"), P(None, "dom", "sub"), P(None, ("dom", "sub")))
    return jax.shard_map(
        on_device, mesh=mesh, in_specs=in_specs, out_specs=out_specs, check_vma=False
    )
```

time: 265 us -> 76.2 us (0.29)
  starting transfers between devices: 107 us -> 26 us
  waiting for transfers between devices: 87.5 us -> 25.5 us
  local copies, waits for them, and re-layouts: 29.4 us -> 5.08 us
  between operations: 15.7 us -> 0.77 us
  other arithmetic: 12.6 us -> 0 us
  Pallas kernels: 0 us -> 10 us
  matrix products: 9.63 us -> 0 us
  blocking collectives: 0 us -> 7.93 us
    ppermute x36 -> x4, starting transfers between devices: 107 us -> 19.4 us  [the longest x1 12.2 us: on_device(): from_right = lax.ppermute(left, 'dom', to_left)]
    ppermute x36 -> x4, waiting for transfers between devices: 55.9 us -> 20.5 us  [the longest x1 8.87 us: on_device(): from_right = lax.ppermute(left, 'dom', to_left)]
    reduce_scatter x1 -> x0, waiting for transfers between devices: 31.6 us -> none  [on_device(): kernel = lax.psum_scatter(projected, 'sub', scatter_dimension=1, tiled=True)]
    pallas_call x0 -> x6, Pallas kernels: none -> 10 us  [call(): pl.pallas_call(kernel, out_shape=[jax.ShapeDtypeStruct(s, jnp.float32) fo...]
    dot_general x19 -> x0, matrix products: 9.63 us -> none  [the longest x8 3.91 us: stiffness_apply(): jnp.einsum('gn,lgc->lnc', GRADIENT_TABLE, fluxes, precision=lax.Precision...]
    add x43 -> x0, other arithmetic: 8.57 us -> none  [the longest x9 3.54 us: merge_y(): lower_face + upper_prev]
    all_gather x0 -> x1, blocking collectives: none -> 7.93 us  [on_device(): edges = lax.all_gather(edges, 'sub')]
    unnamed x83 -> x25, local copies, waits for them, and re-layouts: 12.3 us -> 5.08 us
  transfers between devices with their start and end apart: 37 -> 5, of which waited for: 21 -> 4; matrix products, arithmetic and copies ran while one was open for 9% -> 0% of each run, Pallas kernels for 0% -> 0%
where the time goes in v1:
time: 76.2 us; the launch traced here: 75.3 us
  starting transfers between devices  26 us (34%)
  waiting for transfers between devices  25.5 us (33%)
  Pallas kernels  10 us (13%)
  blocking collectives  7.93 us (10%)
  local copies, waits for them, and re-layouts  5.08 us (7%)
  between operations  0.77 us (1%)
    ppermute x1, starting transfers between devices, on_device(): from_right = lax.ppermute(left, 'dom', to_left)  12.2 us
    pallas_call x6, Pallas kernels, call(): pl.pallas_call(kernel, out_shape=[jax.ShapeDtypeStruct(s, jnp.float32) fo...  10 us
    ppermute x1, waiting for transfers between devices, on_device(): from_right = lax.ppermute(left, 'dom', to_left)  8.87 us
    all_gather x1, blocking collectives, on_device(): edges = lax.all_gather(edges, 'sub')  7.93 us
    ppermute x1, waiting for transfers between devices, on_device(): from_left = lax.ppermute(right, 'dom', to_right)  6.81 us
    all_to_all x1, starting transfers between devices, on_device(): sums = lax.all_to_all(sums, 'sub', 0, 0)  6.56 us
    unnamed x25, local copies, waits for them, and re-layouts  5.08 us
    all_to_all x1, waiting for transfers between devices, on_device(): sums = lax.all_to_all(sums, 'sub', 0, 0)  5.02 us
  transfers between devices with their start and end apart: 5, of which 4 were waited for; matrix products, arithmetic and copies ran while one was open for 0% of the time, Pallas kernels for 0%

profile of v1, /device:TPU:25, one launch (start us, length us, event | category | flops | bytes accessed | tf_op | source)
XLA Modules:
  0.0 75.3 jit_solution(5326390584382652675)
XLA Ops:
  0.6 1.0 %copy-done = f32[3,64,2,256]{3,2,1,0:T(2,128)S(1)} copy-done((f32[3,64,2,256]{3,2,1,0:T(2,128)S(1)}, f32[3,64,2,256]{3,2,1,0:T(2,128)}, u32[]{:S(2)}) %copy-start) | copy-done | bytes 393240
  1.6 0.9 %copy-done.2 = f32[64,2,256]{2,1,0:T(2,128)S(1)} copy-done((f32[64,2,256]{2,1,0:T(2,128)S(1)}, f32[64,2,256]{2,1,0:T(2,128)}, u32[]{:S(2)}) %copy-start.2) | copy-done | bytes 131096
  2.5 0.9 %copy-done.4 = f32[64,2,256]{2,1,0:T(2,128)S(1)} copy-done((f32[64,2,256]{2,1,0:T(2,128)S(1)}, f32[64,2,256]{2,1,0:T(2,128)}, u32[]{:S(2)}) %copy-start.4) | copy-done | bytes 131096
  3.4 0.9 %copy-done.6 = f32[64,2,256]{2,1,0:T(2,128)S(1)} copy-done((f32[64,2,256]{2,1,0:T(2,128)S(1)}, f32[64,2,256]{2,1,0:T(2,128)}, u32[]{:S(2)}) %copy-start.6) | copy-done | bytes 131096
  4.3 0.3 shard_map.104
  4.6 7.9 %all-gather = f32[8,64,128]{2,1,0:T(8,128)S(1)} all-gather(f32[2,64,128]{2,1,0:T(8,128)S(1)} %shard_map.104), channel_id=2, replica_groups=mesh['dom'=128,'sub'=4] {'sub'}, dimensions={0}, use_global_device_ids=true | all-gather | bytes 327680 | tf_op jit(solution)/shard_map/all_gather | solution.py:553
  12.6 0.3 shard_map.103
  13.0 0.5 copy-done.7
  13.5 0.1 copy-done.8
  13.6 0.6 shard_map.105
  14.2 12.2 %collective-permute-start = (f32[124,8,128]{2,1,0:T(8,128)S(1)}, f32[124,8,128]{2,1,0:T(8,128)S(1)}, u32[]{:S(2)}, u32[]{:S(2)}) collective-permute-start(f32[124,8,128]{2,1,0:T(8,128)S(1)} %get-tuple-element.27), channel_id=1, source_target_pairs={{4,0},{8,4},{12,8},{16,12},{20,16},{24,20},{28,24},{32,28},{36,32}... | collective-permute-start | bytes 1523720 | tf_op jit(solution)/shard_map/ppermute | solution.py:561
  26.4 1.9 %collective-permute-start.1 = (f32[124,8,128]{2,1,0:T(8,128)S(1)}, f32[124,8,128]{2,1,0:T(8,128)S(1)}, u32[]{:S(2)}, u32[]{:S(2)}) collective-permute-start(f32[124,8,128]{2,1,0:T(8,128)S(1)} %get-tuple-element.28), channel_id=1, source_target_pairs={{0,4},{4,8},{8,12},{12,16},{16,20},{20,24},{24,28},{28,32},{32,36}... | collective-permute-start | bytes 1523720 | tf_op jit(solution)/shard_map/ppermute | solution.py:562
  28.3 8.9 %collective-permute-done.mr_ref = f32[124,8,128]{2,1,0:T(8,128)S(1)} collective-permute-done((f32[124,8,128]{2,1,0:T(8,128)S(1)}, f32[124,8,128]{2,1,0:T(8,128)S(1)}, u32[]{:S(2)}, u32[]{:S(2)}) %collective-permute-start) | collective-permute-done | bytes 507936 | tf_op jit(solution)/shard_map/ppermute | solution.py:561
  37.2 6.8 %collective-permute-done.1.ml_ref = f32[124,8,128]{2,1,0:T(8,128)S(1)} collective-permute-done((f32[124,8,128]{2,1,0:T(8,128)S(1)}, f32[124,8,128]{2,1,0:T(8,128)S(1)}, u32[]{:S(2)}, u32[]{:S(2)}) %collective-permute-start.1) | collective-permute-done | bytes 507936 | tf_op jit(solution)/shard_map/ppermute | solution.py:562
  44.0 3.6 %shard_map.106 = (f32[20,8,128]{2,1,0:T(8,128)S(1)}, f32[20,8,128]{2,1,0:T(8,128)S(1)}, f32[2,96,8,128]{3,2,1,0:T(8,128)S(1)}, f32[2,64,8,128]{3,2,1,0:T(8,128)S...) custom-call(f32[1,96,8,128]{3,2,1,0:T(8,128)S(1)} %bitcast.51, ...), custom_call_target="tpu_custom_call" | custom-call | tf_op jit(solution)/shard_map/pallas_call | solution.py:519
  47.7 1.9 %collective-permute-start.2 = (f32[20,8,128]{2,1,0:T(8,128)S(1)}, f32[20,8,128]{2,1,0:T(8,128)S(1)}, u32[]{:S(2)}, u32[]{:S(2)}) collective-permute-start(f32[20,8,128]{2,1,0:T(8,128)S(1)} %get-tuple-element.29), channel_id=1, source_target_pairs={{4,0},{8,4},{12,8},{16,12},{20,16},{24,20},{28,24},{32,28},{36,32}... | collective-permute-start | bytes 245768 | tf_op jit(solution)/shard_map/ppermute | solution.py:573
  49.6 3.4 %collective-permute-start.3 = (f32[20,8,128]{2,1,0:T(8,128)S(1)}, f32[20,8,128]{2,1,0:T(8,128)S(1)}, u32[]{:S(2)}, u32[]{:S(2)}) collective-permute-start(f32[20,8,128]{2,1,0:T(8,128)S(1)} %get-tuple-element.30), channel_id=1, source_target_pairs={{0,4},{4,8},{8,12},{12,16},{16,20},{20,24},{24,28},{28,32},{32,36}... | collective-permute-start | bytes 245768 | tf_op jit(solution)/shard_map/ppermute | solution.py:574
  53.0 4.8 %collective-permute-done.3.bl_ref = f32[20,8,128]{2,1,0:T(8,128)S(1)} collective-permute-done((f32[20,8,128]{2,1,0:T(8,128)S(1)}, f32[20,8,128]{2,1,0:T(8,128)S(1)}, u32[]{:S(2)}, u32[]{:S(2)}) %collective-permute-start.3) | collective-permute-done | bytes 81952 | tf_op jit(solution)/shard_map/ppermute | solution.py:574
  57.8 0.7 copy-done.10
  58.5 4.4 %shard_map.107 = (f32[32,8,128]{2,1,0:T(8,128)}, f32[32,8,128]{2,1,0:T(8,128)}, f32[4,64,128]{2,1,0:T(8,128)}) custom-call(f32[20,8,128]{2,1,0:T(8,128)S(1)} %collective-permute-done.2.br_ref, f32[20,8,128]{2,1,0:T(8,128)S(1)} %collective-permute-done.3.bl_ref, f32[2,96,8,128]{3,2,1,0:T(8,128)S(1)} %get-tuple-element.31.mm_ref, ...), custom_call_target="tpu_custom_call" | custom-call | tf_op jit(solution)/shard_map/pallas_call | solution.py:519
  62.9 6.6 %all-to-all-start = ((f32[4,64,128]{2,1,0:T(8,128)}), f32[4,64,128]{2,1,0:T(8,128)S(1)}, u32[]{:S(2)}, u32[]{:S(2)}) async-start(f32[4,64,128]{2,1,0:T(8,128)} %get-tuple-element.44), calls=%async_computation | async-start | bytes 262144 | tf_op jit(solution)/shard_map/all_to_all | solution.py:585
  69.4 0.1 copy.26
  69.5 5.0 %all-to-all-done.x_ref = f32[4,64,128]{2,1,0:T(8,128)S(1)} async-done(((f32[4,64,128]{2,1,0:T(8,128)}), f32[4,64,128]{2,1,0:T(8,128)S(1)}, u32[]{:S(2)}, u32[]{:S(2)}) %all-to-all-start) | async-done | bytes 131104 | tf_op jit(solution)/shard_map/all_to_all | solution.py:585
  74.5 0.8 %shard_map.108 = f32[64,128]{1,0:T(8,128)} custom-call(f32[4,64,128]{2,1,0:T(8,128)S(1)} %all-to-all-done.x_ref, f32[64,64]{1,0:T(8,128)S(1)} %bitcast.62), custom_call_target="tpu_custom_call" | custom-call | tf_op jit(solution)/shard_map/pallas_call | solution.py:519
  (18 shorter events, 0.0 us)
Async XLA Ops:
  0.6 1.0 %copy-start = (f32[3,64,2,256]{3,2,1,0:T(2,128)S(1)}, f32[3,64,2,256]{3,2,1,0:T(2,128)}, u32[]{:S(2)}) copy-start(f32[3,64,2,256]{3,2,1,0:T(2,128)} %param.10) | copy-start | bytes 1179652
  1.6 0.9 %copy-start.2 = (f32[64,2,256]{2,1,0:T(2,128)S(1)}, f32[64,2,256]{2,1,0:T(2,128)}, u32[]{:S(2)}) copy-start(f32[64,2,256]{2,1,0:T(2,128)} %param.8) | copy-start | bytes 393220
  2.5 0.9 %copy-start.4 = (f32[64,2,256]{2,1,0:T(2,128)S(1)}, f32[64,2,256]{2,1,0:T(2,128)}, u32[]{:S(2)}) copy-start(f32[64,2,256]{2,1,0:T(2,128)} %param.9) | copy-start | bytes 393220
  3.4 0.9 %copy-start.6 = (f32[64,2,256]{2,1,0:T(2,128)S(1)}, f32[64,2,256]{2,1,0:T(2,128)}, u32[]{:S(2)}) copy-start(f32[64,2,256]{2,1,0:T(2,128)} %param.11) | copy-start | bytes 393220
  4.3 8.2 %copy-start.1 = (f32[3,64,2,256]{3,2,1,0:T(2,128)S(1)}, f32[3,64,2,256]{3,2,1,0:T(2,128)}, u32[]{:S(2)}) copy-start(f32[3,64,2,256]{3,2,1,0:T(2,128)} %param.10) | copy-start | bytes 1179652
  4.6 8.0 %copy-start.3 = (f32[64,2,256]{2,1,0:T(2,128)S(1)}, f32[64,2,256]{2,1,0:T(2,128)}, u32[]{:S(2)}) copy-start(f32[64,2,256]{2,1,0:T(2,128)} %param.8) | copy-start | bytes 393220
  4.6 8.0 %copy-start.5 = (f32[64,2,256]{2,1,0:T(2,128)S(1)}, f32[64,2,256]{2,1,0:T(2,128)}, u32[]{:S(2)}) copy-start(f32[64,2,256]{2,1,0:T(2,128)} %param.9) | copy-start | bytes 393220
  12.6 0.9 %copy-start.7 = (f32[64,2,256]{2,1,0:T(2,128)S(1)}, f32[64,2,256]{2,1,0:T(2,128)}, u32[]{:S(2)}) copy-start(f32[64,2,256]{2,1,0:T(2,128)} %param.11) | copy-start | bytes 393220
  12.6 1.0 %copy-start.8 = (f32[192,64]{1,0:T(8,128)S(1)}, f32[192,64]{1,0:T(8,128)}, u32[]{:S(2)}) copy-start(f32[192,64]{1,0:T(8,128)} %constant.8.clone.table_ref) | copy-start | bytes 147460
  12.6 0.9 %copy-start.9 = (f32[64,192]{1,0:T(8,128)S(1)}, f32[64,192]{1,0:T(8,128)}, u32[]{:S(2)}) copy-start(f32[64,192]{1,0:T(8,128)} %constant.9.clone.tablet_ref) | copy-start | bytes 147460
  14.2 23.0 %collective-permute-start = (f32[124,8,128]{2,1,0:T(8,128)S(1)}, f32[124,8,128]{2,1,0:T(8,128)S(1)}, u32[]{:S(2)}, u32[]{:S(2)}) collective-permute-start(f32[124,8,128]{2,1,0:T(8,128)S(1)} %get-tuple-element.27), channel_id=1, source_target_pairs={{4,0},{8,4},{12,8},{16,12},{20,16},{24,20},{28,24},{32,28},{36,32}... | collective-permute-start | bytes 1523720 | tf_op jit(solution)/shard_map/ppermute | solution.py:561
  26.4 17.6 %collective-permute-start.1 = (f32[124,8,128]{2,1,0:T(8,128)S(1)}, f32[124,8,128]{2,1,0:T(8,128)S(1)}, u32[]{:S(2)}, u32[]{:S(2)}) collective-permute-start(f32[124,8,128]{2,1,0:T(8,128)S(1)} %get-tuple-element.28), channel_id=1, source_target_pairs={{0,4},{4,8},{8,12},{12,16},{16,20},{20,24},{24,28},{28,32},{32,36}... | collective-permute-start | bytes 1523720 | tf_op jit(solution)/shard_map/ppermute | solution.py:562
  47.7 5.3 %collective-permute-start.2 = (f32[20,8,128]{2,1,0:T(8,128)S(1)}, f32[20,8,128]{2,1,0:T(8,128)S(1)}, u32[]{:S(2)}, u32[]{:S(2)}) collective-permute-start(f32[20,8,128]{2,1,0:T(8,128)S(1)} %get-tuple-element.29), channel_id=1, source_target_pairs={{4,0},{8,4},{12,8},{16,12},{20,16},{24,20},{28,24},{32,28},{36,32}... | collective-permute-start | bytes 245768 | tf_op jit(solution)/shard_map/ppermute | solution.py:573
  49.6 8.2 %collective-permute-start.3 = (f32[20,8,128]{2,1,0:T(8,128)S(1)}, f32[20,8,128]{2,1,0:T(8,128)S(1)}, u32[]{:S(2)}, u32[]{:S(2)}) collective-permute-start(f32[20,8,128]{2,1,0:T(8,128)S(1)} %get-tuple-element.30), channel_id=1, source_target_pairs={{0,4},{4,8},{8,12},{12,16},{16,20},{20,24},{24,28},{28,32},{32,36}... | collective-permute-start | bytes 245768 | tf_op jit(solution)/shard_map/ppermute | solution.py:574
  57.8 0.7 copy-start.10
  62.9 6.6 %copy-start.11 = (f32[64,64]{1,0:T(8,128)S(1)}, f32[64,64]{1,0:T(8,128)}, u32[]{:S(2)}) copy-start(f32[64,64]{1,0:T(8,128)} %param.13) | copy-start | bytes 49156
  62.9 11.7 %all-to-all-start = ((f32[4,64,128]{2,1,0:T(8,128)}), f32[4,64,128]{2,1,0:T(8,128)S(1)}, u32[]{:S(2)}, u32[]{:S(2)}) async-start(f32[4,64,128]{2,1,0:T(8,128)} %get-tuple-element.44), calls=%async_computation | async-start | bytes 262144 | tf_op jit(solution)/shard_map/all_to_all | solution.py:585

commit v2 on v1

v2 whole, which is shorter than its diff:
```python
import jax
import jax.numpy as jnp
import numpy as np
from jax import lax
from jax.experimental import pallas as pl
from jax.experimental.pallas import tpu as pltpu
from jax.sharding import PartitionSpec as P

STEPS = 4
TIME_STEP = 0.1
KERNEL_SCALE = 0.05
PUSH = TIME_STEP * TIME_STEP

DERIVATIVE = np.array(
    [
        [-3.0, 4.04508497187474, -1.54508497187474, 0.5],
        [-0.80901699437495, 0.0, 1.11803398874989, -0.30901699437495],
        [0.30901699437495, -1.11803398874989, 0.0, 0.80901699437495],
        [-0.5, 1.54508497187474, -4.04508497187474, 3.0],
    ]
)
HALF_AMB = float((DERIVATIVE[0, 1] - DERIVATIVE[0, 2]) / 2)
HALF_CME = float((DERIVATIVE[1, 0] - DERIVATIVE[1, 3]) / 2)
HALF_D = float(DERIVATIVE[1, 2] / 2)

FAR, MFAR, MSG = 96, 104, 112
ZST, SFAR, SMFAR, MSG_S = 0, 8, 10, 12
MSG_B = 20
FIRST_LIMIT = 62


def strip_coefficients():
    tiles = []
    for d in (DERIVATIVE, DERIVATIVE.T):
        for out in range(2):
            for term in range(4):
                col = np.zeros(8)
                for s in range(8):
                    j = 2 * out + s // 4
                    half = s // 4 if term % 2 == 0 else 1 - s // 4
                    col[s] = d[j, 2 * (term // 2) + half]
                tiles.append(col)
        for delta in range(-3, 4):
            col = np.zeros(8)
            for s in range(8):
                k = s % 4
                if 0 <= k + delta < 4:
                    col[s] = d[k, k + delta]
            tiles.append(col)
    return np.broadcast_to(np.array(tiles, np.float32)[:, :, None], (30, 8, 128))


COEFFICIENTS = np.ascontiguousarray(strip_coefficients())


def sub_iota():
    return lax.broadcasted_iota(jnp.int32, (8, 128), 0)


def lane_iota(rows=8):
    return lax.broadcasted_iota(jnp.int32, (rows, 128), 1)


def rs(x, shift):
    return pltpu.roll(x, shift, 0)


def rl(x, shift):
    return pltpu.roll(x, shift, 1)


def masks():
    s = sub_iota()
    lane = lane_iota()
    return dict(
        even=(s % 2) == 0,
        lo=s < 4,
        ct0=((s // 2) % 2) == 0,
        first=lane == 0,
        last=lane == 127,
    )


def d_line(x0, x1, x2, x3):
    p, m, q, n = x0 + x3, x0 - x3, x1 + x2, x1 - x2
    r = q - p
    s1 = -1.75 * m + HALF_AMB * n
    s2 = HALF_CME * m - HALF_D * n
    r1, r2 = 1.25 * r, HALF_D * r
    return s1 + r1, s2 + r2, s2 - r2, s1 - r1


def dt_line(x0, x1, x2, x3):
    p, m, q, n = x0 + x3, x0 - x3, x1 + x2, x1 - x2
    t = 1.25 * m + HALF_D * n
    q1 = HALF_CME * q - 1.75 * p
    q2 = HALF_AMB * p - HALF_D * q
    return q1 - t, t + q2, t - q2, -(q1 + t)


def line_nodes(direction, a, b):
    if direction == 0:
        return [16 * i + 4 * a + b for i in range(4)]
    if direction == 1:
        return [16 * a + 4 * j + b for j in range(4)]
    return [16 * a + 4 * b + k for k in range(4)]


def expanded(x, upper, mk):
    r = rs(x, 4)
    return jnp.where(mk["lo"], r, x) if upper else jnp.where(mk["lo"], x, r)


def forces(u, f, mod, mk, planes=(0, 1, 2, 3), hook=None):
    for direction in (2, 1, 0):
        for a in range(4):
            if direction and a not in planes:
                continue
            for b in range(4):
                nodes = line_nodes(direction, a, b)
                g = d_line(*[u(n) for n in nodes])
                if hook is not None:
                    for n, gn in zip(nodes, g):
                        hook(direction, n, gn)
                t = []
                for n, gn in zip(nodes, g):
                    at = 64 * direction + n
                    t.append(expanded(mod(at // 2), at % 2, mk) * gn)
                for n, o in zip(nodes, dt_line(*t)):
                    if n // 16 in planes:
                        f(n, o, direction == 2)


def into(ref, h):
    def put(n, value, first):
        ref[h, n] = value if first else ref[h, n] + value

    return put


def far_pack(f, mk):
    left, right = [], []
    for p in range(8):
        left.append(jnp.where(mk["even"], rs(f(2 * p), 7), f(2 * p + 1)))
        right.append(jnp.where(mk["even"], f(48 + 2 * p), rs(f(48 + 2 * p + 1), 1)))
    return left, right


def along_x(f, far, h, i, q, mk):
    even = mk["even"]
    x = f(h, 16 * i + q)
    if i in (1, 2):
        return x
    other = 3 - i
    if h == 0:
        inside, beside = f(0, 16 * other + q), f(1, 16 * other + q)
        if i == 3:
            return x + jnp.where(even, rs(inside, 7), rs(beside, 1))
        return x + jnp.where(even, rs(beside, 7), rs(inside, 1))
    near = f(0, 16 * other + q)
    if i == 3:
        beyond = far[0][far[2] + q // 2]
        beyond = rs(beyond, 7) if q % 2 else beyond
        return x + jnp.where(even, beyond, rs(near, 1))
    beyond = far[1][far[2] + q // 2]
    beyond = beyond if q % 2 else rs(beyond, 1)
    return x + jnp.where(even, rs(near, 7), beyond)


def assembled(f, far, strip, h, i, k, mk):
    vals = [along_x(f, far, h, i, 4 * j + k, mk) for j in range(4)]
    shift = 4 if h else 68

    def inject(row):
        return pltpu.roll(
            jnp.broadcast_to(strip[row : row + 1, :], (8, 128)), shift, 1, stride=8, stride_axis=0
        )

    b, a = vals[0], vals[3]
    up, down = rl(b, 127), rl(a, 1)
    up = jnp.where(mk["last"], jnp.where(mk["ct0"], rs(up, 6), inject(16 * i + k)), up)
    down = jnp.where(mk["first"], jnp.where(mk["ct0"], inject(16 * i + 12 + k), rs(down, 2)), down)
    return [b + down, vals[1], vals[2], a + up]


def update(f, far, strip, h, mk, inv, u, v, put):
    for i in range(4):
        for k in range(4):
            for j, total in enumerate(assembled(f, far, strip, h, i, k, mk)):
                n = 16 * i + 4 * j + k
                vel = -inv(n) * total if v is None else v(n) - inv(n) * total
                put(n, u(n) + vel, vel)


def strip_lines(x, cf, base):
    along_j, along_k = [], []
    for i in range(4):
        a, b = x[2 * i], x[2 * i + 1]
        terms = (a, rs(a, 4), b, rs(b, 4))
        for out in range(2):
            along_j.append(sum(cf[base + 4 * out + t] * terms[t] for t in range(4)))
    for v in range(8):
        along_k.append(
            sum(cf[base + 8 + d] * (rs(x[v], (3 - d) % 8) if d != 3 else x[v]) for d in range(7))
        )
    return along_j, along_k


def strip_forces(us, mods, cf):
    x = [us[8 * v : 8 * v + 8] for v in range(8)]
    gj, gk = strip_lines(x, cf, 0)
    gi = [None] * 8
    for e in range(2):
        for i, g in enumerate(d_line(*[x[2 * m + e] for m in range(4)])):
            gi[2 * i + e] = g
    ti, tj, tk = (
        [mods[64 * d + 8 * v : 64 * d + 8 * v + 8] * g[v] for v in range(8)]
        for d, g in enumerate((gi, gj, gk))
    )
    fj = strip_lines(tj, cf, 15)[0]
    fk = strip_lines(tk, cf, 15)[1]
    f = [fj[v] + fk[v] for v in range(8)]
    for e in range(2):
        for i, o in enumerate(dt_line(*[ti[2 * m + e] for m in range(4)])):
            f[2 * i + e] = f[2 * i + e] + o
    return jnp.concatenate(f, axis=0)


def strip_x(f, far_right, far_left):
    lane = lane_iota(16)
    even, own = ((lane // 8) % 2) == 1, lane < 64
    b, a = f[0:16], f[48:64]
    na = a + jnp.where(even, jnp.where(own, rl(b, 8), rl(far_right, 72)), rl(b, 56))
    nb = b + jnp.where(even, rl(a, 72), jnp.where(own, rl(a, 120), rl(far_left, 56)))
    return jnp.concatenate([nb, f[16:48], na], axis=0)


def strip_y(f):
    low = sub_iota() < 4
    parts = []
    for i in range(4):
        x, y = f[16 * i : 16 * i + 8], f[16 * i + 8 : 16 * i + 16]
        parts.append(x + jnp.where(low, rs(rl(y, 1), 4), 0.0))
        parts.append(y + jnp.where(low, 0.0, rs(rl(x, 127), 4)))
    return jnp.concatenate(parts, axis=0)


def inverse_mass(m):
    return jnp.where(m > 0.5, PUSH / jnp.where(m > 0.5, m, 1.0), 0.0)


def strip_arrays(z1o, z2o, z1s, z2s):
    q = lane_iota(64) // 32

    def four(a, b, c, d):
        return jnp.where(q < 2, jnp.where(q == 0, a, b), jnp.where(q == 2, c, d))

    us = jnp.where(q < 2, z1o, rl(z1s, 64))
    m0 = four(rl(z1o, 64), rl(z1o, 96), z1s, rl(z1s, 32))
    m1 = four(rl(z1o, 32), rl(z1o, 64), rl(z1s, 96), z1s)
    m2 = four(z2o, rl(z2o, 32), rl(z2s, 64), rl(z2s, 96))
    mass = four(rl(z2o, 96), z2o, rl(z2s, 32), rl(z2s, 64))
    return us, jnp.concatenate([m0, m1, m2], axis=0), mass


def state_expand(xu, xw, mk):
    return jnp.where(mk["lo"], xu, rs(xw, 4)), jnp.where(mk["lo"], rs(xu, 4), xw)


def tile(ref, p):
    return ref[8 * p : 8 * p + 8, :]


def first_kernel(
    u_hbm, w_hbm, mod_hbm, mass_hbm, z_ref, state_ref, f_ref, left_ref, right_ref,
    u_ref, w_ref, m_ref, mass_ref, sems,
):
    copies = [
        pltpu.make_async_copy(src, dst, sems.at[i])
        for i, (src, dst) in enumerate(
            ((u_hbm, u_ref), (w_hbm, w_ref), (mod_hbm, m_ref), (mass_hbm, mass_ref))
        )
    ]
    for c in copies:
        c.start()
    for c in copies:
        c.wait()
    mk = masks()
    even = mk["even"]
    lane = lane_iota(64)
    pieces = (
        (w_ref, 0, 0, 0),
        (u_ref, 0, 0, 1),
        (m_ref, 0, 0, 2),
        (m_ref, 256, 0, 3),
        (m_ref, 512, 1, 0),
        (mass_ref, 0, 1, 1),
    )
    z = [jnp.zeros((64, 128), jnp.float32), jnp.zeros((64, 128), jnp.float32)]
    for ref, base, half, slot in pieces:
        for side in range(2):
            for r in range(2):
                rows = ref[pl.ds(base + 2 * (1 - side) + r, 64, stride=4), :]
                dest = slot * 32 + (1 - side) * 16 + (1 - r) * 8 + (3 if side else 1)
                src = 0 if side else 124
                moved = rl(rows, (dest - src) % 128)
                z[half] = jnp.where((lane >= dest) & (lane < dest + 4), moved, z[half])
    z_ref[0] = z[0]
    z_ref[1] = z[1]
    base = 0
    for ref in (u_ref, w_ref, m_ref, mass_ref):
        count = ref.shape[0] // 16
        for p in range(count):
            x, y = tile(ref, 2 * p), tile(ref, 2 * p + 1)
            left_ref[base + p] = jnp.where(even, x, rs(y, 1))
            right_ref[base + p] = jnp.where(even, rs(x, 7), y)
        base += count
    for p in range(32):
        a, b = state_expand(tile(u_ref, p), tile(w_ref, p), mk)
        state_ref[0, 2 * p] = a
        state_ref[0, 2 * p + 1] = b
    forces(lambda n: state_ref[0, n], into(f_ref, 0), lambda p: tile(m_ref, p), mk)
    packs = (
        (FAR, far_pack(lambda n: f_ref[0, n], mk)),
        (MFAR, far_pack(lambda n: expanded(tile(mass_ref, n // 2), n % 2, mk), mk)),
    )
    for at, (left, right) in packs:
        for p in range(8):
            left_ref[at + p] = left[p]
            right_ref[at + p] = right[p]


def strip_kernel(sub_ref, z_ref, cf_ref, left_ref, right_ref, zo_ref):
    sub = sub_ref[0]
    lane = lane_iota(64)
    side0 = ((lane // 16) % 2) == 1
    c = lane % 8
    below, above = jnp.maximum(sub - 1, 0), jnp.minimum(sub + 1, 3)
    zs = []
    for half in range(2):
        own = z_ref[sub, half]
        zl = jnp.where(sub > 0, z_ref[below, half], 0.0)
        zr = jnp.where(sub < 3, z_ref[above, half], 0.0)
        low = jnp.where(c == 0, 0.0, jnp.where(c <= 4, zl, rl(own, 18)))
        high = jnp.where(c <= 2, rl(own, 110), jnp.where(c == 7, 0.0, zr))
        z = jnp.where(side0, low, high)
        zo_ref[half] = z
        zs.append(z)
    zero = jnp.zeros((64, 128), jnp.float32)
    us, mods, mass = strip_arrays(zs[0], zs[1], zero, zero)
    fs = strip_forces(us, mods, cf_ref)
    evg = ((lane // 8) % 2) == 0
    wl = jnp.where(evg, rl(zs[1], 120), zs[0])
    wr = jnp.where(evg, zs[0], rl(zs[1], 8))
    for p in range(8):
        left_ref[ZST + p] = wl[8 * p : 8 * p + 8]
        right_ref[ZST + p] = wr[8 * p : 8 * p + 8]
    for p in range(2):
        left_ref[SFAR + p] = fs[8 * p : 8 * p + 8]
        right_ref[SFAR + p] = fs[48 + 8 * p : 56 + 8 * p]
        left_ref[SMFAR + p] = mass[8 * p : 8 * p + 8]
        right_ref[SMFAR + p] = mass[48 + 8 * p : 56 + 8 * p]


def rows16(ref, at):
    return jnp.concatenate([ref[at], ref[at + 1]], axis=0)


def shadow_kernel(
    mod_ref, mass_ref, mr_ref, ml_ref, order_ref, mm_ref, us_ref, mass2_ref, f_ref
):
    mk = masks()
    even = mk["even"]

    def shadow(p):
        r, l = mr_ref[p], ml_ref[p]
        return jnp.where(even, r, rs(l, 1)), jnp.where(even, rs(r, 7), l)

    for p in range(16):
        su, sw = shadow(p), shadow(16 + p)
        for e in range(2):
            us_ref[0, 4 * p + 2 * e], us_ref[0, 4 * p + 2 * e + 1] = state_expand(su[e], sw[e], mk)
    for p in range(48):
        mm_ref[1, 2 * p], mm_ref[1, 2 * p + 1] = shadow(32 + p)
    for p in range(96):
        mm_ref[0, p] = mod_ref[p]
    for p in range(16):
        sm = shadow(80 + p)
        for e in range(2):
            for o in range(2):
                mass2_ref[1, 4 * p + 2 * e + o] = expanded(sm[e], o, mk)
    for p in range(32):
        for o in range(2):
            mass2_ref[0, 2 * p + o] = expanded(mass_ref[p], o, mk)
    forces(lambda n: us_ref[0, n], into(f_ref, 0), lambda p: mm_ref[1, p], mk)


def middle_kernel(
    mm_ref, mass2_ref, u0_ref, us0_ref, f0_ref, f0s_ref, mr_ref, ml_ref, zo_ref, sr_ref, sl_ref,
    cf_ref,
    bl_ref, br_ref, inv_ref, u1_ref, v1_ref, f1_ref, u2_ref, v2_ref, f2_ref,
    smod_ref, sinv_ref, sstate_ref, sx,
):
    mk = masks()
    wr = jnp.concatenate([sr_ref[ZST + p] for p in range(8)], axis=0)
    wl = jnp.concatenate([sl_ref[ZST + p] for p in range(8)], axis=0)
    evg = ((lane_iota(64) // 8) % 2) == 0
    z1s = jnp.where(evg, wl, wr)
    z2s = jnp.where(evg, rl(wl, 120), rl(wr, 8))
    us, mods, smass = strip_arrays(zo_ref[0], zo_ref[1], z1s, z2s)
    smod_ref[...] = mods
    smass = strip_x(smass, rows16(sr_ref, SMFAR), rows16(sl_ref, SMFAR))
    sx[0] = smass
    sinv = inverse_mass(strip_y(smass))
    sinv_ref[...] = sinv
    for h in range(2):
        for i in range(4):
            for k in range(4):
                line = assembled(
                    lambda hh, n: mass2_ref[hh, n], (mr_ref, ml_ref, MFAR), sx.at[0], h, i, k, mk
                )
                for j, total in enumerate(line):
                    inv_ref[h, 16 * i + 4 * j + k] = inverse_mass(total)
    fs = strip_forces(us, mods, cf_ref)
    fs = strip_x(fs, rows16(sr_ref, SFAR), rows16(sl_ref, SFAR))
    sx[1] = fs
    svel = -sinv * strip_y(fs)
    us = us + svel

    def first_forces(h, n):
        return f0s_ref[0, n] if h else f0_ref[0, n]

    for h in range(2):

        def put(n, disp, vel):
            u1_ref[h, n] = disp
            v1_ref[h, n] = vel

        update(
            first_forces, (mr_ref, ml_ref, FAR), sx.at[1], h, mk, lambda n: inv_ref[h, n],
            lambda n: us0_ref[0, n] if h else u0_ref[0, n], None, put,
        )

    def both(h, carry):
        forces(lambda n: u1_ref[h, n], into(f1_ref, h), lambda p: mm_ref[h, p], mk)
        return carry

    lax.fori_loop(0, 2, both, 0)
    fs = strip_forces(us, mods, cf_ref)
    sstate_ref[0] = us
    sstate_ref[1] = svel
    sstate_ref[2] = fs
    left, right = far_pack(lambda n: f1_ref[0, n], mk)
    for p in range(8):
        bl_ref[p] = left[p]
        br_ref[p] = right[p]
    for p in range(2):
        bl_ref[16 + p] = fs[8 * p : 8 * p + 8]
        br_ref[16 + p] = fs[48 + 8 * p : 56 + 8 * p]
    zero = jnp.zeros((16, 128), jnp.float32)
    fs = strip_x(fs, zero, zero)
    sx[2] = fs
    svel = svel - sinv * strip_y(fs)
    us = us + svel

    def put2(n, disp, vel):
        u2_ref[0, n] = disp
        v2_ref[0, n] = vel

    update(
        lambda h, n: f1_ref[h, n], None, sx.at[2], 0, mk, lambda n: inv_ref[0, n],
        lambda n: u1_ref[0, n], lambda n: v1_ref[0, n], put2,
    )
    forces(lambda n: u2_ref[0, n], into(f2_ref, 0), lambda p: mm_ref[0, p], mk)
    fs = strip_forces(us, mods, cf_ref)
    left, right = far_pack(lambda n: f2_ref[0, n], mk)
    for p in range(8):
        bl_ref[8 + p] = left[p]
        br_ref[8 + p] = right[p]
    for p in range(2):
        bl_ref[18 + p] = fs[8 * p : 8 * p + 8]
        br_ref[18 + p] = fs[48 + 8 * p : 56 + 8 * p]


def density_kernel(mm_ref, u0_ref, u1_ref, u2_ref, owner_ref, d2_ref, x0_ref, x1_ref, hot_ref):
    mk = masks()
    lo = mk["lo"]
    for direction in (2, 1, 0):
        for a in range(4):
            for b in range(4):
                nodes = line_nodes(direction, a, b)
                g0 = d_line(*[u0_ref[0, n] for n in nodes])
                g1 = d_line(*[u1_ref[0, n] for n in nodes])
                g2 = d_line(*[u2_ref[0, n] for n in nodes])
                for e, n in enumerate(nodes):
                    at = 64 * direction + n
                    m = expanded(mm_ref[0, at // 2], at % 2, mk)
                    x0_ref[at] = jnp.where(lo, m * rs(g0[e], 4), 0.0)
                    x1_ref[at] = m * rs(g1[e], 4)
                    t = jnp.where(lo, m * g2[e] * rs(g2[e], 4), 0.0)
                    d2_ref[n] = t if direction == 2 else d2_ref[n] + t
    block = lax.broadcasted_iota(jnp.int32, (512, 128), 0)
    for s in range(4):
        owner = jnp.broadcast_to(owner_ref[s : s + 1, :], (512, 128))
        hot_ref[:, 128 * s : 128 * s + 128] = (
            (block == owner).astype(jnp.float32).astype(jnp.bfloat16)
        )


def three_way(x):
    hi = x.astype(jnp.bfloat16)
    rest = x - hi.astype(jnp.float32)
    mid = rest.astype(jnp.bfloat16)
    return hi, mid, (rest - mid.astype(jnp.float32)).astype(jnp.bfloat16)


def last_kernel(
    br_ref, bl_ref, mm_ref, inv_ref, u1_ref, v1_ref, f1_ref, u2_ref, v2_ref, f2_ref,
    smod_ref, sinv_ref, sstate_ref, d2_ref, x0_ref, x1_ref, hot_ref, cf_ref,
    out_u_ref, out_w_ref, sums_ref,
    u, v, f, sx, dens,
):
    mk = masks()
    lo = mk["lo"]
    mods, sinv = smod_ref[...], sinv_ref[...]
    us, svel, fs = sstate_ref[0], sstate_ref[1], sstate_ref[2]

    def put(h):
        def store(n, disp, vel):
            u[h, n] = disp
            v[h, n] = vel

        return store

    fs = strip_x(fs, rows16(br_ref, 16), rows16(bl_ref, 16))
    sx[0] = fs
    svel = svel - sinv * strip_y(fs)
    us = us + svel
    update(
        lambda h, n: f1_ref[h, n], (br_ref, bl_ref, 0), sx.at[0], 1, mk, lambda n: inv_ref[1, n],
        lambda n: u1_ref[1, n], lambda n: v1_ref[1, n], put(1),
    )
    forces(lambda n: u[1, n], into(f, 1), lambda p: mm_ref[1, p], mk)
    fs = strip_forces(us, mods, cf_ref)
    fs = strip_x(fs, rows16(br_ref, 18), rows16(bl_ref, 18))
    sx[1] = fs
    svel = svel - sinv * strip_y(fs)
    us = us + svel

    def step_two(h, n):
        return f[1, n] if h else f2_ref[0, n]

    far = (br_ref, bl_ref, 8)
    update(
        step_two, far, sx.at[1], 0, mk, lambda n: inv_ref[0, n],
        lambda n: u2_ref[0, n], lambda n: v2_ref[0, n], put(0),
    )
    update(
        step_two, far, sx.at[1], 1, mk, lambda n: inv_ref[1, n],
        lambda n: u[1, n], lambda n: v[1, n], put(1),
    )

    def add_third(direction, n, g):
        at = pl.ds(8 * n, 8)
        before = d2_ref[n] if direction == 2 else dens[at, :]
        dens[at, :] = before + x1_ref[64 * direction + n] * g

    forces(lambda n: u[1, n], into(f, 1), lambda p: mm_ref[1, p], mk, planes=(0, 3))
    forces(lambda n: u[0, n], into(f, 0), lambda p: mm_ref[0, p], mk, hook=add_third)
    fs = strip_forces(us, mods, cf_ref)
    zero = jnp.zeros((16, 128), jnp.float32)
    sx[2] = strip_x(fs, zero, zero)
    update(
        lambda h, n: f[h, n], None, sx.at[2], 0, mk, lambda n: inv_ref[0, n],
        lambda n: u[0, n], lambda n: v[0, n], put(0),
    )
    for direction in (2, 1, 0):
        for a in range(4):
            for b in range(4):
                nodes = line_nodes(direction, a, b)
                for n, g in zip(nodes, d_line(*[u[0, n] for n in nodes])):
                    at = pl.ds(8 * n, 8)
                    dens[at, :] = dens[at, :] + x0_ref[64 * direction + n] * g
    cols = [
        dens[pl.ds(s, 64, stride=8), :] + dens[pl.ds(s + 4, 64, stride=8), :] for s in range(4)
    ]
    split = jnp.concatenate(three_way(jnp.concatenate(cols, axis=1)), axis=0)
    res = lax.dot_general(
        split, hot_ref[...], (((1,), (1,)), ((), ())), preferred_element_type=jnp.float32
    )
    sums = res[0:64] + (res[64:128] + res[128:192])
    for q in range(4):
        sums_ref[q] = sums[:, 128 * q : 128 * q + 128]
    for p in range(32):
        a, b = u[0, 2 * p], u[0, 2 * p + 1]
        out_u_ref[p] = jnp.where(lo, a, rs(b, 4))
        out_w_ref[p] = jnp.where(lo, rs(a, 4), b)


def project_kernel(x_ref, basis_ref, out_ref):
    total = (x_ref[0] + x_ref[1]) + (x_ref[2] + x_ref[3])
    t0, t1, t2 = three_way(total)
    b0, b1, b2 = three_way(basis_ref[...])
    out_ref[...] = KERNEL_SCALE * jnp.dot(
        jnp.concatenate([b0, b1, b0, b1, b0, b2], axis=1),
        jnp.concatenate([t0, t0, t1, t1, t2, t0], axis=0),
        preferred_element_type=jnp.float32,
    )


VMEM = pl.BlockSpec(memory_space=pltpu.VMEM)
SMEM = pl.BlockSpec(memory_space=pltpu.SMEM)
HBM = pl.BlockSpec(memory_space=pltpu.HBM)
F32, BF16 = jnp.float32, jnp.bfloat16


def call(kernel, outs, ins, scratch=(), specs=(), limit=24):
    specs = list(specs) + [VMEM] * (len(ins) - len(specs))
    outs = [o if isinstance(o, jax.ShapeDtypeStruct) else jax.ShapeDtypeStruct(o, F32) for o in outs]
    return pl.pallas_call(
        kernel,
        out_shape=outs,
        in_specs=specs,
        out_specs=[VMEM] * len(outs),
        scratch_shapes=list(scratch),
        compiler_params=pltpu.CompilerParams(vmem_limit_bytes=limit * 1024 * 1024),
    )(*ins)


def raw_tiles(x):
    lead = int(np.prod(x.shape[:-2]))
    return x.reshape(lead, 2, 2, 128).transpose(0, 2, 1, 3).reshape(lead * 4, 128)


def from_tiles(x):
    return x.reshape(64, 2, 2, 128).transpose(0, 2, 1, 3).reshape(64, 2, 256)


def on_device(initial_field, adjoint_source, moduli, node_mass, block_owner, spline_basis):
    count = lax.axis_size("dom")
    to_right = [(i, i + 1) for i in range(count - 1)]
    to_left = [(b, a) for a, b in to_right]
    cf = jnp.asarray(COEFFICIENTS)
    sub = lax.axis_index("sub").astype(jnp.int32).reshape(1)
    u2d, w2d, m2d, mass2d = map(raw_tiles, (initial_field, adjoint_source, moduli, node_mass))
    owner = raw_tiles(block_owner[None])
    mass = mass2d.reshape(32, 8, 128)
    mod = m2d.reshape(96, 8, 128)
    one, two = (1, 64, 8, 128), (2, 64, 8, 128)

    def swap_rows(left, right):
        return lax.ppermute(left, "dom", to_left), lax.ppermute(right, "dom", to_right)

    edges, u0, f0, left, right = call(
        first_kernel,
        [(2, 64, 128), one, one, (MSG, 8, 128), (MSG, 8, 128)],
        [u2d, w2d, m2d, mass2d],
        [pltpu.VMEM((n, 128), F32) for n in (256, 256, 768, 256)] + [pltpu.SemaphoreType.DMA((4,))],
        [HBM] * 4,
        limit=FIRST_LIMIT,
    )
    raw_right, raw_left = swap_rows(left, right)
    edges = lax.all_gather(edges, "sub")
    left, right, zo = call(
        strip_kernel,
        [(MSG_S, 8, 128), (MSG_S, 8, 128), (2, 64, 128)],
        [sub, edges, cf],
        specs=[SMEM],
    )
    strip_right, strip_left = swap_rows(left, right)
    mm, us0, mass2, f0s = call(
        shadow_kernel,
        [(2, 96, 8, 128), one, two, one],
        [mod, mass, raw_right, raw_left, zo],
        specs=[VMEM] * 4 + [pl.BlockSpec(memory_space=pl.ANY)],
    )
    bl, br, inv, u1, v1, f1, u2, v2, f2, smod, sinv, sstate = call(
        middle_kernel,
        [
            (MSG_B, 8, 128), (MSG_B, 8, 128), two, two, two, two, one, one, one,
            (192, 128), (64, 128), (3, 64, 128),
        ],
        [mm, mass2, u0, us0, f0, f0s, raw_right, raw_left, zo, strip_right, strip_left, cf],
        [pltpu.VMEM((3, 64, 128), F32)],
    )
    far_right, far_left = swap_rows(bl, br)
    d2, x0, x1, hot = call(
        density_kernel,
        [(64, 8, 128), (192, 8, 128), (192, 8, 128), jax.ShapeDtypeStruct((512, 512), BF16)],
        [mm, u0, u1, u2, owner],
    )
    out_u, out_w, sums = call(
        last_kernel,
        [(32, 8, 128), (32, 8, 128), (4, 64, 128)],
        [
            far_right, far_left, mm, inv, u1, v1, f1, u2, v2, f2, smod, sinv, sstate,
            d2, x0, x1, hot, cf,
        ],
        [pltpu.VMEM(two, F32)] * 3 + [pltpu.VMEM((3, 64, 128), F32), pltpu.VMEM((512, 128), F32)],
    )
    sums = lax.all_to_all(sums, "sub", 0, 0)
    (kernel,) = call(project_kernel, [(64, 128)], [sums, spline_basis.T])
    return from_tiles(out_u), from_tiles(out_w), kernel


def solution(mesh):
    in_specs = (
        P(None, "dom", "sub"),
        P(None, "dom", "sub"),
        P(None, None, "dom", "sub"),
        P(None, "dom", "sub"),
        P("dom", "sub"),
        P(),
    )
    out_specs = (P(None, "dom", "sub"), P(None, "dom", "sub"), P(None, ("dom", "sub")))
    return jax.shard_map(
        on_device, mesh=mesh, in_specs=in_specs, out_specs=out_specs, check_vma=False
    )
```

time: 76.2 us -> 72.9 us (0.957)
  waiting for transfers between devices: 25.5 us -> 12.3 us
  blocking collectives: 7.93 us -> 17.9 us
  starting transfers between devices: 26 us -> 30.7 us
  local copies, waits for them, and re-layouts: 5.08 us -> 0.78 us
    ppermute x4 -> x6, waiting for transfers between devices: 20.5 us -> 7.28 us  [the longest x3 7.27 us: swap_rows(): lax.ppermute(right, 'dom', to_right)]
    all_gather x1, blocking collectives: 7.93 us -> 17.9 us  [on_device(): edges = lax.all_gather(edges, 'sub')]
    ppermute x4 -> x6, starting transfers between devices: 19.4 us -> 24.8 us  [the longest x3 16.2 us: swap_rows(): lax.ppermute(left, 'dom', to_left)]
    unnamed x25 -> x15, local copies, waits for them, and re-layouts: 5.08 us -> 0.78 us
    pallas_call x6 -> x7, Pallas kernels: 10 us -> 9.52 us  [call(): pl.pallas_call(kernel, out_shape=outs, in_specs=specs, out_specs=[VMEM] *...]
  transfers between devices with their start and end apart: 5 -> 7, of which waited for: 4 -> 3; matrix products, arithmetic and copies ran while one was open for 0% -> 0% of each run, Pallas kernels for 0% -> 2%
where the time goes in v2:
time: 72.9 us; the launch traced here: 72.1 us
  starting transfers between devices  30.7 us (42%)
  blocking collectives  17.9 us (25%)
  waiting for transfers between devices  12.3 us (17%)
  Pallas kernels  9.52 us (13%)
  between operations  0.8 us (1%)
  local copies, waits for them, and re-layouts  0.78 us (1%)
    all_gather x1, blocking collectives, on_device(): edges = lax.all_gather(edges, 'sub')  17.9 us
    ppermute x3, starting transfers between devices, swap_rows(): lax.ppermute(left, 'dom', to_left)  16.2 us
    pallas_call x7, Pallas kernels, call(): pl.pallas_call(kernel, out_shape=outs, in_specs=specs, out_specs=[VMEM] *...  9.52 us
    ppermute x3, starting transfers between devices, swap_rows(): lax.ppermute(right, 'dom', to_right)  8.64 us
    ppermute x3, waiting for transfers between devices, swap_rows(): lax.ppermute(right, 'dom', to_right)  7.27 us
    all_to_all x1, starting transfers between devices, on_device(): sums = lax.all_to_all(sums, 'sub', 0, 0)  5.88 us
    all_to_all x1, waiting for transfers between devices, on_device(): sums = lax.all_to_all(sums, 'sub', 0, 0)  5.03 us
  transfers between devices with their start and end apart: 7, of which 3 were waited for; matrix products, arithmetic and copies ran while one was open for 0% of the time, Pallas kernels for 2%

profile of v2, /device:TPU:25, one launch (start us, length us, event | category | flops | bytes accessed | tf_op | source)
XLA Modules:
  0.0 72.1 jit_solution(7765896490190739347)
XLA Ops:
  0.6 0.0 copy-start.1
  0.6 2.8 %shard_map.94 = (f32[2,64,128]{2,1,0:T(8,128)}, f32[1,64,8,128]{3,2,1,0:T(8,128)}, f32[1,64,8,128]{3,2,1,0:T(8,128)}, f32[112,8,128]{2,1,0:T(8,128)}, f32[112,8,128]{2,1,0:T(8,128)}) custom-call(f32[256,128]{1,0:T(8,128)} %bitcast.49, f32[256,128]{1,0:T(8,128)} %bitcast.50, f32[768,128]{1,0:T(8,128)} %bitcast.42, f32[256,128]{1,0:T(8,128)} %bitcast.45), custom_call_target="tpu_custom_call" | custom-call | tf_op jit(solution)/shard_map/pallas_call | solution.py:620
  3.4 0.0 copy-start
  3.4 12.4 %collective-permute-start = (f32[112,8,128]{2,1,0:T(8,128)}, f32[112,8,128]{2,1,0:T(8,128)S(1)}, u32[]{:S(2)}, u32[]{:S(2)}) collective-permute-start(f32[112,8,128]{2,1,0:T(8,128)} %get-tuple-element.34), channel_id=1, source_target_pairs={{4,0},{8,4},{12,8},{16,12},{20,16},{24,20},{28,24},{32,28},{36,32}... | collective-permute-start | bytes 1376264 | tf_op jit(solution)/shard_map/ppermute | solution.py:652
  15.8 1.9 %collective-permute-start.1 = (f32[112,8,128]{2,1,0:T(8,128)}, f32[112,8,128]{2,1,0:T(8,128)S(1)}, u32[]{:S(2)}, u32[]{:S(2)}) collective-permute-start(f32[112,8,128]{2,1,0:T(8,128)} %get-tuple-element.35), channel_id=1, source_target_pairs={{0,4},{4,8},{8,12},{12,16},{16,20},{20,24},{24,28},{28,32},{32,36}... | collective-permute-start | bytes 1376264 | tf_op jit(solution)/shard_map/ppermute | solution.py:652
  17.7 17.9 %all-gather = f32[8,64,128]{2,1,0:T(8,128)S(1)} all-gather(f32[2,64,128]{2,1,0:T(8,128)} %get-tuple-element.36), channel_id=2, replica_groups=mesh['dom'=128,'sub'=4] {'sub'}, dimensions={0}, use_global_device_ids=true | all-gather | bytes 327680 | tf_op jit(solution)/shard_map/all_gather | solution.py:663
  35.7 0.2 shard_map.95
  35.9 1.9 %collective-permute-start.2 = (f32[12,8,128]{2,1,0:T(8,128)S(1)}, f32[12,8,128]{2,1,0:T(8,128)S(1)}, u32[]{:S(2)}, u32[]{:S(2)}) collective-permute-start(f32[12,8,128]{2,1,0:T(8,128)S(1)} %get-tuple-element.44), channel_id=1, source_target_pairs={{4,0},{8,4},{12,8},{16,12},{20,16},{24,20},{28,24},{32,28},{36,32}... | collective-permute-start | bytes 147464 | tf_op jit(solution)/shard_map/ppermute | solution.py:652
  37.8 3.4 %collective-permute-start.3 = (f32[12,8,128]{2,1,0:T(8,128)S(1)}, f32[12,8,128]{2,1,0:T(8,128)S(1)}, u32[]{:S(2)}, u32[]{:S(2)}) collective-permute-start(f32[12,8,128]{2,1,0:T(8,128)S(1)} %get-tuple-element.45), channel_id=1, source_target_pairs={{0,4},{4,8},{8,12},{12,16},{16,20},{20,24},{24,28},{28,32},{32,36}... | collective-permute-start | bytes 147464 | tf_op jit(solution)/shard_map/ppermute | solution.py:652
  41.2 0.0 collective-permute-done.1.ml_ref
  41.2 0.4 shard_map.96
  41.7 4.0 %collective-permute-done.3.sl_ref = f32[12,8,128]{2,1,0:T(8,128)S(1)} collective-permute-done((f32[12,8,128]{2,1,0:T(8,128)S(1)}, f32[12,8,128]{2,1,0:T(8,128)S(1)}, u32[]{:S(2)}, u32[]{:S(2)}) %collective-permute-start.3) | collective-permute-done | bytes 49184 | tf_op jit(solution)/shard_map/ppermute | solution.py:652
  45.6 1.9 %shard_map.97 = (f32[20,8,128]{2,1,0:T(8,128)S(1)}, f32[20,8,128]{2,1,0:T(8,128)S(1)}, f32[2,64,8,128]{3,2,1,0:T(8,128)S(1)}, f32[2,64,8,128]{3,2,1,0:T(8,128)S(...) custom-call(f32[2,96,8,128]{3,2,1,0:T(8,128)S(1)} %get-tuple-element, ...), custom_call_target="tpu_custom_call" | custom-call | tf_op jit(solution)/shard_map/pallas_call | solution.py:620
  47.5 1.9 %collective-permute-start.4 = (f32[20,8,128]{2,1,0:T(8,128)S(1)}, f32[20,8,128]{2,1,0:T(8,128)S(1)}, u32[]{:S(2)}, u32[]{:S(2)}) collective-permute-start(f32[20,8,128]{2,1,0:T(8,128)S(1)} %get-tuple-element.46), channel_id=1, source_target_pairs={{4,0},{8,4},{12,8},{16,12},{20,16},{24,20},{28,24},{32,28},{36,32}... | collective-permute-start | bytes 245768 | tf_op jit(solution)/shard_map/ppermute | solution.py:652
  49.5 3.4 %collective-permute-start.5 = (f32[20,8,128]{2,1,0:T(8,128)S(1)}, f32[20,8,128]{2,1,0:T(8,128)S(1)}, u32[]{:S(2)}, u32[]{:S(2)}) collective-permute-start(f32[20,8,128]{2,1,0:T(8,128)S(1)} %get-tuple-element.47), channel_id=1, source_target_pairs={{0,4},{4,8},{8,12},{12,16},{16,20},{20,24},{24,28},{28,32},{32,36}... | collective-permute-start | bytes 245768 | tf_op jit(solution)/shard_map/ppermute | solution.py:652
  52.8 0.0 copy-start.5
  52.8 0.7 copy-done.5
  53.5 0.8 %shard_map.98 = (f32[64,8,128]{2,1,0:T(8,128)S(1)}, f32[192,8,128]{2,1,0:T(8,128)S(1)}, f32[192,8,128]{2,1,0:T(8,128)S(1)}, bf16[512,512]{1,0:T(8,128)(2,1)S(1)}) custom-call(f32[2,96,8,128]{3,2,1,0:T(8,128)S(1)} %get-tuple-element.38.mm_ref, f32[1,64,8,128]{3,2,1,0:T(8,128)S(1)} %copy-done.2, f32[2,64,8,128]{3,2,1,0:T(8,128)S(1)} %get-tuple-element.49.u1_ref, ...), custom_call_target="tpu_custom_call" | custom-call | tf_op jit(solution)/shard_map/pallas_call | solution.py:620
  54.4 3.3 %collective-permute-done.5.bl_ref = f32[20,8,128]{2,1,0:T(8,128)S(1)} collective-permute-done((f32[20,8,128]{2,1,0:T(8,128)S(1)}, f32[20,8,128]{2,1,0:T(8,128)S(1)}, u32[]{:S(2)}, u32[]{:S(2)}) %collective-permute-start.5) | collective-permute-done | bytes 81952 | tf_op jit(solution)/shard_map/ppermute | solution.py:652
  57.7 2.6 %shard_map.99 = (f32[32,8,128]{2,1,0:T(8,128)}, f32[32,8,128]{2,1,0:T(8,128)}, f32[4,64,128]{2,1,0:T(8,128)}) custom-call(f32[20,8,128]{2,1,0:T(8,128)S(1)} %collective-permute-done.4.br_ref, f32[20,8,128]{2,1,0:T(8,128)S(1)} %collective-permute-done.5.bl_ref, f32[2,96,8,128]{3,2,1,0:T(8,128)S(1)} %get-tuple-element.38.mm_ref, ...), custom_call_target="tpu_custom_call" | custom-call | tf_op jit(solution)/shard_map/pallas_call | solution.py:620
  60.3 5.9 %all-to-all-start = ((f32[4,64,128]{2,1,0:T(8,128)}), f32[4,64,128]{2,1,0:T(8,128)S(1)}, u32[]{:S(2)}, u32[]{:S(2)}) async-start(f32[4,64,128]{2,1,0:T(8,128)} %get-tuple-element.64), calls=%async_computation | async-start | bytes 262144 | tf_op jit(solution)/shard_map/all_to_all | solution.py:701
  66.2 0.1 copy.25
  66.2 5.0 %all-to-all-done.x_ref = f32[4,64,128]{2,1,0:T(8,128)S(1)} async-done(((f32[4,64,128]{2,1,0:T(8,128)}), f32[4,64,128]{2,1,0:T(8,128)S(1)}, u32[]{:S(2)}, u32[]{:S(2)}) %all-to-all-start) | async-done | bytes 131104 | tf_op jit(solution)/shard_map/all_to_all | solution.py:701
  71.3 0.8 %shard_map.100 = f32[64,128]{1,0:T(8,128)} custom-call(f32[4,64,128]{2,1,0:T(8,128)S(1)} %all-to-all-done.x_ref, f32[64,64]{1,0:T(8,128)S(1)} %bitcast.47), custom_call_target="tpu_custom_call" | custom-call | tf_op jit(solution)/shard_map/pallas_call | solution.py:620
  (13 shorter events, 0.0 us)
Async XLA Ops:
  0.6 35.0 %copy-start.1 = (f32[30,8,128]{2,1,0:T(8,128)S(1)}, f32[30,8,128]{2,1,0:T(8,128)}, u32[]{:S(2)}) copy-start(f32[30,8,128]{2,1,0:T(8,128)} %constant.6.clone.cf_ref) | copy-start | bytes 368644
  3.4 37.8 %copy-start = (f32[3,64,2,256]{3,2,1,0:T(2,128)S(1)}, f32[3,64,2,256]{3,2,1,0:T(2,128)}, u32[]{:S(2)}) copy-start(f32[3,64,2,256]{3,2,1,0:T(2,128)} %param.9) | copy-start | bytes 1179652
  3.4 37.8 %collective-permute-start = (f32[112,8,128]{2,1,0:T(8,128)}, f32[112,8,128]{2,1,0:T(8,128)S(1)}, u32[]{:S(2)}, u32[]{:S(2)}) collective-permute-start(f32[112,8,128]{2,1,0:T(8,128)} %get-tuple-element.34), channel_id=1, source_target_pairs={{4,0},{8,4},{12,8},{16,12},{20,16},{24,20},{28,24},{32,28},{36,32}... | collective-permute-start | bytes 1376264 | tf_op jit(solution)/shard_map/ppermute | solution.py:652
  15.8 25.4 %collective-permute-start.1 = (f32[112,8,128]{2,1,0:T(8,128)}, f32[112,8,128]{2,1,0:T(8,128)S(1)}, u32[]{:S(2)}, u32[]{:S(2)}) collective-permute-start(f32[112,8,128]{2,1,0:T(8,128)} %get-tuple-element.35), channel_id=1, source_target_pairs={{0,4},{4,8},{8,12},{12,16},{16,20},{20,24},{24,28},{28,32},{32,36}... | collective-permute-start | bytes 1376264 | tf_op jit(solution)/shard_map/ppermute | solution.py:652
  35.7 5.5 %copy-start.3 = (f32[64,2,256]{2,1,0:T(2,128)S(1)}, f32[64,2,256]{2,1,0:T(2,128)}, u32[]{:S(2)}) copy-start(f32[64,2,256]{2,1,0:T(2,128)} %param.10) | copy-start | bytes 393220
  35.9 5.8 %collective-permute-start.2 = (f32[12,8,128]{2,1,0:T(8,128)S(1)}, f32[12,8,128]{2,1,0:T(8,128)S(1)}, u32[]{:S(2)}, u32[]{:S(2)}) collective-permute-start(f32[12,8,128]{2,1,0:T(8,128)S(1)} %get-tuple-element.44), channel_id=1, source_target_pairs={{4,0},{8,4},{12,8},{16,12},{20,16},{24,20},{28,24},{32,28},{36,32}... | collective-permute-start | bytes 147464 | tf_op jit(solution)/shard_map/ppermute | solution.py:652
  37.8 7.8 %collective-permute-start.3 = (f32[12,8,128]{2,1,0:T(8,128)S(1)}, f32[12,8,128]{2,1,0:T(8,128)S(1)}, u32[]{:S(2)}, u32[]{:S(2)}) collective-permute-start(f32[12,8,128]{2,1,0:T(8,128)S(1)} %get-tuple-element.45), channel_id=1, source_target_pairs={{0,4},{4,8},{8,12},{12,16},{16,20},{20,24},{24,28},{28,32},{32,36}... | collective-permute-start | bytes 147464 | tf_op jit(solution)/shard_map/ppermute | solution.py:652
  41.2 4.4 %copy-start.2 = (f32[1,64,8,128]{3,2,1,0:T(8,128)S(1)}, f32[1,64,8,128]{3,2,1,0:T(8,128)}, u32[]{:S(2)}) copy-start(f32[1,64,8,128]{3,2,1,0:T(8,128)} %get-tuple-element.40.u0_ref) | copy-start | bytes 786436
  41.2 4.4 %copy-start.4 = (f32[1,64,8,128]{3,2,1,0:T(8,128)S(1)}, f32[1,64,8,128]{3,2,1,0:T(8,128)}, u32[]{:S(2)}) copy-start(f32[1,64,8,128]{3,2,1,0:T(8,128)} %get-tuple-element.42.f0_ref) | copy-start | bytes 786436
  47.5 6.8 %collective-permute-start.4 = (f32[20,8,128]{2,1,0:T(8,128)S(1)}, f32[20,8,128]{2,1,0:T(8,128)S(1)}, u32[]{:S(2)}, u32[]{:S(2)}) collective-permute-start(f32[20,8,128]{2,1,0:T(8,128)S(1)} %get-tuple-element.46), channel_id=1, source_target_pairs={{4,0},{8,4},{12,8},{16,12},{20,16},{24,20},{28,24},{32,28},{36,32}... | collective-permute-start | bytes 245768 | tf_op jit(solution)/shard_map/ppermute | solution.py:652
  49.5 8.2 %collective-permute-start.5 = (f32[20,8,128]{2,1,0:T(8,128)S(1)}, f32[20,8,128]{2,1,0:T(8,128)S(1)}, u32[]{:S(2)}, u32[]{:S(2)}) collective-permute-start(f32[20,8,128]{2,1,0:T(8,128)S(1)} %get-tuple-element.47), channel_id=1, source_target_pairs={{0,4},{4,8},{8,12},{12,16},{16,20},{20,24},{24,28},{28,32},{32,36}... | collective-permute-start | bytes 245768 | tf_op jit(solution)/shard_map/ppermute | solution.py:652
  52.8 0.7 copy-start.5
  60.3 5.9 %copy-start.6 = (f32[64,64]{1,0:T(8,128)S(1)}, f32[64,64]{1,0:T(8,128)}, u32[]{:S(2)}) copy-start(f32[64,64]{1,0:T(8,128)} %param.12) | copy-start | bytes 49156
  60.3 11.0 %all-to-all-start = ((f32[4,64,128]{2,1,0:T(8,128)}), f32[4,64,128]{2,1,0:T(8,128)S(1)}, u32[]{:S(2)}, u32[]{:S(2)}) async-start(f32[4,64,128]{2,1,0:T(8,128)} %get-tuple-element.64), calls=%async_computation | async-start | bytes 262144 | tf_op jit(solution)/shard_map/all_to_all | solution.py:701

commit v3 on v2

v3 whole, which is shorter than its diff:
```python
import jax
import jax.numpy as jnp
import numpy as np
from jax import lax
from jax.experimental import pallas as pl
from jax.experimental.pallas import tpu as pltpu
from jax.sharding import PartitionSpec as P

STEPS = 4
TIME_STEP = 0.1
KERNEL_SCALE = 0.05
PUSH = TIME_STEP * TIME_STEP

DERIVATIVE = np.array(
    [
        [-3.0, 4.04508497187474, -1.54508497187474, 0.5],
        [-0.80901699437495, 0.0, 1.11803398874989, -0.30901699437495],
        [0.30901699437495, -1.11803398874989, 0.0, 0.80901699437495],
        [-0.5, 1.54508497187474, -4.04508497187474, 3.0],
    ]
)
HALF_AMB = float((DERIVATIVE[0, 1] - DERIVATIVE[0, 2]) / 2)
HALF_CME = float((DERIVATIVE[1, 0] - DERIVATIVE[1, 3]) / 2)
HALF_D = float(DERIVATIVE[1, 2] / 2)

MSG, CONST, STRIP = 38, 16, 32
MSG_B, STRIP_B = 18, 16
FIRST_LIMIT = 62


def strip_coefficients():
    tiles = []
    for d in (DERIVATIVE, DERIVATIVE.T):
        for out in range(2):
            for term in range(4):
                col = np.zeros(8)
                for s in range(8):
                    j = 2 * out + s // 4
                    half = s // 4 if term % 2 == 0 else 1 - s // 4
                    col[s] = d[j, 2 * (term // 2) + half]
                tiles.append(col)
        for delta in range(-3, 4):
            col = np.zeros(8)
            for s in range(8):
                k = s % 4
                if 0 <= k + delta < 4:
                    col[s] = d[k, k + delta]
            tiles.append(col)
    return np.broadcast_to(np.array(tiles, np.float32)[:, :, None], (30, 8, 128))


COEFFICIENTS = np.ascontiguousarray(strip_coefficients())


def sub_iota():
    return lax.broadcasted_iota(jnp.int32, (8, 128), 0)


def lane_iota(rows=8):
    return lax.broadcasted_iota(jnp.int32, (rows, 128), 1)


def rs(x, shift):
    return pltpu.roll(x, shift, 0)


def rl(x, shift):
    return pltpu.roll(x, shift, 1)


def masks():
    s = sub_iota()
    lane = lane_iota()
    return dict(
        even=(s % 2) == 0,
        lo=s < 4,
        ct0=((s // 2) % 2) == 0,
        first=lane == 0,
        last=lane == 127,
    )


def d_line(x0, x1, x2, x3):
    p, m, q, n = x0 + x3, x0 - x3, x1 + x2, x1 - x2
    r = q - p
    s1 = -1.75 * m + HALF_AMB * n
    s2 = HALF_CME * m - HALF_D * n
    r1, r2 = 1.25 * r, HALF_D * r
    return s1 + r1, s2 + r2, s2 - r2, s1 - r1


def dt_line(x0, x1, x2, x3):
    p, m, q, n = x0 + x3, x0 - x3, x1 + x2, x1 - x2
    t = 1.25 * m + HALF_D * n
    q1 = HALF_CME * q - 1.75 * p
    q2 = HALF_AMB * p - HALF_D * q
    return q1 - t, t + q2, t - q2, -(q1 + t)


def line_nodes(direction, a, b):
    if direction == 0:
        return [16 * i + 4 * a + b for i in range(4)]
    if direction == 1:
        return [16 * a + 4 * j + b for j in range(4)]
    return [16 * a + 4 * b + k for k in range(4)]


def expanded(x, upper, mk):
    r = rs(x, 4)
    return jnp.where(mk["lo"], r, x) if upper else jnp.where(mk["lo"], x, r)


def forces(u, f, mod, mk, planes=(0, 1, 2, 3), hook=None):
    for direction in (2, 1, 0):
        for a in range(4):
            if direction and a not in planes:
                continue
            for b in range(4):
                nodes = line_nodes(direction, a, b)
                g = d_line(*[u(n) for n in nodes])
                if hook is not None:
                    for n, gn in zip(nodes, g):
                        hook(direction, n, gn)
                t = []
                for n, gn in zip(nodes, g):
                    at = 64 * direction + n
                    t.append(expanded(mod(at // 2), at % 2, mk) * gn)
                for n, o in zip(nodes, dt_line(*t)):
                    if n // 16 in planes:
                        f(n, o, direction == 2)


def into(ref):
    def put(n, value, first):
        ref[n] = value if first else ref[n] + value

    return put


def face_tile(get, q, mk):
    return jnp.where(mk["even"], get(q), get(48 + q))


def pack_faces(left_ref, right_ref, base, get, mk):
    even = mk["even"]
    for p in range(8):
        x, y = get(2 * p), get(2 * p + 1)
        left_ref[base + p] = jnp.where(even, x, rs(y, 1))
        right_ref[base + p] = jnp.where(even, rs(x, 7), y)


def unpack_face(from_right, from_left, base, q, mk):
    r, l = from_right[base + q // 2], from_left[base + q // 2]
    if q % 2:
        return jnp.where(mk["even"], rs(l, 7), r)
    return jnp.where(mk["even"], l, rs(r, 1))


def face_response(delta, diagonal, mod_j, mod_k):
    out = [diagonal(q) * delta[q] for q in range(16)]
    for mod, lines in (
        (mod_j, [[4 * j + k for j in range(4)] for k in range(4)]),
        (mod_k, [[4 * j + k for k in range(4)] for j in range(4)]),
    ):
        for line in lines:
            t = [mod(q) * g for q, g in zip(line, d_line(*[delta[q] for q in line]))]
            for q, o in zip(line, dt_line(*t)):
                out[q] = out[q] + o
    return out


def along_x(f, beside, i, q, mk):
    even = mk["even"]
    x = f(16 * i + q)
    if i in (1, 2):
        return x
    other = beside(q) if beside is not None else 0.0
    if i == 3:
        return x + jnp.where(even, rs(f(q), 7), other)
    return x + jnp.where(even, other, rs(f(48 + q), 1))


def assembled(f, beside, strip, i, k, mk):
    vals = [along_x(f, beside, i, 4 * j + k, mk) for j in range(4)]

    def inject(row):
        return pltpu.roll(
            jnp.broadcast_to(strip[row : row + 1, :], (8, 128)), 68, 1, stride=8, stride_axis=0
        )

    b, a = vals[0], vals[3]
    up, down = rl(b, 127), rl(a, 1)
    up = jnp.where(mk["last"], jnp.where(mk["ct0"], rs(up, 6), inject(16 * i + k)), up)
    down = jnp.where(mk["first"], jnp.where(mk["ct0"], inject(16 * i + 12 + k), rs(down, 2)), down)
    return [b + down, vals[1], vals[2], a + up]


def assemble(f, beside, strip, mk, put, planes=(0, 1, 2, 3)):
    for i in planes:
        for k in range(4):
            for j, total in enumerate(assembled(f, beside, strip, i, k, mk)):
                put(16 * i + 4 * j + k, total)


def not_shared(n, x, mk):
    if n < 16:
        return jnp.where(mk["even"], 0.0, x)
    if n >= 48:
        return jnp.where(mk["even"], x, 0.0)
    return x


def strip_lines(x, cf, base):
    along_j, along_k = [], []
    for i in range(len(x) // 2):
        a, b = x[2 * i], x[2 * i + 1]
        terms = (a, rs(a, 4), b, rs(b, 4))
        for out in range(2):
            along_j.append(sum(cf[base + 4 * out + t] * terms[t] for t in range(4)))
    for y in x:
        along_k.append(
            sum(cf[base + 8 + d] * (rs(y, (3 - d) % 8) if d != 3 else y) for d in range(7))
        )
    return along_j, along_k


def strip_forces(us, mods, cf):
    x = [us[8 * v : 8 * v + 8] for v in range(8)]
    gj, gk = strip_lines(x, cf, 0)
    gi = [None] * 8
    for e in range(2):
        for i, g in enumerate(d_line(*[x[2 * m + e] for m in range(4)])):
            gi[2 * i + e] = g
    ti, tj, tk = (
        [mods[64 * d + 8 * v : 64 * d + 8 * v + 8] * g[v] for v in range(8)]
        for d, g in enumerate((gi, gj, gk))
    )
    fj = strip_lines(tj, cf, 15)[0]
    fk = strip_lines(tk, cf, 15)[1]
    f = [fj[v] + fk[v] for v in range(8)]
    for e in range(2):
        for i, o in enumerate(dt_line(*[ti[2 * m + e] for m in range(4)])):
            f[2 * i + e] = f[2 * i + e] + o
    return jnp.concatenate(f, axis=0)


def row_zero(rows):
    return ((lane_iota(rows) // 8) % 2) == 1


def strip_faces(f):
    return jnp.where(row_zero(16), f[0:16], f[48:64])


def strip_beside(from_right, from_left, base):
    r = jnp.concatenate([from_right[base], from_right[base + 1]], axis=0)
    l = jnp.concatenate([from_left[base], from_left[base + 1]], axis=0)
    both = jnp.where(row_zero(16), rl(l, 8), rl(r, 120))
    return both, rl(both, 64)


def strip_send(left_ref, right_ref, base, x, y):
    both = jnp.where(lane_iota(16) < 64, x, rl(y, 64))
    for p in range(2):
        left_ref[base + p] = both[8 * p : 8 * p + 8]
        right_ref[base + p] = both[8 * p : 8 * p + 8]


def strip_response(delta, diagonal, mod_j, mod_k, cf):
    x = [delta[0:8], delta[8:16]]
    gj, gk = strip_lines(x, cf, 0)
    fj = strip_lines([mod_j[8 * v : 8 * v + 8] * gj[v] for v in range(2)], cf, 15)[0]
    fk = strip_lines([mod_k[8 * v : 8 * v + 8] * gk[v] for v in range(2)], cf, 15)[1]
    return diagonal * delta + jnp.concatenate([fj[v] + fk[v] for v in range(2)], axis=0)


def strip_x(f, beside):
    zero = row_zero(16)
    b, a = f[0:16], f[48:64]
    na = a + jnp.where(zero, rl(b, 8), beside)
    nb = b + jnp.where(zero, beside, rl(a, 120))
    return jnp.concatenate([nb, f[16:48], na], axis=0)


def strip_y(f):
    low = sub_iota() < 4
    parts = []
    for i in range(4):
        x, y = f[16 * i : 16 * i + 8], f[16 * i + 8 : 16 * i + 16]
        parts.append(x + jnp.where(low, rs(rl(y, 1), 4), 0.0))
        parts.append(y + jnp.where(low, 0.0, rs(rl(x, 127), 4)))
    return jnp.concatenate(parts, axis=0)


def inverse_mass(m):
    return jnp.where(m > 0.5, PUSH / jnp.where(m > 0.5, m, 1.0), 0.0)


def strip_not_shared(x):
    zero = row_zero(16)
    return jnp.concatenate(
        [jnp.where(zero, 0.0, x[0:16]), x[16:48], jnp.where(zero, x[48:64], 0.0)], axis=0
    )


def strip_arrays(z1, z2):
    q = lane_iota(64) // 32

    def two(a, b):
        return jnp.where(q == 0, a, jnp.where(q == 1, b, 0.0))

    us = two(z1, z1)
    m0 = two(rl(z1, 64), rl(z1, 96))
    m1 = two(rl(z1, 32), rl(z1, 64))
    m2 = two(z2, rl(z2, 32))
    mass = two(rl(z2, 96), z2)
    return us, jnp.concatenate([m0, m1, m2], axis=0), mass


def state_expand(xu, xw, mk):
    return jnp.where(mk["lo"], xu, rs(xw, 4)), jnp.where(mk["lo"], rs(xu, 4), xw)


def tile(ref, p):
    return ref[8 * p : 8 * p + 8, :]


def first_kernel(
    u_hbm, w_hbm, mod_hbm, mass_hbm, z_ref, state_ref, f_ref, mass2_ref, const_ref,
    u_ref, w_ref, m_ref, mass_ref, sems,
):
    copies = [
        pltpu.make_async_copy(src, dst, sems.at[i])
        for i, (src, dst) in enumerate(
            ((u_hbm, u_ref), (w_hbm, w_ref), (mod_hbm, m_ref), (mass_hbm, mass_ref))
        )
    ]
    for c in copies:
        c.start()
    for c in copies:
        c.wait()
    mk = masks()
    lane = lane_iota(64)
    pieces = (
        (w_ref, 0, 0, 0),
        (u_ref, 0, 0, 1),
        (m_ref, 0, 0, 2),
        (m_ref, 256, 0, 3),
        (m_ref, 512, 1, 0),
        (mass_ref, 0, 1, 1),
    )
    z = [jnp.zeros((64, 128), jnp.float32), jnp.zeros((64, 128), jnp.float32)]
    for ref, base, half, slot in pieces:
        for side in range(2):
            for r in range(2):
                rows = ref[pl.ds(base + 2 * (1 - side) + r, 64, stride=4), :]
                dest = slot * 32 + (1 - side) * 16 + (1 - r) * 8 + (3 if side else 1)
                src = 0 if side else 124
                moved = rl(rows, (dest - src) % 128)
                z[half] = jnp.where((lane >= dest) & (lane < dest + 4), moved, z[half])
    z_ref[0] = z[0]
    z_ref[1] = z[1]
    for p in range(32):
        a, b = state_expand(tile(u_ref, p), tile(w_ref, p), mk)
        state_ref[2 * p] = a
        state_ref[2 * p + 1] = b
        mass2_ref[2 * p] = expanded(tile(mass_ref, p), 0, mk)
        mass2_ref[2 * p + 1] = expanded(tile(mass_ref, p), 1, mk)

    def moduli(direction):
        def get(n):
            at = 64 * direction + n
            return expanded(tile(m_ref, at // 2), at % 2, mk)

        return get

    for q in range(16):
        mi = [moduli(0)(16 * i + q) for i in range(4)]
        diagonal = [sum(float(DERIVATIVE[i, e] ** 2) * mi[i] for i in range(4)) for e in (0, 3)]
        diagonal = jnp.where(mk["even"], diagonal[0], diagonal[1])
        own_mass = face_tile(lambda n: mass2_ref[n], q, mk)
        const_ref[q] = jnp.where(mk["lo"], own_mass, diagonal)
        const_ref[16 + q] = jnp.where(
            mk["lo"], face_tile(moduli(1), q, mk), face_tile(moduli(2), q, mk)
        )
    forces(lambda n: state_ref[n], into(f_ref), lambda p: tile(m_ref, p), mk)


def open_kernel(
    sub_ref, z_ref, u0_ref, f0_ref, mass2_ref, const_ref, mod_ref, cf_ref,
    left_ref, right_ref, u1_ref, v1_ref, inv_ref, strip_ref, smod_ref,
    f, sx,
):
    mk = masks()
    sub = sub_ref[0]
    lane = lane_iota(64)
    side0 = ((lane // 16) % 2) == 1
    c = lane % 8
    below, above = jnp.maximum(sub - 1, 0), jnp.minimum(sub + 1, 3)
    zs = []
    for half in range(2):
        own = z_ref[sub, half]
        zl = jnp.where(sub > 0, z_ref[below, half], 0.0)
        zr = jnp.where(sub < 3, z_ref[above, half], 0.0)
        low = jnp.where(c == 0, 0.0, jnp.where(c <= 4, zl, rl(own, 18)))
        high = jnp.where(c <= 2, rl(own, 110), jnp.where(c == 7, 0.0, zr))
        zs.append(jnp.where(side0, low, high))
    us, mods, smass = strip_arrays(zs[0], zs[1])
    fs = strip_forces(us, mods, cf_ref)
    smod_ref[...] = mods
    strip_ref[0] = us
    strip_ref[1] = fs
    strip_ref[2] = smass
    zero = row_zero(16)
    diagonal = [
        sum(float(DERIVATIVE[i, e] ** 2) * mods[16 * i : 16 * i + 16] for i in range(4))
        for e in (0, 3)
    ]
    strip_send(
        left_ref, right_ref, STRIP + 2, strip_faces(smass), jnp.where(zero, *diagonal)
    )
    strip_send(
        left_ref, right_ref, STRIP + 4, strip_faces(mods[64:128]), strip_faces(mods[128:192])
    )
    sm = strip_x(smass, 0.0)
    sx[0] = sm
    fx = strip_x(fs, 0.0)
    sx[1] = fx
    sinv = strip_not_shared(inverse_mass(strip_y(sm)))
    partial = strip_forces(us - sinv * strip_y(fx), mods, cf_ref)
    strip_send(left_ref, right_ref, STRIP, strip_faces(fs), strip_faces(partial))

    def put_mass(n, total):
        inv_ref[n] = not_shared(n, inverse_mass(total), mk)

    assemble(lambda n: mass2_ref[n], None, sx.at[0], mk, put_mass)

    def put(n, total):
        vel = -inv_ref[n] * total
        v1_ref[n] = vel
        u1_ref[n] = u0_ref[n] + vel

    assemble(lambda n: f0_ref[n], None, sx.at[1], mk, put)
    forces(lambda n: u1_ref[n], into(f), lambda p: mod_ref[p], mk, planes=(0, 3))
    pack_faces(left_ref, right_ref, 0, lambda q: face_tile(lambda n: f0_ref[n], q, mk), mk)
    pack_faces(left_ref, right_ref, 8, lambda q: face_tile(lambda n: f[n], q, mk), mk)
    pack_faces(left_ref, right_ref, CONST, lambda q: const_ref[q], mk)
    pack_faces(left_ref, right_ref, CONST + 8, lambda q: const_ref[16 + q], mk)


def middle_kernel(
    mr_ref, ml_ref, u0_ref, f0_ref, mass2_ref, u1p_ref, v1p_ref, invp_ref, strip_ref, smod_ref,
    mod_ref, cf_ref,
    bl_ref, br_ref, inv_ref, u1_ref, u2_ref, v2_ref, f2_ref, u3_ref, v3_ref, resp_ref,
    sresp_ref, sstate_ref,
    v1, f, sx, beside,
):
    mk = masks()
    lo = mk["lo"]
    us, fs, smass = strip_ref[0], strip_ref[1], strip_ref[2]
    mods = smod_ref[...]
    sf0, sp1 = strip_beside(mr_ref, ml_ref, STRIP)
    smn, sresp0 = strip_beside(mr_ref, ml_ref, STRIP + 2)
    sresp1, sresp2 = strip_beside(mr_ref, ml_ref, STRIP + 4)
    sresp_ref[0] = sresp0
    sresp_ref[1] = sresp1
    sresp_ref[2] = sresp2
    for q in range(16):
        x = unpack_face(mr_ref, ml_ref, CONST, q, mk)
        r = rs(x, 4)
        beside[q] = jnp.where(lo, x, r)
        resp_ref[0, q] = jnp.where(lo, r, x)
        x = unpack_face(mr_ref, ml_ref, CONST + 8, q, mk)
        r = rs(x, 4)
        resp_ref[1, q] = jnp.where(lo, x, r)
        resp_ref[2, q] = jnp.where(lo, r, x)
    responses = [lambda q, d=d: resp_ref[d, q] for d in range(3)]
    sm = strip_x(smass, smn)
    sx[0] = sm
    sinv = inverse_mass(strip_y(sm))
    for n in range(16, 48):
        inv_ref[n] = invp_ref[n]
        u1_ref[n] = u1p_ref[n]
        v1[n] = v1p_ref[n]

    def put_mass(n, total):
        inv_ref[n] = inverse_mass(total)

    assemble(lambda n: mass2_ref[n], lambda q: beside[q], sx.at[0], mk, put_mass, (0, 3))
    fs = strip_x(fs, sf0)
    sx[1] = fs
    svel = -sinv * strip_y(fs)
    us = us + svel

    def put0(n, total):
        vel = -inv_ref[n] * total
        v1[n] = vel
        u1_ref[n] = u0_ref[n] + vel

    assemble(
        lambda n: f0_ref[n], lambda q: unpack_face(mr_ref, ml_ref, 0, q, mk), sx.at[1], mk, put0,
        (0, 3),
    )
    forces(lambda n: u1_ref[n], into(f), lambda p: mod_ref[p], mk)
    delta = [face_tile(lambda n: v1[n], q, mk) for q in range(16)]
    for q, x in enumerate(face_response(delta, *responses)):
        beside[q] = unpack_face(mr_ref, ml_ref, 8, q, mk) + x
    sbeside = sp1 + strip_response(strip_faces(svel), sresp0, sresp1, sresp2, cf_ref)
    fs = strip_x(strip_forces(us, mods, cf_ref), sbeside)
    sx[2] = fs
    svel = svel - sinv * strip_y(fs)
    us = us + svel

    def put1(n, total):
        vel = v1[n] - inv_ref[n] * total
        v2_ref[n] = vel
        u2_ref[n] = u1_ref[n] + vel

    assemble(lambda n: f[n], lambda q: beside[q], sx.at[2], mk, put1)
    forces(lambda n: u2_ref[n], into(f2_ref), lambda p: mod_ref[p], mk)
    fs = strip_forces(us, mods, cf_ref)
    sstate_ref[0] = us
    sstate_ref[1] = svel
    sstate_ref[2] = fs
    sstate_ref[3] = sinv
    fx = strip_x(fs, 0.0)
    sx[3] = fx
    partial = strip_forces(
        us + (svel - strip_not_shared(sinv) * strip_y(fx)), mods, cf_ref
    )

    def put2(n, total):
        vel = v2_ref[n] - not_shared(n, inv_ref[n], mk) * total
        v3_ref[n] = vel
        u3_ref[n] = u2_ref[n] + vel

    assemble(lambda n: f2_ref[n], None, sx.at[3], mk, put2)
    forces(lambda n: u3_ref[n], into(f), lambda p: mod_ref[p], mk, planes=(0, 3))
    pack_faces(bl_ref, br_ref, 0, lambda q: face_tile(lambda n: f2_ref[n], q, mk), mk)
    pack_faces(bl_ref, br_ref, 8, lambda q: face_tile(lambda n: f[n], q, mk), mk)
    strip_send(bl_ref, br_ref, STRIP_B, strip_faces(fs), strip_faces(partial))


def density_kernel(mod_ref, u0_ref, u1_ref, u2_ref, owner_ref, d2_ref, x0_ref, x1_ref, hot_ref):
    mk = masks()
    lo = mk["lo"]
    for direction in (2, 1, 0):
        for a in range(4):
            for b in range(4):
                nodes = line_nodes(direction, a, b)
                g0 = d_line(*[u0_ref[n] for n in nodes])
                g1 = d_line(*[u1_ref[n] for n in nodes])
                g2 = d_line(*[u2_ref[n] for n in nodes])
                for e, n in enumerate(nodes):
                    at = 64 * direction + n
                    m = expanded(mod_ref[at // 2], at % 2, mk)
                    x0_ref[at] = jnp.where(lo, m * rs(g0[e], 4), 0.0)
                    x1_ref[at] = m * rs(g1[e], 4)
                    t = jnp.where(lo, m * g2[e] * rs(g2[e], 4), 0.0)
                    d2_ref[n] = t if direction == 2 else d2_ref[n] + t
    block = lax.broadcasted_iota(jnp.int32, (512, 128), 0)
    for s in range(4):
        owner = jnp.broadcast_to(owner_ref[s : s + 1, :], (512, 128))
        hot_ref[:, 128 * s : 128 * s + 128] = (
            (block == owner).astype(jnp.float32).astype(jnp.bfloat16)
        )


def three_way(x):
    hi = x.astype(jnp.bfloat16)
    rest = x - hi.astype(jnp.float32)
    mid = rest.astype(jnp.bfloat16)
    return hi, mid, (rest - mid.astype(jnp.float32)).astype(jnp.bfloat16)


def last_kernel(
    br_ref, bl_ref, mod_ref, inv_ref, u2_ref, v2_ref, f2_ref, u3p_ref, v3p_ref, resp_ref,
    sresp_ref, sstate_ref, smod_ref, d2_ref, x0_ref, x1_ref, hot_ref, cf_ref,
    out_u_ref, out_w_ref, sums_ref,
    u, v, f, sx, beside, dens,
):
    mk = masks()
    lo = mk["lo"]
    mods = smod_ref[...]
    us, svel, fs, sinv = sstate_ref[0], sstate_ref[1], sstate_ref[2], sstate_ref[3]
    sf2, sp3 = strip_beside(br_ref, bl_ref, STRIP_B)
    fs = strip_x(fs, sf2)
    sx[0] = fs
    spush = -sinv * strip_y(fs)
    us = us + (svel + spush)
    for n in range(16, 48):
        u[n] = u3p_ref[n]
        v[n] = v3p_ref[n]

    def put2(n, total):
        vel = v2_ref[n] - inv_ref[n] * total
        v[n] = vel
        u[n] = u2_ref[n] + vel

    assemble(
        lambda n: f2_ref[n], lambda q: unpack_face(br_ref, bl_ref, 0, q, mk), sx.at[0], mk, put2,
        (0, 3),
    )

    def add_third(direction, n, g):
        at = pl.ds(8 * n, 8)
        before = d2_ref[n] if direction == 2 else dens[at, :]
        dens[at, :] = before + x1_ref[64 * direction + n] * g

    forces(lambda n: u[n], into(f), lambda p: mod_ref[p], mk, hook=add_third)
    delta = [face_tile(lambda n: v[n] - v2_ref[n], q, mk) for q in range(16)]
    for q, x in enumerate(face_response(delta, *[lambda q, d=d: resp_ref[d, q] for d in range(3)])):
        beside[q] = unpack_face(br_ref, bl_ref, 8, q, mk) + x
    sbeside = sp3 + strip_response(
        strip_faces(spush), sresp_ref[0], sresp_ref[1], sresp_ref[2], cf_ref
    )
    sx[1] = strip_x(strip_forces(us, mods, cf_ref), sbeside)

    def put3(n, total):
        u[n] = u[n] + (v[n] - inv_ref[n] * total)

    assemble(lambda n: f[n], lambda q: beside[q], sx.at[1], mk, put3)
    for direction in (2, 1, 0):
        for a in range(4):
            for b in range(4):
                nodes = line_nodes(direction, a, b)
                for n, g in zip(nodes, d_line(*[u[n] for n in nodes])):
                    at = pl.ds(8 * n, 8)
                    dens[at, :] = dens[at, :] + x0_ref[64 * direction + n] * g
    cols = [
        dens[pl.ds(s, 64, stride=8), :] + dens[pl.ds(s + 4, 64, stride=8), :] for s in range(4)
    ]
    split = jnp.concatenate(three_way(jnp.concatenate(cols, axis=1)), axis=0)
    res = lax.dot_general(
        split, hot_ref[...], (((1,), (1,)), ((), ())), preferred_element_type=jnp.float32
    )
    sums = res[0:64] + (res[64:128] + res[128:192])
    for q in range(4):
        sums_ref[q] = sums[:, 128 * q : 128 * q + 128]
    for p in range(32):
        a, b = u[2 * p], u[2 * p + 1]
        out_u_ref[p] = jnp.where(lo, a, rs(b, 4))
        out_w_ref[p] = jnp.where(lo, rs(a, 4), b)


def project_kernel(x_ref, basis_ref, out_ref):
    total = (x_ref[0] + x_ref[1]) + (x_ref[2] + x_ref[3])
    t0, t1, t2 = three_way(total)
    b0, b1, b2 = three_way(basis_ref[...])
    out_ref[...] = KERNEL_SCALE * jnp.dot(
        jnp.concatenate([b0, b1, b0, b1, b0, b2], axis=1),
        jnp.concatenate([t0, t0, t1, t1, t2, t0], axis=0),
        preferred_element_type=jnp.float32,
    )


VMEM = pl.BlockSpec(memory_space=pltpu.VMEM)
SMEM = pl.BlockSpec(memory_space=pltpu.SMEM)
HBM = pl.BlockSpec(memory_space=pltpu.HBM)
F32, BF16 = jnp.float32, jnp.bfloat16


def call(kernel, outs, ins, scratch=(), specs=(), limit=24):
    specs = list(specs) + [VMEM] * (len(ins) - len(specs))
    outs = [o if isinstance(o, jax.ShapeDtypeStruct) else jax.ShapeDtypeStruct(o, F32) for o in outs]
    return pl.pallas_call(
        kernel,
        out_shape=outs,
        in_specs=specs,
        out_specs=[VMEM] * len(outs),
        scratch_shapes=list(scratch),
        compiler_params=pltpu.CompilerParams(vmem_limit_bytes=limit * 1024 * 1024),
    )(*ins)


def raw_tiles(x):
    lead = int(np.prod(x.shape[:-2]))
    return x.reshape(lead, 2, 2, 128).transpose(0, 2, 1, 3).reshape(lead * 4, 128)


def from_tiles(x):
    return x.reshape(64, 2, 2, 128).transpose(0, 2, 1, 3).reshape(64, 2, 256)


def on_device(initial_field, adjoint_source, moduli, node_mass, block_owner, spline_basis):
    count = lax.axis_size("dom")
    to_right = [(i, i + 1) for i in range(count - 1)]
    to_left = [(b, a) for a, b in to_right]
    cf = jnp.asarray(COEFFICIENTS)
    sub = lax.axis_index("sub").astype(jnp.int32).reshape(1)
    u2d, w2d, m2d, mass2d = map(raw_tiles, (initial_field, adjoint_source, moduli, node_mass))
    owner = raw_tiles(block_owner[None])
    mod = m2d.reshape(96, 8, 128)
    full, face, strip = (64, 8, 128), (16, 8, 128), (64, 128)

    def swap_rows(left, right):
        return lax.ppermute(left, "dom", to_left), lax.ppermute(right, "dom", to_right)

    edges, u0, f0, mass2, const = call(
        first_kernel,
        [(2, 64, 128), full, full, full, (32, 8, 128)],
        [u2d, w2d, m2d, mass2d],
        [pltpu.VMEM((n, 128), F32) for n in (256, 256, 768, 256)] + [pltpu.SemaphoreType.DMA((4,))],
        [HBM] * 4,
        limit=FIRST_LIMIT,
    )
    edges = lax.all_gather(edges, "sub")
    left, right, u1p, v1p, invp, strips, smod = call(
        open_kernel,
        [(MSG, 8, 128), (MSG, 8, 128), full, full, full, (3, 64, 128), (192, 128)],
        [sub, edges, u0, f0, mass2, const, mod, cf],
        [pltpu.VMEM(full, F32), pltpu.VMEM((2, 64, 128), F32)],
        specs=[SMEM],
    )
    from_right, from_left = swap_rows(left, right)
    left, right, inv, u1, u2, v2, f2, u3p, v3p, resp, sresp, sstate = call(
        middle_kernel,
        [
            (MSG_B, 8, 128), (MSG_B, 8, 128), full, full, full, full, full, full, full,
            (3, 16, 8, 128), (3, 16, 128), (4, 64, 128),
        ],
        [from_right, from_left, u0, f0, mass2, u1p, v1p, invp, strips, smod, mod, cf],
        [pltpu.VMEM(full, F32)] * 2 + [pltpu.VMEM((4, 64, 128), F32), pltpu.VMEM(face, F32)],
    )
    from_right, from_left = swap_rows(left, right)
    d2, x0, x1, hot = call(
        density_kernel,
        [full, (192, 8, 128), (192, 8, 128), jax.ShapeDtypeStruct((512, 512), BF16)],
        [mod, u0, u1, u2, owner],
    )
    out_u, out_w, sums = call(
        last_kernel,
        [(32, 8, 128), (32, 8, 128), (4, 64, 128)],
        [
            from_right, from_left, mod, inv, u2, v2, f2, u3p, v3p, resp, sresp, sstate, smod,
            d2, x0, x1, hot, cf,
        ],
        [pltpu.VMEM(full, F32)] * 3
        + [pltpu.VMEM((2, 64, 128), F32), pltpu.VMEM(face, F32), pltpu.VMEM((512, 128), F32)],
    )
    sums = lax.all_to_all(sums, "sub", 0, 0)
    (kernel,) = call(project_kernel, [(64, 128)], [sums, spline_basis.T])
    return from_tiles(out_u), from_tiles(out_w), kernel


def solution(mesh):
    in_specs = (
        P(None, "dom", "sub"),
        P(None, "dom", "sub"),
        P(None, None, "dom", "sub"),
        P(None, "dom", "sub"),
        P("dom", "sub"),
        P(),
    )
    out_specs = (P(None, "dom", "sub"), P(None, "dom", "sub"), P(None, ("dom", "sub")))
    return jax.shard_map(
        on_device, mesh=mesh, in_specs=in_specs, out_specs=out_specs, check_vma=False
    )
```

time: 72.9 us -> 64 us (0.88)
  blocking collectives: 17.9 us -> 8.15 us
  starting transfers between devices: 30.7 us -> 26 us
  waiting for transfers between devices: 12.3 us -> 16.4 us
  local copies, waits for them, and re-layouts: 0.78 us -> 3.57 us
  Pallas kernels: 9.52 us -> 8.38 us
    all_gather x1, blocking collectives: 17.9 us -> 8.15 us  [on_device(): edges = lax.all_gather(edges, 'sub')]
    ppermute x3 -> x2, starting transfers between devices: 8.64 us -> 5.28 us  [swap_rows(): lax.ppermute(right, 'dom', to_right)]
    unnamed x15 -> x17, local copies, waits for them, and re-layouts: 0.78 us -> 3.57 us
    ppermute x3 -> x2, waiting for transfers between devices: 7.27 us -> 10 us  [swap_rows(): lax.ppermute(right, 'dom', to_right)]
    ppermute x3 -> x2, starting transfers between devices: 16.2 us -> 14.2 us  [swap_rows(): lax.ppermute(left, 'dom', to_left)]
    ppermute x3 -> x2, waiting for transfers between devices: 0.01 us -> 1.33 us  [swap_rows(): lax.ppermute(left, 'dom', to_left)]
    pallas_call x7 -> x6, Pallas kernels: 9.52 us -> 8.38 us  [call(): pl.pallas_call(kernel, out_shape=outs, in_specs=specs, out_specs=[VMEM] *...]
  transfers between devices with their start and end apart: 7 -> 5, of which waited for: 3 -> 4; matrix products, arithmetic and copies ran while one was open for 0% -> 0% of each run, Pallas kernels for 2% -> 1%
where the time goes in v3:
time: 64 us; the launch traced here: 63.2 us
  starting transfers between devices  26 us (41%)
  waiting for transfers between devices  16.4 us (26%)
  Pallas kernels  8.38 us (13%)
  blocking collectives  8.15 us (13%)
  local copies, waits for them, and re-layouts  3.57 us (6%)
  between operations  0.75 us (1%)
    ppermute x2, starting transfers between devices, swap_rows(): lax.ppermute(left, 'dom', to_left)  14.2 us
    ppermute x2, waiting for transfers between devices, swap_rows(): lax.ppermute(right, 'dom', to_right)  10 us
    pallas_call x6, Pallas kernels, call(): pl.pallas_call(kernel, out_shape=outs, in_specs=specs, out_specs=[VMEM] *...  8.38 us
    all_gather x1, blocking collectives, on_device(): edges = lax.all_gather(edges, 'sub')  8.15 us
    all_to_all x1, starting transfers between devices, on_device(): sums = lax.all_to_all(sums, 'sub', 0, 0)  6.56 us
    ppermute x2, starting transfers between devices, swap_rows(): lax.ppermute(right, 'dom', to_right)  5.28 us
    all_to_all x1, waiting for transfers between devices, on_device(): sums = lax.all_to_all(sums, 'sub', 0, 0)  5.02 us
    unnamed x17, local copies, waits for them, and re-layouts  3.57 us
  transfers between devices with their start and end apart: 5, of which 4 were waited for; matrix products, arithmetic and copies ran while one was open for 0% of the time, Pallas kernels for 1%

profile of v3, /device:TPU:25, one launch (start us, length us, event | category | flops | bytes accessed | tf_op | source)
XLA Modules:
  0.0 63.2 jit_solution(6282234963657687242)
XLA Ops:
  0.6 0.0 copy-start.2
  0.7 2.5 %shard_map.94 = (f32[2,64,128]{2,1,0:T(8,128)}, f32[64,8,128]{2,1,0:T(8,128)}, f32[64,8,128]{2,1,0:T(8,128)}, f32[64,8,128]{2,1,0:T(8,128)}, f32[32,8,128]{2,1,0:T(8,128)}) custom-call(f32[256,128]{1,0:T(8,128)} %bitcast.48, f32[256,128]{1,0:T(8,128)} %bitcast.49, f32[768,128]{1,0:T(8,128)} %bitcast.40, f32[256,128]{1,0:T(8,128)} %bitcast.50), custom_call_target="tpu_custom_call" | custom-call | tf_op jit(solution)/shard_map/pallas_call | solution.py:666
  3.2 8.1 %all-gather = f32[8,64,128]{2,1,0:T(8,128)S(1)} all-gather(f32[2,64,128]{2,1,0:T(8,128)} %get-tuple-element.34), channel_id=2, replica_groups=mesh['dom'=128,'sub'=4] {'sub'}, dimensions={0}, use_global_device_ids=true | all-gather | bytes 327680 | tf_op jit(solution)/shard_map/all_gather | solution.py:707
  11.4 0.9 %copy-done.3 = f32[64,8,128]{2,1,0:T(8,128)S(1)} copy-done((f32[64,8,128]{2,1,0:T(8,128)S(1)}, f32[64,8,128]{2,1,0:T(8,128)}, u32[]{:S(2)}) %copy-start.3) | copy-done | bytes 262168
  12.3 0.9 %copy-done.4 = f32[64,8,128]{2,1,0:T(8,128)S(1)} copy-done((f32[64,8,128]{2,1,0:T(8,128)S(1)}, f32[64,8,128]{2,1,0:T(8,128)}, u32[]{:S(2)}) %copy-start.4) | copy-done | bytes 262168
  13.3 0.9 %copy-done.5 = f32[32,8,128]{2,1,0:T(8,128)S(1)} copy-done((f32[32,8,128]{2,1,0:T(8,128)S(1)}, f32[32,8,128]{2,1,0:T(8,128)}, u32[]{:S(2)}) %copy-start.5) | copy-done | bytes 131096
  14.2 0.7 %shard_map.95 = (f32[38,8,128]{2,1,0:T(8,128)S(1)}, f32[38,8,128]{2,1,0:T(8,128)S(1)}, f32[64,8,128]{2,1,0:T(8,128)S(1)}, f32[64,8,128]{2,1,0:T(8,128)S(1)}, f32...) custom-call(s32[1]{0:T(128)} %bitcast.sub_ref, f32[4,2,64,128]{3,2,1,0:T(8,128)S(1)} %bitcast.45, ...), custom_call_target="tpu_custom_call" | custom-call | tf_op jit(solution)/shard_map/pallas_call | solution.py:666
  14.9 12.2 %collective-permute-start = (f32[38,8,128]{2,1,0:T(8,128)S(1)}, f32[38,8,128]{2,1,0:T(8,128)S(1)}, u32[]{:S(2)}, u32[]{:S(2)}) collective-permute-start(f32[38,8,128]{2,1,0:T(8,128)S(1)} %get-tuple-element.39), channel_id=1, source_target_pairs={{4,0},{8,4},{12,8},{16,12},{20,16},{24,20},{28,24},{32,28},{36,32}... | collective-permute-start | bytes 466952 | tf_op jit(solution)/shard_map/ppermute | solution.py:697
  27.1 1.9 %collective-permute-start.1 = (f32[38,8,128]{2,1,0:T(8,128)S(1)}, f32[38,8,128]{2,1,0:T(8,128)S(1)}, u32[]{:S(2)}, u32[]{:S(2)}) collective-permute-start(f32[38,8,128]{2,1,0:T(8,128)S(1)} %get-tuple-element.40), channel_id=1, source_target_pairs={{0,4},{4,8},{8,12},{12,16},{16,20},{20,24},{24,28},{28,32},{32,36}... | collective-permute-start | bytes 466952 | tf_op jit(solution)/shard_map/ppermute | solution.py:697
  29.0 1.3 %collective-permute-done.mr_ref = f32[38,8,128]{2,1,0:T(8,128)S(1)} collective-permute-done((f32[38,8,128]{2,1,0:T(8,128)S(1)}, f32[38,8,128]{2,1,0:T(8,128)S(1)}, u32[]{:S(2)}, u32[]{:S(2)}) %collective-permute-start) | collective-permute-done | bytes 155680 | tf_op jit(solution)/shard_map/ppermute | solution.py:697
  30.4 6.8 %collective-permute-done.1.ml_ref = f32[38,8,128]{2,1,0:T(8,128)S(1)} collective-permute-done((f32[38,8,128]{2,1,0:T(8,128)S(1)}, f32[38,8,128]{2,1,0:T(8,128)S(1)}, u32[]{:S(2)}, u32[]{:S(2)}) %collective-permute-start.1) | collective-permute-done | bytes 155680 | tf_op jit(solution)/shard_map/ppermute | solution.py:697
  37.2 1.6 %shard_map.96 = (f32[18,8,128]{2,1,0:T(8,128)S(1)}, f32[18,8,128]{2,1,0:T(8,128)S(1)}, f32[64,8,128]{2,1,0:T(8,128)S(1)}, f32[64,8,128]{2,1,0:T(8,128)S(1)}, f32...) custom-call(f32[38,8,128]{2,1,0:T(8,128)S(1)} %collective-permute-do, ...), custom_call_target="tpu_custom_call" | custom-call | tf_op jit(solution)/shard_map/pallas_call | solution.py:666
  38.7 1.9 %collective-permute-start.2 = (f32[18,8,128]{2,1,0:T(8,128)S(1)}, f32[18,8,128]{2,1,0:T(8,128)S(1)}, u32[]{:S(2)}, u32[]{:S(2)}) collective-permute-start(f32[18,8,128]{2,1,0:T(8,128)S(1)} %get-tuple-element.46), channel_id=1, source_target_pairs={{4,0},{8,4},{12,8},{16,12},{20,16},{24,20},{28,24},{32,28},{36,32}... | collective-permute-start | bytes 221192 | tf_op jit(solution)/shard_map/ppermute | solution.py:697
  40.7 3.4 %collective-permute-start.3 = (f32[18,8,128]{2,1,0:T(8,128)S(1)}, f32[18,8,128]{2,1,0:T(8,128)S(1)}, u32[]{:S(2)}, u32[]{:S(2)}) collective-permute-start(f32[18,8,128]{2,1,0:T(8,128)S(1)} %get-tuple-element.47), channel_id=1, source_target_pairs={{0,4},{4,8},{8,12},{12,16},{16,20},{20,24},{24,28},{28,32},{32,36}... | collective-permute-start | bytes 221192 | tf_op jit(solution)/shard_map/ppermute | solution.py:697
  44.0 0.0 copy-start.6
  44.1 0.7 %copy-done.6 = s32[2,256]{1,0:T(2,128)S(1)} copy-done((s32[2,256]{1,0:T(2,128)S(1)}, s32[2,256]{1,0:T(2,128)}, u32[]{:S(2)}) %copy-start.6) | copy-done | bytes 2072
  44.7 0.8 %shard_map.97 = (f32[64,8,128]{2,1,0:T(8,128)S(1)}, f32[192,8,128]{2,1,0:T(8,128)S(1)}, f32[192,8,128]{2,1,0:T(8,128)S(1)}, bf16[512,512]{1,0:T(8,128)(2,1)S(1)}) custom-call(f32[96,8,128]{2,1,0:T(8,128)S(1)} %bitcast.43, f32[64,8,128]{2,1,0:T(8,128)S(1)} %copy-done.1, f32[64,8,128]{2,1,0:T(8,128)S(1)} %get-tuple-element.57.u1_ref, ...), custom_call_target="tpu_custom_call" | custom-call | tf_op jit(solution)/shard_map/pallas_call | solution.py:666
  45.6 0.0 collective-permute-done.2.br_ref
  45.6 3.2 %collective-permute-done.3.bl_ref = f32[18,8,128]{2,1,0:T(8,128)S(1)} collective-permute-done((f32[18,8,128]{2,1,0:T(8,128)S(1)}, f32[18,8,128]{2,1,0:T(8,128)S(1)}, u32[]{:S(2)}, u32[]{:S(2)}) %collective-permute-start.3) | collective-permute-done | bytes 73760 | tf_op jit(solution)/shard_map/ppermute | solution.py:697
  48.8 1.9 %shard_map.98 = (f32[32,8,128]{2,1,0:T(8,128)}, f32[32,8,128]{2,1,0:T(8,128)}, f32[4,64,128]{2,1,0:T(8,128)}) custom-call(f32[18,8,128]{2,1,0:T(8,128)S(1)} %collective-permute-done.2.br_ref, f32[18,8,128]{2,1,0:T(8,128)S(1)} %collective-permute-done.3.bl_ref, f32[96,8,128]{2,1,0:T(8,128)S(1)} %bitcast.44, f32[64,8,128]{2,1,0:T(8,128)S(1)} %get-tuple-element.48.inv_ref, ...), custom_call_target="tpu_custom_call" | custom-call | tf_op jit(solution)/shard_map/pallas_call | solution.py:666
  50.7 6.6 %all-to-all-start = ((f32[4,64,128]{2,1,0:T(8,128)}), f32[4,64,128]{2,1,0:T(8,128)S(1)}, u32[]{:S(2)}, u32[]{:S(2)}) async-start(f32[4,64,128]{2,1,0:T(8,128)} %get-tuple-element.64), calls=%async_computation | async-start | bytes 262144 | tf_op jit(solution)/shard_map/all_to_all | solution.py:741
  57.3 0.1 copy.25
  57.3 5.0 %all-to-all-done.x_ref = f32[4,64,128]{2,1,0:T(8,128)S(1)} async-done(((f32[4,64,128]{2,1,0:T(8,128)}), f32[4,64,128]{2,1,0:T(8,128)S(1)}, u32[]{:S(2)}, u32[]{:S(2)}) %all-to-all-start) | async-done | bytes 131104 | tf_op jit(solution)/shard_map/all_to_all | solution.py:741
  62.4 0.8 %shard_map.99 = f32[64,128]{1,0:T(8,128)} custom-call(f32[4,64,128]{2,1,0:T(8,128)S(1)} %all-to-all-done.x_ref, f32[64,64]{1,0:T(8,128)S(1)} %bitcast.46), custom_call_target="tpu_custom_call" | custom-call | tf_op jit(solution)/shard_map/pallas_call | solution.py:666
  (10 shorter events, 0.0 us)
Async XLA Ops:
  0.6 10.7 %copy-start = (f32[3,64,2,256]{3,2,1,0:T(2,128)S(1)}, f32[3,64,2,256]{3,2,1,0:T(2,128)}, u32[]{:S(2)}) copy-start(f32[3,64,2,256]{3,2,1,0:T(2,128)} %param.9) | copy-start | bytes 1179652
  0.6 10.7 %copy-start.2 = (f32[30,8,128]{2,1,0:T(8,128)S(1)}, f32[30,8,128]{2,1,0:T(8,128)}, u32[]{:S(2)}) copy-start(f32[30,8,128]{2,1,0:T(8,128)} %constant.6.clone.cf_ref) | copy-start | bytes 368644
  3.2 8.2 %copy-start.1 = (f32[64,8,128]{2,1,0:T(8,128)S(1)}, f32[64,8,128]{2,1,0:T(8,128)}, u32[]{:S(2)}) copy-start(f32[64,8,128]{2,1,0:T(8,128)} %get-tuple-element.35.u0_ref) | copy-start | bytes 786436
  11.4 1.0 %copy-start.3 = (f32[64,8,128]{2,1,0:T(8,128)S(1)}, f32[64,8,128]{2,1,0:T(8,128)}, u32[]{:S(2)}) copy-start(f32[64,8,128]{2,1,0:T(8,128)} %get-tuple-element.36.f0_ref) | copy-start | bytes 786436
  12.3 0.9 %copy-start.4 = (f32[64,8,128]{2,1,0:T(8,128)S(1)}, f32[64,8,128]{2,1,0:T(8,128)}, u32[]{:S(2)}) copy-start(f32[64,8,128]{2,1,0:T(8,128)} %get-tuple-element.37.mass2_ref) | copy-start | bytes 786436
  13.3 0.9 %copy-start.5 = (f32[32,8,128]{2,1,0:T(8,128)S(1)}, f32[32,8,128]{2,1,0:T(8,128)}, u32[]{:S(2)}) copy-start(f32[32,8,128]{2,1,0:T(8,128)} %get-tuple-element.38.const_ref) | copy-start | bytes 393220
  14.9 15.5 %collective-permute-start = (f32[38,8,128]{2,1,0:T(8,128)S(1)}, f32[38,8,128]{2,1,0:T(8,128)S(1)}, u32[]{:S(2)}, u32[]{:S(2)}) collective-permute-start(f32[38,8,128]{2,1,0:T(8,128)S(1)} %get-tuple-element.39), channel_id=1, source_target_pairs={{4,0},{8,4},{12,8},{16,12},{20,16},{24,20},{28,24},{32,28},{36,32}... | collective-permute-start | bytes 466952 | tf_op jit(solution)/shard_map/ppermute | solution.py:697
  27.1 10.1 %collective-permute-start.1 = (f32[38,8,128]{2,1,0:T(8,128)S(1)}, f32[38,8,128]{2,1,0:T(8,128)S(1)}, u32[]{:S(2)}, u32[]{:S(2)}) collective-permute-start(f32[38,8,128]{2,1,0:T(8,128)S(1)} %get-tuple-element.40), channel_id=1, source_target_pairs={{0,4},{4,8},{8,12},{12,16},{16,20},{20,24},{24,28},{28,32},{32,36}... | collective-permute-start | bytes 466952 | tf_op jit(solution)/shard_map/ppermute | solution.py:697
  38.7 6.8 %collective-permute-start.2 = (f32[18,8,128]{2,1,0:T(8,128)S(1)}, f32[18,8,128]{2,1,0:T(8,128)S(1)}, u32[]{:S(2)}, u32[]{:S(2)}) collective-permute-start(f32[18,8,128]{2,1,0:T(8,128)S(1)} %get-tuple-element.46), channel_id=1, source_target_pairs={{4,0},{8,4},{12,8},{16,12},{20,16},{24,20},{28,24},{32,28},{36,32}... | collective-permute-start | bytes 221192 | tf_op jit(solution)/shard_map/ppermute | solution.py:697
  40.7 8.1 %collective-permute-start.3 = (f32[18,8,128]{2,1,0:T(8,128)S(1)}, f32[18,8,128]{2,1,0:T(8,128)S(1)}, u32[]{:S(2)}, u32[]{:S(2)}) collective-permute-start(f32[18,8,128]{2,1,0:T(8,128)S(1)} %get-tuple-element.47), channel_id=1, source_target_pairs={{0,4},{4,8},{8,12},{12,16},{16,20},{20,24},{24,28},{28,32},{32,36}... | collective-permute-start | bytes 221192 | tf_op jit(solution)/shard_map/ppermute | solution.py:697
  44.0 0.7 %copy-start.6 = (s32[2,256]{1,0:T(2,128)S(1)}, s32[2,256]{1,0:T(2,128)}, u32[]{:S(2)}) copy-start(s32[2,256]{1,0:T(2,128)} %param.11) | copy-start | bytes 6148
  50.7 6.6 %copy-start.7 = (f32[64,64]{1,0:T(8,128)S(1)}, f32[64,64]{1,0:T(8,128)}, u32[]{:S(2)}) copy-start(f32[64,64]{1,0:T(8,128)} %param.12) | copy-start | bytes 49156
  50.7 11.7 %all-to-all-start = ((f32[4,64,128]{2,1,0:T(8,128)}), f32[4,64,128]{2,1,0:T(8,128)S(1)}, u32[]{:S(2)}, u32[]{:S(2)}) async-start(f32[4,64,128]{2,1,0:T(8,128)} %get-tuple-element.64), calls=%async_computation | async-start | bytes 262144 | tf_op jit(solution)/shard_map/all_to_all | solution.py:741

commit v4 on v3

--- a/solution.py
+++ b/solution.py
@@ -25,7 +25,9 @@
 
 MSG, CONST, STRIP = 38, 16, 32
 MSG_B, STRIP_B = 18, 16
-FIRST_LIMIT = 62
+FIRST_LIMIT = 54
+U0, OWNER, WEIGHTS, BASE = 0, 64, 65, 95
+F0, MASS, FACES, HEAD = 0, 64, 128, 160
 
 
 def strip_coefficients():
@@ -326,13 +328,18 @@
 
 
 def first_kernel(
-    u_hbm, w_hbm, mod_hbm, mass_hbm, z_ref, state_ref, f_ref, mass2_ref, const_ref,
-    u_ref, w_ref, m_ref, mass_ref, sems,
+    u_hbm, w_hbm, mod_hbm, mass_hbm, owner_hbm, cf_hbm, z_ref, base_ref, head_ref,
+    u_ref, w_ref, m_ref, mass_ref, owner_ref, cf_ref, sems,
 ):
+    state_ref, f_ref = base_ref.at[U0:OWNER], head_ref.at[F0:MASS]
+    mass2_ref, const_ref = head_ref.at[MASS:FACES], head_ref.at[FACES:HEAD]
     copies = [
         pltpu.make_async_copy(src, dst, sems.at[i])
         for i, (src, dst) in enumerate(
-            ((u_hbm, u_ref), (w_hbm, w_ref), (mod_hbm, m_ref), (mass_hbm, mass_ref))
+            (
+                (u_hbm, u_ref), (w_hbm, w_ref), (mod_hbm, m_ref), (mass_hbm, mass_ref),
+                (owner_hbm, owner_ref), (cf_hbm, cf_ref),
+            )
         )
     ]
     for c in copies:
@@ -384,13 +391,20 @@
             mk["lo"], face_tile(moduli(1), q, mk), face_tile(moduli(2), q, mk)
         )
     forces(lambda n: state_ref[n], into(f_ref), lambda p: tile(m_ref, p), mk)
+    owner = owner_ref[...].astype(jnp.float32)
+    base_ref[OWNER] = jnp.concatenate([owner, owner], axis=0)
+    for t in range(WEIGHTS, BASE):
+        base_ref[t] = cf_ref[t - WEIGHTS]
 
 
 def open_kernel(
-    sub_ref, z_ref, u0_ref, f0_ref, mass2_ref, const_ref, mod_ref, cf_ref,
+    sub_ref, z_ref, base_ref, head_ref, mod_ref,
     left_ref, right_ref, u1_ref, v1_ref, inv_ref, strip_ref, smod_ref,
     f, sx,
 ):
+    u0_ref, f0_ref = base_ref.at[U0:OWNER], head_ref.at[F0:MASS]
+    mass2_ref, const_ref = head_ref.at[MASS:FACES], head_ref.at[FACES:HEAD]
+    cf_ref = base_ref.at[WEIGHTS:BASE]
     mk = masks()
     sub = sub_ref[0]
     lane = lane_iota(64)
@@ -449,12 +463,14 @@
 
 
 def middle_kernel(
-    mr_ref, ml_ref, u0_ref, f0_ref, mass2_ref, u1p_ref, v1p_ref, invp_ref, strip_ref, smod_ref,
-    mod_ref, cf_ref,
+    mr_ref, ml_ref, base_ref, head_ref, u1p_ref, v1p_ref, invp_ref, strip_ref, smod_ref,
+    mod_ref,
     bl_ref, br_ref, inv_ref, u1_ref, u2_ref, v2_ref, f2_ref, u3_ref, v3_ref, resp_ref,
     sresp_ref, sstate_ref,
     v1, f, sx, beside,
 ):
+    u0_ref, f0_ref = base_ref.at[U0:OWNER], head_ref.at[F0:MASS]
+    mass2_ref, cf_ref = head_ref.at[MASS:FACES], base_ref.at[WEIGHTS:BASE]
     mk = masks()
     lo = mk["lo"]
     us, fs, smass = strip_ref[0], strip_ref[1], strip_ref[2]
@@ -541,14 +557,23 @@
     strip_send(bl_ref, br_ref, STRIP_B, strip_faces(fs), strip_faces(partial))
 
 
-def density_kernel(mod_ref, u0_ref, u1_ref, u2_ref, owner_ref, d2_ref, x0_ref, x1_ref, hot_ref):
+def three_way(x):
+    hi = x.astype(jnp.bfloat16)
+    rest = x - hi.astype(jnp.float32)
+    mid = rest.astype(jnp.bfloat16)
+    return hi, mid, (rest - mid.astype(jnp.float32)).astype(jnp.bfloat16)
+
+
+def density_kernel(
+    mod_ref, base_ref, u1_ref, u2_ref, basis_ref, d2_ref, x0_ref, x1_ref, hot_ref, stack_ref
+):
     mk = masks()
     lo = mk["lo"]
     for direction in (2, 1, 0):
         for a in range(4):
             for b in range(4):
                 nodes = line_nodes(direction, a, b)
-                g0 = d_line(*[u0_ref[n] for n in nodes])
+                g0 = d_line(*[base_ref[U0 + n] for n in nodes])
                 g1 = d_line(*[u1_ref[n] for n in nodes])
                 g2 = d_line(*[u2_ref[n] for n in nodes])
                 for e, n in enumerate(nodes):
@@ -558,27 +583,23 @@
                     x1_ref[at] = m * rs(g1[e], 4)
                     t = jnp.where(lo, m * g2[e] * rs(g2[e], 4), 0.0)
                     d2_ref[n] = t if direction == 2 else d2_ref[n] + t
-    block = lax.broadcasted_iota(jnp.int32, (512, 128), 0)
+    block = lax.broadcasted_iota(jnp.int32, (512, 128), 0).astype(jnp.float32)
     for s in range(4):
-        owner = jnp.broadcast_to(owner_ref[s : s + 1, :], (512, 128))
+        owner = jnp.broadcast_to(base_ref[OWNER][s : s + 1, :], (512, 128))
         hot_ref[:, 128 * s : 128 * s + 128] = (
             (block == owner).astype(jnp.float32).astype(jnp.bfloat16)
         )
-
-
-def three_way(x):
-    hi = x.astype(jnp.bfloat16)
-    rest = x - hi.astype(jnp.float32)
-    mid = rest.astype(jnp.bfloat16)
-    return hi, mid, (rest - mid.astype(jnp.float32)).astype(jnp.bfloat16)
+    b0, b1, b2 = three_way(basis_ref[...])
+    stack_ref[...] = jnp.concatenate([b0, b1, b0, b1, b0, b2], axis=1)
 
 
 def last_kernel(
     br_ref, bl_ref, mod_ref, inv_ref, u2_ref, v2_ref, f2_ref, u3p_ref, v3p_ref, resp_ref,
-    sresp_ref, sstate_ref, smod_ref, d2_ref, x0_ref, x1_ref, hot_ref, cf_ref,
+    sresp_ref, sstate_ref, smod_ref, d2_ref, x0_ref, x1_ref, hot_ref, base_ref,
     out_u_ref, out_w_ref, sums_ref,
     u, v, f, sx, beside, dens,
 ):
+    cf_ref = base_ref.at[WEIGHTS:BASE]
     mk = masks()
     lo = mk["lo"]
     mods = smod_ref[...]
@@ -643,13 +664,12 @@
         out_w_ref[p] = jnp.where(lo, rs(a, 4), b)
 
 
-def project_kernel(x_ref, basis_ref, out_ref):
-    total = (x_ref[0] + x_ref[1]) + (x_ref[2] + x_ref[3])
+def project_kernel(sub_ref, x_ref, stack_ref, out_ref):
+    sub = sub_ref[0]
+    total = (x_ref[0, sub] + x_ref[1, sub]) + (x_ref[2, sub] + x_ref[3, sub])
     t0, t1, t2 = three_way(total)
-    b0, b1, b2 = three_way(basis_ref[...])
     out_ref[...] = KERNEL_SCALE * jnp.dot(
-        jnp.concatenate([b0, b1, b0, b1, b0, b2], axis=1),
-        jnp.concatenate([t0, t0, t1, t1, t2, t0], axis=0),
+        stack_ref[...], jnp.concatenate([t0, t0, t1, t1, t2, t0], axis=0),
         preferred_element_type=jnp.float32,
     )
 
@@ -660,9 +680,11 @@
 F32, BF16 = jnp.float32, jnp.bfloat16
 
 
-def call(kernel, outs, ins, scratch=(), specs=(), limit=24):
+def call(kernel, outs, ins, scratch=(), specs=(), limit=24, space=None):
     specs = list(specs) + [VMEM] * (len(ins) - len(specs))
     outs = [o if isinstance(o, jax.ShapeDtypeStruct) else jax.ShapeDtypeStruct(o, F32) for o in outs]
+    if space is not None:
+        outs = [space(o.shape, o.dtype) for o in outs]
     return pl.pallas_call(
         kernel,
         out_shape=outs,
@@ -691,26 +713,30 @@
     u2d, w2d, m2d, mass2d = map(raw_tiles, (initial_field, adjoint_source, moduli, node_mass))
     owner = raw_tiles(block_owner[None])
     mod = m2d.reshape(96, 8, 128)
-    full, face, strip = (64, 8, 128), (16, 8, 128), (64, 128)
+    full, face = (64, 8, 128), (16, 8, 128)
 
     def swap_rows(left, right):
         return lax.ppermute(left, "dom", to_left), lax.ppermute(right, "dom", to_right)
 
-    edges, u0, f0, mass2, const = call(
+    edges, base, head = call(
         first_kernel,
-        [(2, 64, 128), full, full, full, (32, 8, 128)],
-        [u2d, w2d, m2d, mass2d],
-        [pltpu.VMEM((n, 128), F32) for n in (256, 256, 768, 256)] + [pltpu.SemaphoreType.DMA((4,))],
-        [HBM] * 4,
+        [(2, 64, 128), (BASE, 8, 128), (HEAD, 8, 128)],
+        [u2d, w2d, m2d, mass2d, owner, cf],
+        [pltpu.VMEM((n, 128), F32) for n in (256, 256, 768, 256)]
+        + [pltpu.VMEM((4, 128), jnp.int32), pltpu.VMEM((BASE - WEIGHTS, 8, 128), F32)]
+        + [pltpu.SemaphoreType.DMA((6,))],
+        [HBM] * 6,
         limit=FIRST_LIMIT,
+        space=pltpu.VMEM,
     )
     edges = lax.all_gather(edges, "sub")
     left, right, u1p, v1p, invp, strips, smod = call(
         open_kernel,
         [(MSG, 8, 128), (MSG, 8, 128), full, full, full, (3, 64, 128), (192, 128)],
-        [sub, edges, u0, f0, mass2, const, mod, cf],
+        [sub, edges, base, head, mod],
         [pltpu.VMEM(full, F32), pltpu.VMEM((2, 64, 128), F32)],
         specs=[SMEM],
+        space=pltpu.VMEM,
     )
     from_right, from_left = swap_rows(left, right)
     left, right, inv, u1, u2, v2, f2, u3p, v3p, resp, sresp, sstate = call(
@@ -719,27 +745,30 @@
             (MSG_B, 8, 128), (MSG_B, 8, 128), full, full, full, full, full, full, full,
             (3, 16, 8, 128), (3, 16, 128), (4, 64, 128),
         ],
-        [from_right, from_left, u0, f0, mass2, u1p, v1p, invp, strips, smod, mod, cf],
+        [from_right, from_left, base, head, u1p, v1p, invp, strips, smod, mod],
         [pltpu.VMEM(full, F32)] * 2 + [pltpu.VMEM((4, 64, 128), F32), pltpu.VMEM(face, F32)],
+        space=pltpu.VMEM,
     )
     from_right, from_left = swap_rows(left, right)
-    d2, x0, x1, hot = call(
+    wide = jax.ShapeDtypeStruct((512, 512), BF16)
+    d2, x0, x1, hot, stack = call(
         density_kernel,
-        [full, (192, 8, 128), (192, 8, 128), jax.ShapeDtypeStruct((512, 512), BF16)],
-        [mod, u0, u1, u2, owner],
+        [full, (192, 8, 128), (192, 8, 128), wide, jax.ShapeDtypeStruct((64, 384), BF16)],
+        [mod, base, u1, u2, spline_basis.T],
+        space=pltpu.VMEM,
     )
     out_u, out_w, sums = call(
         last_kernel,
         [(32, 8, 128), (32, 8, 128), (4, 64, 128)],
         [
             from_right, from_left, mod, inv, u2, v2, f2, u3p, v3p, resp, sresp, sstate, smod,
-            d2, x0, x1, hot, cf,
+            d2, x0, x1, hot, base,
         ],
         [pltpu.VMEM(full, F32)] * 3
         + [pltpu.VMEM((2, 64, 128), F32), pltpu.VMEM(face, F32), pltpu.VMEM((512, 128), F32)],
     )
-    sums = lax.all_to_all(sums, "sub", 0, 0)
-    (kernel,) = call(project_kernel, [(64, 128)], [sums, spline_basis.T])
+    sums = lax.all_gather(sums, "sub")
+    (kernel,) = call(project_kernel, [(64, 128)], [sub, sums, stack], specs=[SMEM])
     return from_tiles(out_u), from_tiles(out_w), kernel
 
 

time: 64 us -> 58.4 us (0.912)
  blocking collectives: 8.15 us -> 18.5 us
  starting transfers between devices: 26 us -> 19.4 us
  waiting for transfers between devices: 16.4 us -> 12 us
  local copies, waits for them, and re-layouts: 3.57 us -> 0.08 us
  Pallas kernels: 8.38 us -> 7.47 us
    all_gather x0 -> x1, blocking collectives: none -> 10.7 us  [on_device(): sums = lax.all_gather(sums, 'sub')]
    all_to_all x1 -> x0, starting transfers between devices: 6.56 us -> none  [on_device(): sums = lax.all_to_all(sums, 'sub', 0, 0)]
    all_to_all x1 -> x0, waiting for transfers between devices: 5.02 us -> none  [on_device(): sums = lax.all_to_all(sums, 'sub', 0, 0)]
    unnamed x17 -> x5, local copies, waits for them, and re-layouts: 3.57 us -> 0.08 us
    pallas_call x6, Pallas kernels: 8.38 us -> 7.47 us  [call(): pl.pallas_call(kernel, out_shape=outs, in_specs=specs, out_specs=[VMEM] *...]
  transfers between devices with their start and end apart: 5 -> 4, of which waited for: 4 -> 3; matrix products, arithmetic and copies ran while one was open for 0% -> 0% of each run, Pallas kernels for 1% -> 1%
where the time goes in v4:
time: 58.4 us; the launch traced here: 58.1 us
  starting transfers between devices  19.4 us (33%)
  blocking collectives  18.5 us (32%)
  waiting for transfers between devices  12 us (21%)
  Pallas kernels  7.47 us (13%)
  between operations  0.72 us (1%)
    ppermute x2, starting transfers between devices, swap_rows(): lax.ppermute(left, 'dom', to_left)  14.2 us
    all_gather x1, blocking collectives, on_device(): sums = lax.all_gather(sums, 'sub')  10.7 us
    ppermute x2, waiting for transfers between devices, swap_rows(): lax.ppermute(right, 'dom', to_right)  10.6 us
    all_gather x1, blocking collectives, on_device(): edges = lax.all_gather(edges, 'sub')  7.8 us
    pallas_call x6, Pallas kernels, call(): pl.pallas_call(kernel, out_shape=outs, in_specs=specs, out_specs=[VMEM] *...  7.47 us
    ppermute x2, starting transfers between devices, swap_rows(): lax.ppermute(right, 'dom', to_right)  5.28 us
    ppermute x2, waiting for transfers between devices, swap_rows(): lax.ppermute(left, 'dom', to_left)  1.33 us
  transfers between devices with their start and end apart: 4, of which 3 were waited for; matrix products, arithmetic and copies ran while one was open for 0% of the time, Pallas kernels for 1%

profile of v4, /device:TPU:25, one launch (start us, length us, event | category | flops | bytes accessed | tf_op | source)
XLA Modules:
  0.0 58.1 jit_solution(5152756161594521513)
XLA Ops:
  0.6 0.0 copy-start
  0.6 1.9 %shard_map.94 = (f32[2,64,128]{2,1,0:T(8,128)S(1)}, f32[95,8,128]{2,1,0:T(8,128)S(1)}, f32[160,8,128]{2,1,0:T(8,128)S(1)}) custom-call(f32[256,128]{1,0:T(8,128)} %bitcast.49, f32[256,128]{1,0:T(8,128)} %bitcast.50, f32[768,128]{1,0:T(8,128)} %bitcast.41, f32[256,128]{1,0:T(8,128)} %bitcast.51, s32[4,128]{1,0:T(4,128)} %bitcast.52, ...), custom_call_target="tpu_custom_call" | custom-call | tf_op jit(solution)/shard_map/pallas_call | solution.py:688
  2.5 7.8 %all-gather = f32[8,64,128]{2,1,0:T(8,128)S(1)} all-gather(f32[2,64,128]{2,1,0:T(8,128)S(1)} %get-tuple-element.33), channel_id=2, replica_groups=mesh['dom'=128,'sub'=4] {'sub'}, dimensions={0}, use_global_device_ids=true | all-gather | bytes 327680 | tf_op jit(solution)/shard_map/all_gather | solution.py:732
  10.3 0.0 copy-done
  10.3 0.7 %shard_map.95 = (f32[38,8,128]{2,1,0:T(8,128)S(1)}, f32[38,8,128]{2,1,0:T(8,128)S(1)}, f32[64,8,128]{2,1,0:T(8,128)S(1)}, f32[64,8,128]{2,1,0:T(8,128)S(1)}, f32...) custom-call(s32[1]{0:T(128)} %bitcast.sub_ref, f32[4,2,64,128]{3,2,1,0:T(8,128)S(1)} %bitcast.47, ...), custom_call_target="tpu_custom_call" | custom-call | tf_op jit(solution)/shard_map/pallas_call | solution.py:688
  11.0 12.2 %collective-permute-start = (f32[38,8,128]{2,1,0:T(8,128)S(1)}, f32[38,8,128]{2,1,0:T(8,128)S(1)}, u32[]{:S(2)}, u32[]{:S(2)}) collective-permute-start(f32[38,8,128]{2,1,0:T(8,128)S(1)} %get-tuple-element.36), channel_id=1, source_target_pairs={{4,0},{8,4},{12,8},{16,12},{20,16},{24,20},{28,24},{32,28},{36,32}... | collective-permute-start | bytes 466952 | tf_op jit(solution)/shard_map/ppermute | solution.py:719
  23.3 1.9 %collective-permute-start.1 = (f32[38,8,128]{2,1,0:T(8,128)S(1)}, f32[38,8,128]{2,1,0:T(8,128)S(1)}, u32[]{:S(2)}, u32[]{:S(2)}) collective-permute-start(f32[38,8,128]{2,1,0:T(8,128)S(1)} %get-tuple-element.37), channel_id=1, source_target_pairs={{0,4},{4,8},{8,12},{12,16},{16,20},{20,24},{24,28},{28,32},{32,36}... | collective-permute-start | bytes 466952 | tf_op jit(solution)/shard_map/ppermute | solution.py:719
  25.2 1.3 %collective-permute-done.mr_ref = f32[38,8,128]{2,1,0:T(8,128)S(1)} collective-permute-done((f32[38,8,128]{2,1,0:T(8,128)S(1)}, f32[38,8,128]{2,1,0:T(8,128)S(1)}, u32[]{:S(2)}, u32[]{:S(2)}) %collective-permute-start) | collective-permute-done | bytes 155680 | tf_op jit(solution)/shard_map/ppermute | solution.py:719
  26.5 6.8 %collective-permute-done.1.ml_ref = f32[38,8,128]{2,1,0:T(8,128)S(1)} collective-permute-done((f32[38,8,128]{2,1,0:T(8,128)S(1)}, f32[38,8,128]{2,1,0:T(8,128)S(1)}, u32[]{:S(2)}, u32[]{:S(2)}) %collective-permute-start.1) | collective-permute-done | bytes 155680 | tf_op jit(solution)/shard_map/ppermute | solution.py:719
  33.3 0.0 copy-start.1
  33.3 1.6 %shard_map.96 = (f32[18,8,128]{2,1,0:T(8,128)S(1)}, f32[18,8,128]{2,1,0:T(8,128)S(1)}, f32[64,8,128]{2,1,0:T(8,128)S(1)}, f32[64,8,128]{2,1,0:T(8,128)S(1)}, f32...) custom-call(f32[38,8,128]{2,1,0:T(8,128)S(1)} %collective-permute-do, ...), custom_call_target="tpu_custom_call" | custom-call | tf_op jit(solution)/shard_map/pallas_call | solution.py:688
  34.9 1.9 %collective-permute-start.2 = (f32[18,8,128]{2,1,0:T(8,128)S(1)}, f32[18,8,128]{2,1,0:T(8,128)S(1)}, u32[]{:S(2)}, u32[]{:S(2)}) collective-permute-start(f32[18,8,128]{2,1,0:T(8,128)S(1)} %get-tuple-element.43), channel_id=1, source_target_pairs={{4,0},{8,4},{12,8},{16,12},{20,16},{24,20},{28,24},{32,28},{36,32}... | collective-permute-start | bytes 221192 | tf_op jit(solution)/shard_map/ppermute | solution.py:719
  36.9 3.4 %collective-permute-start.3 = (f32[18,8,128]{2,1,0:T(8,128)S(1)}, f32[18,8,128]{2,1,0:T(8,128)S(1)}, u32[]{:S(2)}, u32[]{:S(2)}) collective-permute-start(f32[18,8,128]{2,1,0:T(8,128)S(1)} %get-tuple-element.44), channel_id=1, source_target_pairs={{0,4},{4,8},{8,12},{12,16},{16,20},{20,24},{24,28},{28,32},{32,36}... | collective-permute-start | bytes 221192 | tf_op jit(solution)/shard_map/ppermute | solution.py:719
  40.2 0.0 copy-done.1
  40.2 0.1 copy.23
  40.3 0.8 %shard_map.97 = (f32[64,8,128]{2,1,0:T(8,128)S(1)}, f32[192,8,128]{2,1,0:T(8,128)S(1)}, f32[192,8,128]{2,1,0:T(8,128)S(1)}, bf16[512,512]{1,0:T(8,128)(2,1)S(1)}, bf16[64,384]{1,0:T(8,128)(2,1)S(1)}) custom-call(f32[96,8,128]{2,1,0:T(8,128)S(1)} %bitcast.44, f32[95,8,128]{2,1,0:T(8,128)S(1)} %get-tuple-element.34.base_ref, ...), custom_call_target="tpu_custom_call" | custom-call | tf_op jit(solution)/shard_map/pallas_call | solution.py:688
  41.1 0.0 collective-permute-done.2.br_ref
  41.1 3.8 %collective-permute-done.3.bl_ref = f32[18,8,128]{2,1,0:T(8,128)S(1)} collective-permute-done((f32[18,8,128]{2,1,0:T(8,128)S(1)}, f32[18,8,128]{2,1,0:T(8,128)S(1)}, u32[]{:S(2)}, u32[]{:S(2)}) %collective-permute-start.3) | collective-permute-done | bytes 73760 | tf_op jit(solution)/shard_map/ppermute | solution.py:719
  45.0 1.7 %shard_map.98 = (f32[32,8,128]{2,1,0:T(8,128)}, f32[32,8,128]{2,1,0:T(8,128)}, f32[4,64,128]{2,1,0:T(8,128)S(1)}) custom-call(f32[18,8,128]{2,1,0:T(8,128)S(1)} %collective-permute-done.2.br_ref, f32[18,8,128]{2,1,0:T(8,128)S(1)} %collective-permute-done.3.bl_ref, f32[96,8,128]{2,1,0:T(8,128)S(1)} %bitcast.45, f32[64,8,128]{2,1,0:T(8,128)S(1)} %get-tuple-element.45.inv_ref, ...), custom_call_target="tpu_custom_call" | custom-call | tf_op jit(solution)/shard_map/pallas_call | solution.py:688
  46.7 10.7 %all-gather.1 = f32[16,64,128]{2,1,0:T(8,128)S(1)} all-gather(f32[4,64,128]{2,1,0:T(8,128)S(1)} %get-tuple-element.61), channel_id=3, replica_groups=mesh['dom'=128,'sub'=4] {'sub'}, dimensions={0}, use_global_device_ids=true | all-gather | bytes 655360 | tf_op jit(solution)/shard_map/all_gather | solution.py:770
  57.4 0.8 %shard_map.99 = f32[64,128]{1,0:T(8,128)} custom-call(s32[1]{0:T(128)} %bitcast.sub_ref, f32[4,4,64,128]{3,2,1,0:T(8,128)S(1)} %bitcast.46, bf16[64,384]{1,0:T(8,128)(2,1)S(1)} %get-tuple-element.62.stack_ref), custom_call_target="tpu_custom_call" | custom-call | tf_op jit(solution)/shard_map/pallas_call | solution.py:688
Async XLA Ops:
  0.6 9.7 %copy-start = (f32[3,64,2,256]{3,2,1,0:T(2,128)S(1)}, f32[3,64,2,256]{3,2,1,0:T(2,128)}, u32[]{:S(2)}) copy-start(f32[3,64,2,256]{3,2,1,0:T(2,128)} %param.9) | copy-start | bytes 1179652
  11.0 15.5 %collective-permute-start = (f32[38,8,128]{2,1,0:T(8,128)S(1)}, f32[38,8,128]{2,1,0:T(8,128)S(1)}, u32[]{:S(2)}, u32[]{:S(2)}) collective-permute-start(f32[38,8,128]{2,1,0:T(8,128)S(1)} %get-tuple-element.36), channel_id=1, source_target_pairs={{4,0},{8,4},{12,8},{16,12},{20,16},{24,20},{28,24},{32,28},{36,32}... | collective-permute-start | bytes 466952 | tf_op jit(solution)/shard_map/ppermute | solution.py:719
  23.3 10.1 %collective-permute-start.1 = (f32[38,8,128]{2,1,0:T(8,128)S(1)}, f32[38,8,128]{2,1,0:T(8,128)S(1)}, u32[]{:S(2)}, u32[]{:S(2)}) collective-permute-start(f32[38,8,128]{2,1,0:T(8,128)S(1)} %get-tuple-element.37), channel_id=1, source_target_pairs={{0,4},{4,8},{8,12},{12,16},{16,20},{20,24},{24,28},{28,32},{32,36}... | collective-permute-start | bytes 466952 | tf_op jit(solution)/shard_map/ppermute | solution.py:719
  33.3 6.9 %copy-start.1 = (f32[64,64]{1,0:T(8,128)S(1)}, f32[64,64]{1,0:T(8,128)}, u32[]{:S(2)}) copy-start(f32[64,64]{1,0:T(8,128)} %param.12) | copy-start | bytes 49156
  34.9 6.2 %collective-permute-start.2 = (f32[18,8,128]{2,1,0:T(8,128)S(1)}, f32[18,8,128]{2,1,0:T(8,128)S(1)}, u32[]{:S(2)}, u32[]{:S(2)}) collective-permute-start(f32[18,8,128]{2,1,0:T(8,128)S(1)} %get-tuple-element.43), channel_id=1, source_target_pairs={{4,0},{8,4},{12,8},{16,12},{20,16},{24,20},{28,24},{32,28},{36,32}... | collective-permute-start | bytes 221192 | tf_op jit(solution)/shard_map/ppermute | solution.py:719
  36.9 8.1 %collective-permute-start.3 = (f32[18,8,128]{2,1,0:T(8,128)S(1)}, f32[18,8,128]{2,1,0:T(8,128)S(1)}, u32[]{:S(2)}, u32[]{:S(2)}) collective-permute-start(f32[18,8,128]{2,1,0:T(8,128)S(1)} %get-tuple-element.44), channel_id=1, source_target_pairs={{0,4},{4,8},{8,12},{12,16},{16,20},{20,24},{24,28},{28,32},{32,36}... | collective-permute-start | bytes 221192 | tf_op jit(solution)/shard_map/ppermute | solution.py:719

commit v5 on v4

--- a/solution.py
+++ b/solution.py
@@ -143,12 +143,28 @@
     return jnp.where(mk["even"], get(q), get(48 + q))
 
 
-def pack_faces(left_ref, right_ref, base, get, mk):
+class Send:
+    def __init__(self, far_ref, near_ref, odd):
+        self.far, self.near, self.odd = far_ref, near_ref, odd
+
+    def put(self, at, left, right):
+        self.far[at] = jnp.where(self.odd, right, left)
+        self.near[at] = jnp.where(self.odd, left, right)
+
+
+class Receive:
+    def __init__(self, odd_ref, even_ref, odd):
+        self.odd_ref, self.even_ref, self.odd = odd_ref, even_ref, odd
+
+    def __getitem__(self, at):
+        return jnp.where(self.odd, self.odd_ref[at], self.even_ref[at])
+
+
+def pack_faces(send, base, get, mk):
     even = mk["even"]
     for p in range(8):
         x, y = get(2 * p), get(2 * p + 1)
-        left_ref[base + p] = jnp.where(even, x, rs(y, 1))
-        right_ref[base + p] = jnp.where(even, rs(x, 7), y)
+        send.put(base + p, jnp.where(even, x, rs(y, 1)), jnp.where(even, rs(x, 7), y))
 
 
 def unpack_face(from_right, from_left, base, q, mk):
@@ -261,11 +277,10 @@
     return both, rl(both, 64)
 
 
-def strip_send(left_ref, right_ref, base, x, y):
+def strip_send(send, base, x, y):
     both = jnp.where(lane_iota(16) < 64, x, rl(y, 64))
     for p in range(2):
-        left_ref[base + p] = both[8 * p : 8 * p + 8]
-        right_ref[base + p] = both[8 * p : 8 * p + 8]
+        send.put(base + p, both[8 * p : 8 * p + 8], both[8 * p : 8 * p + 8])
 
 
 def strip_response(delta, diagonal, mod_j, mod_k, cf):
@@ -398,15 +413,16 @@
 
 
 def open_kernel(
-    sub_ref, z_ref, base_ref, head_ref, mod_ref,
-    left_ref, right_ref, u1_ref, v1_ref, inv_ref, strip_ref, smod_ref,
+    place_ref, z_ref, base_ref, head_ref, mod_ref,
+    far_ref, near_ref, u1_ref, v1_ref, inv_ref, strip_ref, smod_ref,
     f, sx,
 ):
     u0_ref, f0_ref = base_ref.at[U0:OWNER], head_ref.at[F0:MASS]
     mass2_ref, const_ref = head_ref.at[MASS:FACES], head_ref.at[FACES:HEAD]
     cf_ref = base_ref.at[WEIGHTS:BASE]
     mk = masks()
-    sub = sub_ref[0]
+    sub = place_ref[0]
+    send = Send(far_ref, near_ref, place_ref[1] == 1)
     lane = lane_iota(64)
     side0 = ((lane // 16) % 2) == 1
     c = lane % 8
@@ -431,10 +447,10 @@
         for e in (0, 3)
     ]
     strip_send(
-        left_ref, right_ref, STRIP + 2, strip_faces(smass), jnp.where(zero, *diagonal)
+        send, STRIP + 2, strip_faces(smass), jnp.where(zero, *diagonal)
     )
     strip_send(
-        left_ref, right_ref, STRIP + 4, strip_faces(mods[64:128]), strip_faces(mods[128:192])
+        send, STRIP + 4, strip_faces(mods[64:128]), strip_faces(mods[128:192])
     )
     sm = strip_x(smass, 0.0)
     sx[0] = sm
@@ -442,7 +458,7 @@
     sx[1] = fx
     sinv = strip_not_shared(inverse_mass(strip_y(sm)))
     partial = strip_forces(us - sinv * strip_y(fx), mods, cf_ref)
-    strip_send(left_ref, right_ref, STRIP, strip_faces(fs), strip_faces(partial))
+    strip_send(send, STRIP, strip_faces(fs), strip_faces(partial))
 
     def put_mass(n, total):
         inv_ref[n] = not_shared(n, inverse_mass(total), mk)
@@ -456,22 +472,28 @@
 
     assemble(lambda n: f0_ref[n], None, sx.at[1], mk, put)
     forces(lambda n: u1_ref[n], into(f), lambda p: mod_ref[p], mk, planes=(0, 3))
-    pack_faces(left_ref, right_ref, 0, lambda q: face_tile(lambda n: f0_ref[n], q, mk), mk)
-    pack_faces(left_ref, right_ref, 8, lambda q: face_tile(lambda n: f[n], q, mk), mk)
-    pack_faces(left_ref, right_ref, CONST, lambda q: const_ref[q], mk)
-    pack_faces(left_ref, right_ref, CONST + 8, lambda q: const_ref[16 + q], mk)
+    pack_faces(send, 0, lambda q: face_tile(lambda n: f0_ref[n], q, mk), mk)
+    pack_faces(send, 8, lambda q: face_tile(lambda n: f[n], q, mk), mk)
+    pack_faces(send, CONST, lambda q: const_ref[q], mk)
+    pack_faces(send, CONST + 8, lambda q: const_ref[16 + q], mk)
+
+
+def rim(n):
+    return n if n < 16 else n - 32
 
 
 def middle_kernel(
-    mr_ref, ml_ref, base_ref, head_ref, u1p_ref, v1p_ref, invp_ref, strip_ref, smod_ref,
+    place_ref, far_in, near_in, base_ref, head_ref, u1p_ref, v1p_ref, invp_ref, strip_ref, smod_ref,
     mod_ref,
-    bl_ref, br_ref, inv_ref, u1_ref, u2_ref, v2_ref, f2_ref, u3_ref, v3_ref, resp_ref,
-    sresp_ref, sstate_ref,
-    v1, f, sx, beside,
+    far_ref, near_ref, inv_ref, u1_ref, u2_ref, rims_ref, inner_ref, resp_ref, sresp_ref, sstate_ref,
+    v1, f, v2_ref, f2_ref, u3_ref, sx, beside,
 ):
     u0_ref, f0_ref = base_ref.at[U0:OWNER], head_ref.at[F0:MASS]
     mass2_ref, cf_ref = head_ref.at[MASS:FACES], base_ref.at[WEIGHTS:BASE]
     mk = masks()
+    odd = place_ref[1] == 1
+    mr_ref, ml_ref = Receive(far_in, near_in, odd), Receive(near_in, far_in, odd)
+    send = Send(far_ref, near_ref, odd)
     lo = mk["lo"]
     us, fs, smass = strip_ref[0], strip_ref[1], strip_ref[2]
     mods = smod_ref[...]
@@ -547,14 +569,19 @@
 
     def put2(n, total):
         vel = v2_ref[n] - not_shared(n, inv_ref[n], mk) * total
-        v3_ref[n] = vel
         u3_ref[n] = u2_ref[n] + vel
+        if 16 <= n < 48:
+            inner_ref[0, n - 16] = u3_ref[n]
+            inner_ref[1, n - 16] = vel
 
     assemble(lambda n: f2_ref[n], None, sx.at[3], mk, put2)
+    for n in list(range(16)) + list(range(48, 64)):
+        rims_ref[0, rim(n)] = v2_ref[n]
+        rims_ref[1, rim(n)] = f2_ref[n]
     forces(lambda n: u3_ref[n], into(f), lambda p: mod_ref[p], mk, planes=(0, 3))
-    pack_faces(bl_ref, br_ref, 0, lambda q: face_tile(lambda n: f2_ref[n], q, mk), mk)
-    pack_faces(bl_ref, br_ref, 8, lambda q: face_tile(lambda n: f[n], q, mk), mk)
-    strip_send(bl_ref, br_ref, STRIP_B, strip_faces(fs), strip_faces(partial))
+    pack_faces(send, 0, lambda q: face_tile(lambda n: f2_ref[n], q, mk), mk)
+    pack_faces(send, 8, lambda q: face_tile(lambda n: f[n], q, mk), mk)
+    strip_send(send, STRIP_B, strip_faces(fs), strip_faces(partial))
 
 
 def three_way(x):
@@ -594,13 +621,15 @@
 
 
 def last_kernel(
-    br_ref, bl_ref, mod_ref, inv_ref, u2_ref, v2_ref, f2_ref, u3p_ref, v3p_ref, resp_ref,
+    place_ref, far_in, near_in, mod_ref, inv_ref, u2_ref, rims_ref, inner_ref, resp_ref,
     sresp_ref, sstate_ref, smod_ref, d2_ref, x0_ref, x1_ref, hot_ref, base_ref,
     out_u_ref, out_w_ref, sums_ref,
     u, v, f, sx, beside, dens,
 ):
     cf_ref = base_ref.at[WEIGHTS:BASE]
     mk = masks()
+    odd = place_ref[1] == 1
+    br_ref, bl_ref = Receive(far_in, near_in, odd), Receive(near_in, far_in, odd)
     lo = mk["lo"]
     mods = smod_ref[...]
     us, svel, fs, sinv = sstate_ref[0], sstate_ref[1], sstate_ref[2], sstate_ref[3]
@@ -610,17 +639,17 @@
     spush = -sinv * strip_y(fs)
     us = us + (svel + spush)
     for n in range(16, 48):
-        u[n] = u3p_ref[n]
-        v[n] = v3p_ref[n]
+        u[n] = inner_ref[0, n - 16]
+        v[n] = inner_ref[1, n - 16]
 
     def put2(n, total):
-        vel = v2_ref[n] - inv_ref[n] * total
+        vel = rims_ref[0, rim(n)] - inv_ref[n] * total
         v[n] = vel
         u[n] = u2_ref[n] + vel
 
     assemble(
-        lambda n: f2_ref[n], lambda q: unpack_face(br_ref, bl_ref, 0, q, mk), sx.at[0], mk, put2,
-        (0, 3),
+        lambda n: rims_ref[1, rim(n)], lambda q: unpack_face(br_ref, bl_ref, 0, q, mk), sx.at[0],
+        mk, put2, (0, 3),
     )
 
     def add_third(direction, n, g):
@@ -629,7 +658,7 @@
         dens[at, :] = before + x1_ref[64 * direction + n] * g
 
     forces(lambda n: u[n], into(f), lambda p: mod_ref[p], mk, hook=add_third)
-    delta = [face_tile(lambda n: v[n] - v2_ref[n], q, mk) for q in range(16)]
+    delta = [face_tile(lambda n: v[n] - rims_ref[0, rim(n)], q, mk) for q in range(16)]
     for q, x in enumerate(face_response(delta, *[lambda q, d=d: resp_ref[d, q] for d in range(3)])):
         beside[q] = unpack_face(br_ref, bl_ref, 8, q, mk) + x
     sbeside = sp3 + strip_response(
@@ -664,8 +693,8 @@
         out_w_ref[p] = jnp.where(lo, rs(a, 4), b)
 
 
-def project_kernel(sub_ref, x_ref, stack_ref, out_ref):
-    sub = sub_ref[0]
+def project_kernel(place_ref, x_ref, stack_ref, out_ref):
+    sub = place_ref[0]
     total = (x_ref[0, sub] + x_ref[1, sub]) + (x_ref[2, sub] + x_ref[3, sub])
     t0, t1, t2 = three_way(total)
     out_ref[...] = KERNEL_SCALE * jnp.dot(
@@ -706,17 +735,17 @@
 
 def on_device(initial_field, adjoint_source, moduli, node_mass, block_owner, spline_basis):
     count = lax.axis_size("dom")
-    to_right = [(i, i + 1) for i in range(count - 1)]
-    to_left = [(b, a) for a, b in to_right]
+    near_pairs = [(i, i ^ 1) for i in range(count)]
+    far_pairs = [(i, ((i + 1) ^ 1) - 1) for i in range(1, count - 1)]
     cf = jnp.asarray(COEFFICIENTS)
-    sub = lax.axis_index("sub").astype(jnp.int32).reshape(1)
+    place = jnp.stack([lax.axis_index("sub"), lax.axis_index("dom") & 1]).astype(jnp.int32)
     u2d, w2d, m2d, mass2d = map(raw_tiles, (initial_field, adjoint_source, moduli, node_mass))
     owner = raw_tiles(block_owner[None])
     mod = m2d.reshape(96, 8, 128)
     full, face = (64, 8, 128), (16, 8, 128)
 
-    def swap_rows(left, right):
-        return lax.ppermute(left, "dom", to_left), lax.ppermute(right, "dom", to_right)
+    def swap_rows(far, near):
+        return lax.ppermute(far, "dom", far_pairs), lax.ppermute(near, "dom", near_pairs)
 
     edges, base, head = call(
         first_kernel,
@@ -730,26 +759,27 @@
         space=pltpu.VMEM,
     )
     edges = lax.all_gather(edges, "sub")
-    left, right, u1p, v1p, invp, strips, smod = call(
+    far, near, u1p, v1p, invp, strips, smod = call(
         open_kernel,
         [(MSG, 8, 128), (MSG, 8, 128), full, full, full, (3, 64, 128), (192, 128)],
-        [sub, edges, base, head, mod],
+        [place, edges, base, head, mod],
         [pltpu.VMEM(full, F32), pltpu.VMEM((2, 64, 128), F32)],
         specs=[SMEM],
         space=pltpu.VMEM,
     )
-    from_right, from_left = swap_rows(left, right)
-    left, right, inv, u1, u2, v2, f2, u3p, v3p, resp, sresp, sstate = call(
+    far, near = swap_rows(far, near)
+    far, near, inv, u1, u2, rims, inner, resp, sresp, sstate = call(
         middle_kernel,
         [
-            (MSG_B, 8, 128), (MSG_B, 8, 128), full, full, full, full, full, full, full,
-            (3, 16, 8, 128), (3, 16, 128), (4, 64, 128),
+            (MSG_B, 8, 128), (MSG_B, 8, 128), full, full, full, (2, 32, 8, 128),
+            (2, 32, 8, 128), (3, 16, 8, 128), (3, 16, 128), (4, 64, 128),
         ],
-        [from_right, from_left, base, head, u1p, v1p, invp, strips, smod, mod],
-        [pltpu.VMEM(full, F32)] * 2 + [pltpu.VMEM((4, 64, 128), F32), pltpu.VMEM(face, F32)],
+        [place, far, near, base, head, u1p, v1p, invp, strips, smod, mod],
+        [pltpu.VMEM(full, F32)] * 5 + [pltpu.VMEM((4, 64, 128), F32), pltpu.VMEM(face, F32)],
+        specs=[SMEM],
         space=pltpu.VMEM,
     )
-    from_right, from_left = swap_rows(left, right)
+    far, near = swap_rows(far, near)
     wide = jax.ShapeDtypeStruct((512, 512), BF16)
     d2, x0, x1, hot, stack = call(
         density_kernel,
@@ -761,14 +791,15 @@
         last_kernel,
         [(32, 8, 128), (32, 8, 128), (4, 64, 128)],
         [
-            from_right, from_left, mod, inv, u2, v2, f2, u3p, v3p, resp, sresp, sstate, smod,
+            place, far, near, mod, inv, u2, rims, inner, resp, sresp, sstate, smod,
             d2, x0, x1, hot, base,
         ],
         [pltpu.VMEM(full, F32)] * 3
         + [pltpu.VMEM((2, 64, 128), F32), pltpu.VMEM(face, F32), pltpu.VMEM((512, 128), F32)],
+        specs=[SMEM],
     )
     sums = lax.all_gather(sums, "sub")
-    (kernel,) = call(project_kernel, [(64, 128)], [sub, sums, stack], specs=[SMEM])
+    (kernel,) = call(project_kernel, [(64, 128)], [place, sums, stack], specs=[SMEM])
     return from_tiles(out_u), from_tiles(out_w), kernel
 
 

time: 58.4 us -> 56 us (0.959)
  waiting for transfers between devices: 12 us -> 7.7 us
  Pallas kernels: 7.47 us -> 9.64 us
    ppermute x4, waiting for transfers between devices: 12 us -> 7.7 us  [the longest x2 4.26 us: swap_rows(): lax.ppermute(far, 'dom', far_pairs)]
    pallas_call x6, Pallas kernels: 7.47 us -> 9.64 us  [call(): pl.pallas_call(kernel, out_shape=outs, in_specs=specs, out_specs=[VMEM] *...]
  transfers between devices with their start and end apart: 4 -> 4, of which waited for: 3 -> 4; matrix products, arithmetic and copies ran while one was open for 0% -> 0% of each run, Pallas kernels for 1% -> 1%
where the time goes in v5:
time: 56 us; the launch traced here: 55.7 us
  starting transfers between devices  19.4 us (35%)
  blocking collectives  18.1 us (32%)
  Pallas kernels  9.64 us (17%)
  waiting for transfers between devices  7.7 us (14%)
  between operations  0.71 us (1%)
    ppermute x2, starting transfers between devices, swap_rows(): lax.ppermute(far, 'dom', far_pairs)  15.6 us
    all_gather x1, blocking collectives, on_device(): sums = lax.all_gather(sums, 'sub')  10.3 us
    pallas_call x6, Pallas kernels, call(): pl.pallas_call(kernel, out_shape=outs, in_specs=specs, out_specs=[VMEM] *...  9.64 us
    all_gather x1, blocking collectives, on_device(): edges = lax.all_gather(edges, 'sub')  7.8 us
    ppermute x2, waiting for transfers between devices, swap_rows(): lax.ppermute(far, 'dom', far_pairs)  4.26 us
    ppermute x2, starting transfers between devices, swap_rows(): lax.ppermute(near, 'dom', near_pairs)  3.84 us
    ppermute x2, waiting for transfers between devices, swap_rows(): lax.ppermute(near, 'dom', near_pairs)  3.44 us
  transfers between devices with their start and end apart: 4, of which 4 were waited for; matrix products, arithmetic and copies ran while one was open for 0% of the time, Pallas kernels for 1%

profile of v5, /device:TPU:25, one launch (start us, length us, event | category | flops | bytes accessed | tf_op | source)
XLA Modules:
  0.0 55.7 jit_solution(1185301279275240911)
XLA Ops:
  0.6 0.0 copy-start
  0.6 1.9 %shard_map.94 = (f32[2,64,128]{2,1,0:T(8,128)S(1)}, f32[95,8,128]{2,1,0:T(8,128)S(1)}, f32[160,8,128]{2,1,0:T(8,128)S(1)}) custom-call(f32[256,128]{1,0:T(8,128)} %bitcast.50, f32[256,128]{1,0:T(8,128)} %bitcast.51, f32[768,128]{1,0:T(8,128)} %bitcast.42, f32[256,128]{1,0:T(8,128)} %bitcast.52, s32[4,128]{1,0:T(4,128)} %bitcast.53, ...), custom_call_target="tpu_custom_call" | custom-call | tf_op jit(solution)/shard_map/pallas_call | solution.py:717
  2.5 7.8 %all-gather = f32[8,64,128]{2,1,0:T(8,128)S(1)} all-gather(f32[2,64,128]{2,1,0:T(8,128)S(1)} %get-tuple-element.31), channel_id=2, replica_groups=mesh['dom'=128,'sub'=4] {'sub'}, dimensions={0}, use_global_device_ids=true | all-gather | bytes 327680 | tf_op jit(solution)/shard_map/all_gather | solution.py:761
  10.3 0.1 pad_add_fusion.place_ref
  10.4 0.0 copy-done
  10.4 1.3 %shard_map.95 = (f32[38,8,128]{2,1,0:T(8,128)S(1)}, f32[38,8,128]{2,1,0:T(8,128)S(1)}, f32[64,8,128]{2,1,0:T(8,128)S(1)}, f32[64,8,128]{2,1,0:T(8,128)S(1)}, f32...) custom-call(s32[2]{0:T(128)S(1)} %pad_add_fusion.place_ref, ...), custom_call_target="tpu_custom_call" | custom-call | tf_op jit(solution)/shard_map/pallas_call | solution.py:717
  11.7 12.2 %collective-permute-start = (f32[38,8,128]{2,1,0:T(8,128)S(1)}, f32[38,8,128]{2,1,0:T(8,128)S(1)}, u32[]{:S(2)}, u32[]{:S(2)}) collective-permute-start(f32[38,8,128]{2,1,0:T(8,128)S(1)} %get-tuple-element.34), channel_id=1, source_target_pairs={{4,8},{8,4},{12,16},{16,12},{20,24},{24,20},{28,32},{32,28},{36,40... | collective-permute-start | bytes 466952 | tf_op jit(solution)/shard_map/ppermute | solution.py:748
  23.9 1.9 %collective-permute-start.1 = (f32[38,8,128]{2,1,0:T(8,128)S(1)}, f32[38,8,128]{2,1,0:T(8,128)S(1)}, u32[]{:S(2)}, u32[]{:S(2)}) collective-permute-start(f32[38,8,128]{2,1,0:T(8,128)S(1)} %get-tuple-element.35), channel_id=1, source_target_pairs={{0,4},{4,0},{8,12},{12,8},{16,20},{20,16},{24,28},{28,24},{32,36},... | collective-permute-start | bytes 466952 | tf_op jit(solution)/shard_map/ppermute | solution.py:748
  25.9 2.3 %collective-permute-done.far_in = f32[38,8,128]{2,1,0:T(8,128)S(1)} collective-permute-done((f32[38,8,128]{2,1,0:T(8,128)S(1)}, f32[38,8,128]{2,1,0:T(8,128)S(1)}, u32[]{:S(2)}, u32[]{:S(2)}) %collective-permute-start) | collective-permute-done | bytes 155680 | tf_op jit(solution)/shard_map/ppermute | solution.py:748
  28.2 2.8 %collective-permute-done.1.near_in = f32[38,8,128]{2,1,0:T(8,128)S(1)} collective-permute-done((f32[38,8,128]{2,1,0:T(8,128)S(1)}, f32[38,8,128]{2,1,0:T(8,128)S(1)}, u32[]{:S(2)}, u32[]{:S(2)}) %collective-permute-start.1) | collective-permute-done | bytes 155680 | tf_op jit(solution)/shard_map/ppermute | solution.py:748
  31.0 0.0 copy-start.1
  31.0 2.1 %shard_map.96 = (f32[18,8,128]{2,1,0:T(8,128)S(1)}, f32[18,8,128]{2,1,0:T(8,128)S(1)}, f32[64,8,128]{2,1,0:T(8,128)S(1)}, f32[64,8,128]{2,1,0:T(8,128)S(1)}, f32...) custom-call(s32[2]{0:T(128)S(1)} %pad_add_fusion.place_ref, ...), custom_call_target="tpu_custom_call" | custom-call | tf_op jit(solution)/shard_map/pallas_call | solution.py:717
  33.1 3.3 %collective-permute-start.2 = (f32[18,8,128]{2,1,0:T(8,128)S(1)}, f32[18,8,128]{2,1,0:T(8,128)S(1)}, u32[]{:S(2)}, u32[]{:S(2)}) collective-permute-start(f32[18,8,128]{2,1,0:T(8,128)S(1)} %get-tuple-element.41), channel_id=1, source_target_pairs={{4,8},{8,4},{12,16},{16,12},{20,24},{24,20},{28,32},{32,28},{36,40... | collective-permute-start | bytes 221192 | tf_op jit(solution)/shard_map/ppermute | solution.py:748
  36.4 1.9 %collective-permute-start.3 = (f32[18,8,128]{2,1,0:T(8,128)S(1)}, f32[18,8,128]{2,1,0:T(8,128)S(1)}, u32[]{:S(2)}, u32[]{:S(2)}) collective-permute-start(f32[18,8,128]{2,1,0:T(8,128)S(1)} %get-tuple-element.42), channel_id=1, source_target_pairs={{0,4},{4,0},{8,12},{12,8},{16,20},{20,16},{24,28},{28,24},{32,36},... | collective-permute-start | bytes 221192 | tf_op jit(solution)/shard_map/ppermute | solution.py:748
  38.3 0.0 copy-done.1
  38.3 0.1 copy.23
  38.4 0.8 %shard_map.97 = (f32[64,8,128]{2,1,0:T(8,128)S(1)}, f32[192,8,128]{2,1,0:T(8,128)S(1)}, f32[192,8,128]{2,1,0:T(8,128)S(1)}, bf16[512,512]{1,0:T(8,128)(2,1)S(1)}, bf16[64,384]{1,0:T(8,128)(2,1)S(1)}) custom-call(f32[96,8,128]{2,1,0:T(8,128)S(1)} %bitcast.45, f32[95,8,128]{2,1,0:T(8,128)S(1)} %get-tuple-element.32.base_ref, ...), custom_call_target="tpu_custom_call" | custom-call | tf_op jit(solution)/shard_map/pallas_call | solution.py:717
  39.2 2.0 %collective-permute-done.2.far_in = f32[18,8,128]{2,1,0:T(8,128)S(1)} collective-permute-done((f32[18,8,128]{2,1,0:T(8,128)S(1)}, f32[18,8,128]{2,1,0:T(8,128)S(1)}, u32[]{:S(2)}, u32[]{:S(2)}) %collective-permute-start.2) | collective-permute-done | bytes 73760 | tf_op jit(solution)/shard_map/ppermute | solution.py:748
  41.2 0.6 %collective-permute-done.3.near_in = f32[18,8,128]{2,1,0:T(8,128)S(1)} collective-permute-done((f32[18,8,128]{2,1,0:T(8,128)S(1)}, f32[18,8,128]{2,1,0:T(8,128)S(1)}, u32[]{:S(2)}, u32[]{:S(2)}) %collective-permute-start.3) | collective-permute-done | bytes 73760 | tf_op jit(solution)/shard_map/ppermute | solution.py:748
  41.8 2.3 %shard_map.98 = (f32[32,8,128]{2,1,0:T(8,128)}, f32[32,8,128]{2,1,0:T(8,128)}, f32[4,64,128]{2,1,0:T(8,128)S(1)}) custom-call(s32[2]{0:T(128)S(1)} %pad_add_fusion.place_ref, f32[18,8,128]{2,1,0:T(8,128)S(1)} %collective-permute-done.2.far_in, f32[18,8,128]{2,1,0:T(8,128)S(1)} %collective-permute-done.3.near_in, f32[96,8,128]{2,1,0:T(8,128)S(1)} %bitcast.46, ...), custom_call_target="tpu_custom_call" | custom-call | tf_op jit(solution)/shard_map/pallas_call | solution.py:717
  44.1 10.3 %all-gather.1 = f32[16,64,128]{2,1,0:T(8,128)S(1)} all-gather(f32[4,64,128]{2,1,0:T(8,128)S(1)} %get-tuple-element.57), channel_id=3, replica_groups=mesh['dom'=128,'sub'=4] {'sub'}, dimensions={0}, use_global_device_ids=true | all-gather | bytes 655360 | tf_op jit(solution)/shard_map/all_gather | solution.py:801
  54.4 1.3 %shard_map.99 = f32[64,128]{1,0:T(8,128)} custom-call(s32[2]{0:T(128)S(1)} %pad_add_fusion.place_ref, f32[4,4,64,128]{3,2,1,0:T(8,128)S(1)} %bitcast.47, bf16[64,384]{1,0:T(8,128)(2,1)S(1)} %get-tuple-element.58.stack_ref), custom_call_target="tpu_custom_call" | custom-call | tf_op jit(solution)/shard_map/pallas_call | solution.py:717
Async XLA Ops:
  0.6 9.8 %copy-start = (f32[3,64,2,256]{3,2,1,0:T(2,128)S(1)}, f32[3,64,2,256]{3,2,1,0:T(2,128)}, u32[]{:S(2)}) copy-start(f32[3,64,2,256]{3,2,1,0:T(2,128)} %param.9) | copy-start | bytes 1179652
  11.7 16.5 %collective-permute-start = (f32[38,8,128]{2,1,0:T(8,128)S(1)}, f32[38,8,128]{2,1,0:T(8,128)S(1)}, u32[]{:S(2)}, u32[]{:S(2)}) collective-permute-start(f32[38,8,128]{2,1,0:T(8,128)S(1)} %get-tuple-element.34), channel_id=1, source_target_pairs={{4,8},{8,4},{12,16},{16,12},{20,24},{24,20},{28,32},{32,28},{36,40... | collective-permute-start | bytes 466952 | tf_op jit(solution)/shard_map/ppermute | solution.py:748
  23.9 7.0 %collective-permute-start.1 = (f32[38,8,128]{2,1,0:T(8,128)S(1)}, f32[38,8,128]{2,1,0:T(8,128)S(1)}, u32[]{:S(2)}, u32[]{:S(2)}) collective-permute-start(f32[38,8,128]{2,1,0:T(8,128)S(1)} %get-tuple-element.35), channel_id=1, source_target_pairs={{0,4},{4,0},{8,12},{12,8},{16,20},{20,16},{24,28},{28,24},{32,36},... | collective-permute-start | bytes 466952 | tf_op jit(solution)/shard_map/ppermute | solution.py:748
  31.0 7.3 %copy-start.1 = (f32[64,64]{1,0:T(8,128)S(1)}, f32[64,64]{1,0:T(8,128)}, u32[]{:S(2)}) copy-start(f32[64,64]{1,0:T(8,128)} %param.12) | copy-start | bytes 49156
  33.1 8.1 %collective-permute-start.2 = (f32[18,8,128]{2,1,0:T(8,128)S(1)}, f32[18,8,128]{2,1,0:T(8,128)S(1)}, u32[]{:S(2)}, u32[]{:S(2)}) collective-permute-start(f32[18,8,128]{2,1,0:T(8,128)S(1)} %get-tuple-element.41), channel_id=1, source_target_pairs={{4,8},{8,4},{12,16},{16,12},{20,24},{24,20},{28,32},{32,28},{36,40... | collective-permute-start | bytes 221192 | tf_op jit(solution)/shard_map/ppermute | solution.py:748
  36.4 5.4 %collective-permute-start.3 = (f32[18,8,128]{2,1,0:T(8,128)S(1)}, f32[18,8,128]{2,1,0:T(8,128)S(1)}, u32[]{:S(2)}, u32[]{:S(2)}) collective-permute-start(f32[18,8,128]{2,1,0:T(8,128)S(1)} %get-tuple-element.42), channel_id=1, source_target_pairs={{0,4},{4,0},{8,12},{12,8},{16,20},{20,16},{24,28},{28,24},{32,36},... | collective-permute-start | bytes 221192 | tf_op jit(solution)/shard_map/ppermute | solution.py:748

commit v6 on v5

--- a/solution.py
+++ b/solution.py
@@ -359,8 +359,6 @@
     ]
     for c in copies:
         c.start()
-    for c in copies:
-        c.wait()
     mk = masks()
     lane = lane_iota(64)
     pieces = (
@@ -372,7 +370,9 @@
         (mass_ref, 0, 1, 1),
     )
     z = [jnp.zeros((64, 128), jnp.float32), jnp.zeros((64, 128), jnp.float32)]
-    for ref, base, half, slot in pieces:
+    for step, (ref, base, half, slot) in enumerate(pieces):
+        for arrival in ((1,), (0,), (2,), (), (), (3,))[step]:
+            copies[arrival].wait()
         for side in range(2):
             for r in range(2):
                 rows = ref[pl.ds(base + 2 * (1 - side) + r, 64, stride=4), :]
@@ -406,6 +406,8 @@
             mk["lo"], face_tile(moduli(1), q, mk), face_tile(moduli(2), q, mk)
         )
     forces(lambda n: state_ref[n], into(f_ref), lambda p: tile(m_ref, p), mk)
+    copies[4].wait()
+    copies[5].wait()
     owner = owner_ref[...].astype(jnp.float32)
     base_ref[OWNER] = jnp.concatenate([owner, owner], axis=0)
     for t in range(WEIGHTS, BASE):
@@ -413,7 +415,7 @@
 
 
 def open_kernel(
-    place_ref, z_ref, base_ref, head_ref, mod_ref,
+    odd_ref, sub_ref, z_ref, base_ref, head_ref, mod_ref,
     far_ref, near_ref, u1_ref, v1_ref, inv_ref, strip_ref, smod_ref,
     f, sx,
 ):
@@ -421,8 +423,8 @@
     mass2_ref, const_ref = head_ref.at[MASS:FACES], head_ref.at[FACES:HEAD]
     cf_ref = base_ref.at[WEIGHTS:BASE]
     mk = masks()
-    sub = place_ref[0]
-    send = Send(far_ref, near_ref, place_ref[1] == 1)
+    sub = sub_ref[0]
+    send = Send(far_ref, near_ref, odd_ref[0] == 1)
     lane = lane_iota(64)
     side0 = ((lane // 16) % 2) == 1
     c = lane % 8
@@ -483,7 +485,7 @@
 
 
 def middle_kernel(
-    place_ref, far_in, near_in, base_ref, head_ref, u1p_ref, v1p_ref, invp_ref, strip_ref, smod_ref,
+    odd_ref, far_in, near_in, base_ref, head_ref, u1p_ref, v1p_ref, invp_ref, strip_ref, smod_ref,
     mod_ref,
     far_ref, near_ref, inv_ref, u1_ref, u2_ref, rims_ref, inner_ref, resp_ref, sresp_ref, sstate_ref,
     v1, f, v2_ref, f2_ref, u3_ref, sx, beside,
@@ -491,7 +493,7 @@
     u0_ref, f0_ref = base_ref.at[U0:OWNER], head_ref.at[F0:MASS]
     mass2_ref, cf_ref = head_ref.at[MASS:FACES], base_ref.at[WEIGHTS:BASE]
     mk = masks()
-    odd = place_ref[1] == 1
+    odd = odd_ref[0] == 1
     mr_ref, ml_ref = Receive(far_in, near_in, odd), Receive(near_in, far_in, odd)
     send = Send(far_ref, near_ref, odd)
     lo = mk["lo"]
@@ -621,14 +623,14 @@
 
 
 def last_kernel(
-    place_ref, far_in, near_in, mod_ref, inv_ref, u2_ref, rims_ref, inner_ref, resp_ref,
+    odd_ref, far_in, near_in, mod_ref, inv_ref, u2_ref, rims_ref, inner_ref, resp_ref,
     sresp_ref, sstate_ref, smod_ref, d2_ref, x0_ref, x1_ref, hot_ref, base_ref,
     out_u_ref, out_w_ref, sums_ref,
     u, v, f, sx, beside, dens,
 ):
     cf_ref = base_ref.at[WEIGHTS:BASE]
     mk = masks()
-    odd = place_ref[1] == 1
+    odd = odd_ref[0] == 1
     br_ref, bl_ref = Receive(far_in, near_in, odd), Receive(near_in, far_in, odd)
     lo = mk["lo"]
     mods = smod_ref[...]
@@ -693,8 +695,8 @@
         out_w_ref[p] = jnp.where(lo, rs(a, 4), b)
 
 
-def project_kernel(place_ref, x_ref, stack_ref, out_ref):
-    sub = place_ref[0]
+def project_kernel(sub_ref, x_ref, stack_ref, out_ref):
+    sub = sub_ref[0]
     total = (x_ref[0, sub] + x_ref[1, sub]) + (x_ref[2, sub] + x_ref[3, sub])
     t0, t1, t2 = three_way(total)
     out_ref[...] = KERNEL_SCALE * jnp.dot(
@@ -738,7 +740,8 @@
     near_pairs = [(i, i ^ 1) for i in range(count)]
     far_pairs = [(i, ((i + 1) ^ 1) - 1) for i in range(1, count - 1)]
     cf = jnp.asarray(COEFFICIENTS)
-    place = jnp.stack([lax.axis_index("sub"), lax.axis_index("dom") & 1]).astype(jnp.int32)
+    sub = lax.axis_index("sub").astype(jnp.int32).reshape(1)
+    odd = (lax.axis_index("dom") & 1).astype(jnp.int32).reshape(1)
     u2d, w2d, m2d, mass2d = map(raw_tiles, (initial_field, adjoint_source, moduli, node_mass))
     owner = raw_tiles(block_owner[None])
     mod = m2d.reshape(96, 8, 128)
@@ -762,9 +765,9 @@
     far, near, u1p, v1p, invp, strips, smod = call(
         open_kernel,
         [(MSG, 8, 128), (MSG, 8, 128), full, full, full, (3, 64, 128), (192, 128)],
-        [place, edges, base, head, mod],
+        [odd, sub, edges, base, head, mod],
         [pltpu.VMEM(full, F32), pltpu.VMEM((2, 64, 128), F32)],
-        specs=[SMEM],
+        specs=[SMEM, SMEM],
         space=pltpu.VMEM,
     )
     far, near = swap_rows(far, near)
@@ -774,7 +777,7 @@
             (MSG_B, 8, 128), (MSG_B, 8, 128), full, full, full, (2, 32, 8, 128),
             (2, 32, 8, 128), (3, 16, 8, 128), (3, 16, 128), (4, 64, 128),
         ],
-        [place, far, near, base, head, u1p, v1p, invp, strips, smod, mod],
+        [odd, far, near, base, head, u1p, v1p, invp, strips, smod, mod],
         [pltpu.VMEM(full, F32)] * 5 + [pltpu.VMEM((4, 64, 128), F32), pltpu.VMEM(face, F32)],
         specs=[SMEM],
         space=pltpu.VMEM,
@@ -791,7 +794,7 @@
         last_kernel,
         [(32, 8, 128), (32, 8, 128), (4, 64, 128)],
         [
-            place, far, near, mod, inv, u2, rims, inner, resp, sresp, sstate, smod,
+            odd, far, near, mod, inv, u2, rims, inner, resp, sresp, sstate, smod,
             d2, x0, x1, hot, base,
         ],
         [pltpu.VMEM(full, F32)] * 3
@@ -799,7 +802,7 @@
         specs=[SMEM],
     )
     sums = lax.all_gather(sums, "sub")
-    (kernel,) = call(project_kernel, [(64, 128)], [place, sums, stack], specs=[SMEM])
+    (kernel,) = call(project_kernel, [(64, 128)], [sub, sums, stack], specs=[SMEM])
     return from_tiles(out_u), from_tiles(out_w), kernel
 
 

time: 56 us -> 53.7 us (0.959)
  Pallas kernels: 9.64 us -> 7.49 us
    pallas_call x6, Pallas kernels: 9.64 us -> 7.49 us  [call(): pl.pallas_call(kernel, out_shape=outs, in_specs=specs, out_specs=[VMEM] *...]
where the time goes in v6:
time: 53.7 us; the launch traced here: 53.5 us
  starting transfers between devices  19.4 us (36%)
  blocking collectives  18.1 us (34%)
  waiting for transfers between devices  7.7 us (14%)
  Pallas kernels  7.49 us (14%)
  between operations  0.71 us (1%)
    ppermute x2, starting transfers between devices, swap_rows(): lax.ppermute(far, 'dom', far_pairs)  15.6 us
    all_gather x1, blocking collectives, on_device(): sums = lax.all_gather(sums, 'sub')  10.3 us
    all_gather x1, blocking collectives, on_device(): edges = lax.all_gather(edges, 'sub')  7.8 us
    pallas_call x6, Pallas kernels, call(): pl.pallas_call(kernel, out_shape=outs, in_specs=specs, out_specs=[VMEM] *...  7.49 us
    ppermute x2, waiting for transfers between devices, swap_rows(): lax.ppermute(far, 'dom', far_pairs)  4.26 us
    ppermute x2, starting transfers between devices, swap_rows(): lax.ppermute(near, 'dom', near_pairs)  3.84 us
    ppermute x2, waiting for transfers between devices, swap_rows(): lax.ppermute(near, 'dom', near_pairs)  3.44 us
  transfers between devices with their start and end apart: 4, of which 4 were waited for; matrix products, arithmetic and copies ran while one was open for 0% of the time, Pallas kernels for 1%

profile of v6, /device:TPU:25, one launch (start us, length us, event | category | flops | bytes accessed | tf_op | source)
XLA Modules:
  0.0 53.5 jit_solution(11903395059342098955)
XLA Ops:
  0.6 0.0 copy-start
  0.6 1.9 %shard_map.94 = (f32[2,64,128]{2,1,0:T(8,128)S(1)}, f32[95,8,128]{2,1,0:T(8,128)S(1)}, f32[160,8,128]{2,1,0:T(8,128)S(1)}) custom-call(f32[256,128]{1,0:T(8,128)} %bitcast.50, f32[256,128]{1,0:T(8,128)} %bitcast.51, f32[768,128]{1,0:T(8,128)} %bitcast.42, f32[256,128]{1,0:T(8,128)} %bitcast.52, s32[4,128]{1,0:T(4,128)} %bitcast.53, ...), custom_call_target="tpu_custom_call" | custom-call | tf_op jit(solution)/shard_map/pallas_call | solution.py:719
  2.6 7.8 %all-gather = f32[8,64,128]{2,1,0:T(8,128)S(1)} all-gather(f32[2,64,128]{2,1,0:T(8,128)S(1)} %get-tuple-element.31), channel_id=2, replica_groups=mesh['dom'=128,'sub'=4] {'sub'}, dimensions={0}, use_global_device_ids=true | all-gather | bytes 327680 | tf_op jit(solution)/shard_map/all_gather | solution.py:764
  10.4 0.0 copy-done
  10.4 0.7 %shard_map.95 = (f32[38,8,128]{2,1,0:T(8,128)S(1)}, f32[38,8,128]{2,1,0:T(8,128)S(1)}, f32[64,8,128]{2,1,0:T(8,128)S(1)}, f32[64,8,128]{2,1,0:T(8,128)S(1)}, f32...) custom-call(s32[1]{0:T(128)} %bitcast.odd_ref, s32[1]{0:T(128)} %bitcast.1.sub_ref, ...), custom_call_target="tpu_custom_call" | custom-call | tf_op jit(solution)/shard_map/pallas_call | solution.py:719
  11.1 12.2 %collective-permute-start = (f32[38,8,128]{2,1,0:T(8,128)S(1)}, f32[38,8,128]{2,1,0:T(8,128)S(1)}, u32[]{:S(2)}, u32[]{:S(2)}) collective-permute-start(f32[38,8,128]{2,1,0:T(8,128)S(1)} %get-tuple-element.34), channel_id=1, source_target_pairs={{4,8},{8,4},{12,16},{16,12},{20,24},{24,20},{28,32},{32,28},{36,40... | collective-permute-start | bytes 466952 | tf_op jit(solution)/shard_map/ppermute | solution.py:751
  23.3 1.9 %collective-permute-start.1 = (f32[38,8,128]{2,1,0:T(8,128)S(1)}, f32[38,8,128]{2,1,0:T(8,128)S(1)}, u32[]{:S(2)}, u32[]{:S(2)}) collective-permute-start(f32[38,8,128]{2,1,0:T(8,128)S(1)} %get-tuple-element.35), channel_id=1, source_target_pairs={{0,4},{4,0},{8,12},{12,8},{16,20},{20,16},{24,28},{28,24},{32,36},... | collective-permute-start | bytes 466952 | tf_op jit(solution)/shard_map/ppermute | solution.py:751
  25.2 2.3 %collective-permute-done.far_in = f32[38,8,128]{2,1,0:T(8,128)S(1)} collective-permute-done((f32[38,8,128]{2,1,0:T(8,128)S(1)}, f32[38,8,128]{2,1,0:T(8,128)S(1)}, u32[]{:S(2)}, u32[]{:S(2)}) %collective-permute-start) | collective-permute-done | bytes 155680 | tf_op jit(solution)/shard_map/ppermute | solution.py:751
  27.5 2.8 %collective-permute-done.1.near_in = f32[38,8,128]{2,1,0:T(8,128)S(1)} collective-permute-done((f32[38,8,128]{2,1,0:T(8,128)S(1)}, f32[38,8,128]{2,1,0:T(8,128)S(1)}, u32[]{:S(2)}, u32[]{:S(2)}) %collective-permute-start.1) | collective-permute-done | bytes 155680 | tf_op jit(solution)/shard_map/ppermute | solution.py:751
  30.4 0.0 copy-start.1
  30.4 1.6 %shard_map.96 = (f32[18,8,128]{2,1,0:T(8,128)S(1)}, f32[18,8,128]{2,1,0:T(8,128)S(1)}, f32[64,8,128]{2,1,0:T(8,128)S(1)}, f32[64,8,128]{2,1,0:T(8,128)S(1)}, f32...) custom-call(s32[1]{0:T(128)} %bitcast.odd_ref, ...), custom_call_target="tpu_custom_call" | custom-call | tf_op jit(solution)/shard_map/pallas_call | solution.py:719
  31.9 3.3 %collective-permute-start.2 = (f32[18,8,128]{2,1,0:T(8,128)S(1)}, f32[18,8,128]{2,1,0:T(8,128)S(1)}, u32[]{:S(2)}, u32[]{:S(2)}) collective-permute-start(f32[18,8,128]{2,1,0:T(8,128)S(1)} %get-tuple-element.41), channel_id=1, source_target_pairs={{4,8},{8,4},{12,16},{16,12},{20,24},{24,20},{28,32},{32,28},{36,40... | collective-permute-start | bytes 221192 | tf_op jit(solution)/shard_map/ppermute | solution.py:751
  35.2 1.9 %collective-permute-start.3 = (f32[18,8,128]{2,1,0:T(8,128)S(1)}, f32[18,8,128]{2,1,0:T(8,128)S(1)}, u32[]{:S(2)}, u32[]{:S(2)}) collective-permute-start(f32[18,8,128]{2,1,0:T(8,128)S(1)} %get-tuple-element.42), channel_id=1, source_target_pairs={{0,4},{4,0},{8,12},{12,8},{16,20},{20,16},{24,28},{28,24},{32,36},... | collective-permute-start | bytes 221192 | tf_op jit(solution)/shard_map/ppermute | solution.py:751
  37.2 0.0 copy-done.1
  37.2 0.1 copy.23
  37.3 0.8 %shard_map.97 = (f32[64,8,128]{2,1,0:T(8,128)S(1)}, f32[192,8,128]{2,1,0:T(8,128)S(1)}, f32[192,8,128]{2,1,0:T(8,128)S(1)}, bf16[512,512]{1,0:T(8,128)(2,1)S(1)}, bf16[64,384]{1,0:T(8,128)(2,1)S(1)}) custom-call(f32[96,8,128]{2,1,0:T(8,128)S(1)} %bitcast.45, f32[95,8,128]{2,1,0:T(8,128)S(1)} %get-tuple-element.32.base_ref, ...), custom_call_target="tpu_custom_call" | custom-call | tf_op jit(solution)/shard_map/pallas_call | solution.py:719
  38.1 2.0 %collective-permute-done.2.far_in = f32[18,8,128]{2,1,0:T(8,128)S(1)} collective-permute-done((f32[18,8,128]{2,1,0:T(8,128)S(1)}, f32[18,8,128]{2,1,0:T(8,128)S(1)}, u32[]{:S(2)}, u32[]{:S(2)}) %collective-permute-start.2) | collective-permute-done | bytes 73760 | tf_op jit(solution)/shard_map/ppermute | solution.py:751
  40.0 0.6 %collective-permute-done.3.near_in = f32[18,8,128]{2,1,0:T(8,128)S(1)} collective-permute-done((f32[18,8,128]{2,1,0:T(8,128)S(1)}, f32[18,8,128]{2,1,0:T(8,128)S(1)}, u32[]{:S(2)}, u32[]{:S(2)}) %collective-permute-start.3) | collective-permute-done | bytes 73760 | tf_op jit(solution)/shard_map/ppermute | solution.py:751
  40.6 1.8 %shard_map.98 = (f32[32,8,128]{2,1,0:T(8,128)}, f32[32,8,128]{2,1,0:T(8,128)}, f32[4,64,128]{2,1,0:T(8,128)S(1)}) custom-call(s32[1]{0:T(128)} %bitcast.odd_ref, f32[18,8,128]{2,1,0:T(8,128)S(1)} %collective-permute-done.2.far_in, f32[18,8,128]{2,1,0:T(8,128)S(1)} %collective-permute-done.3.near_in, f32[96,8,128]{2,1,0:T(8,128)S(1)} %bitcast.46, ...), custom_call_target="tpu_custom_call" | custom-call | tf_op jit(solution)/shard_map/pallas_call | solution.py:719
  42.4 10.3 %all-gather.1 = f32[16,64,128]{2,1,0:T(8,128)S(1)} all-gather(f32[4,64,128]{2,1,0:T(8,128)S(1)} %get-tuple-element.57), channel_id=3, replica_groups=mesh['dom'=128,'sub'=4] {'sub'}, dimensions={0}, use_global_device_ids=true | all-gather | bytes 655360 | tf_op jit(solution)/shard_map/all_gather | solution.py:804
  52.7 0.8 %shard_map.99 = f32[64,128]{1,0:T(8,128)} custom-call(s32[1]{0:T(128)} %bitcast.1.sub_ref, f32[4,4,64,128]{3,2,1,0:T(8,128)S(1)} %bitcast.47, bf16[64,384]{1,0:T(8,128)(2,1)S(1)} %get-tuple-element.58.stack_ref), custom_call_target="tpu_custom_call" | custom-call | tf_op jit(solution)/shard_map/pallas_call | solution.py:719
Async XLA Ops:
  0.6 9.7 %copy-start = (f32[3,64,2,256]{3,2,1,0:T(2,128)S(1)}, f32[3,64,2,256]{3,2,1,0:T(2,128)}, u32[]{:S(2)}) copy-start(f32[3,64,2,256]{3,2,1,0:T(2,128)} %param.9) | copy-start | bytes 1179652
  11.1 16.5 %collective-permute-start = (f32[38,8,128]{2,1,0:T(8,128)S(1)}, f32[38,8,128]{2,1,0:T(8,128)S(1)}, u32[]{:S(2)}, u32[]{:S(2)}) collective-permute-start(f32[38,8,128]{2,1,0:T(8,128)S(1)} %get-tuple-element.34), channel_id=1, source_target_pairs={{4,8},{8,4},{12,16},{16,12},{20,24},{24,20},{28,32},{32,28},{36,40... | collective-permute-start | bytes 466952 | tf_op jit(solution)/shard_map/ppermute | solution.py:751
  23.3 7.0 %collective-permute-start.1 = (f32[38,8,128]{2,1,0:T(8,128)S(1)}, f32[38,8,128]{2,1,0:T(8,128)S(1)}, u32[]{:S(2)}, u32[]{:S(2)}) collective-permute-start(f32[38,8,128]{2,1,0:T(8,128)S(1)} %get-tuple-element.35), channel_id=1, source_target_pairs={{0,4},{4,0},{8,12},{12,8},{16,20},{20,16},{24,28},{28,24},{32,36},... | collective-permute-start | bytes 466952 | tf_op jit(solution)/shard_map/ppermute | solution.py:751
  30.4 6.8 %copy-start.1 = (f32[64,64]{1,0:T(8,128)S(1)}, f32[64,64]{1,0:T(8,128)}, u32[]{:S(2)}) copy-start(f32[64,64]{1,0:T(8,128)} %param.12) | copy-start | bytes 49156
  31.9 8.1 %collective-permute-start.2 = (f32[18,8,128]{2,1,0:T(8,128)S(1)}, f32[18,8,128]{2,1,0:T(8,128)S(1)}, u32[]{:S(2)}, u32[]{:S(2)}) collective-permute-start(f32[18,8,128]{2,1,0:T(8,128)S(1)} %get-tuple-element.41), channel_id=1, source_target_pairs={{4,8},{8,4},{12,16},{16,12},{20,24},{24,20},{28,32},{32,28},{36,40... | collective-permute-start | bytes 221192 | tf_op jit(solution)/shard_map/ppermute | solution.py:751
  35.2 5.4 %collective-permute-start.3 = (f32[18,8,128]{2,1,0:T(8,128)S(1)}, f32[18,8,128]{2,1,0:T(8,128)S(1)}, u32[]{:S(2)}, u32[]{:S(2)}) collective-permute-start(f32[18,8,128]{2,1,0:T(8,128)S(1)} %get-tuple-element.42), channel_id=1, source_target_pairs={{0,4},{4,0},{8,12},{12,8},{16,20},{20,16},{24,28},{28,24},{32,36},... | collective-permute-start | bytes 221192 | tf_op jit(solution)/shard_map/ppermute | solution.py:751

commit v7 on v6

--- a/solution.py
+++ b/solution.py
@@ -626,7 +626,7 @@
     odd_ref, far_in, near_in, mod_ref, inv_ref, u2_ref, rims_ref, inner_ref, resp_ref,
     sresp_ref, sstate_ref, smod_ref, d2_ref, x0_ref, x1_ref, hot_ref, base_ref,
     out_u_ref, out_w_ref, sums_ref,
-    u, v, f, sx, beside, dens,
+    u, v, f, sx, beside, dens, finals, sems,
 ):
     cf_ref = base_ref.at[WEIGHTS:BASE]
     mk = masks()
@@ -672,6 +672,16 @@
         u[n] = u[n] + (v[n] - inv_ref[n] * total)
 
     assemble(lambda n: f[n], lambda q: beside[q], sx.at[1], mk, put3)
+    for p in range(32):
+        a, b = u[2 * p], u[2 * p + 1]
+        finals[0, p] = jnp.where(lo, a, rs(b, 4))
+        finals[1, p] = jnp.where(lo, rs(a, 4), b)
+    copies = [
+        pltpu.make_async_copy(finals.at[i], out, sems.at[i])
+        for i, out in enumerate((out_u_ref, out_w_ref))
+    ]
+    for c in copies:
+        c.start()
     for direction in (2, 1, 0):
         for a in range(4):
             for b in range(4):
@@ -689,10 +699,8 @@
     sums = res[0:64] + (res[64:128] + res[128:192])
     for q in range(4):
         sums_ref[q] = sums[:, 128 * q : 128 * q + 128]
-    for p in range(32):
-        a, b = u[2 * p], u[2 * p + 1]
-        out_u_ref[p] = jnp.where(lo, a, rs(b, 4))
-        out_w_ref[p] = jnp.where(lo, rs(a, 4), b)
+    for c in copies:
+        c.wait()
 
 
 def project_kernel(sub_ref, x_ref, stack_ref, out_ref):
@@ -711,7 +719,7 @@
 F32, BF16 = jnp.float32, jnp.bfloat16
 
 
-def call(kernel, outs, ins, scratch=(), specs=(), limit=24, space=None):
+def call(kernel, outs, ins, scratch=(), specs=(), limit=24, space=None, out_specs=()):
     specs = list(specs) + [VMEM] * (len(ins) - len(specs))
     outs = [o if isinstance(o, jax.ShapeDtypeStruct) else jax.ShapeDtypeStruct(o, F32) for o in outs]
     if space is not None:
@@ -720,7 +728,7 @@
         kernel,
         out_shape=outs,
         in_specs=specs,
-        out_specs=[VMEM] * len(outs),
+        out_specs=list(out_specs) + [VMEM] * (len(outs) - len(out_specs)),
         scratch_shapes=list(scratch),
         compiler_params=pltpu.CompilerParams(vmem_limit_bytes=limit * 1024 * 1024),
     )(*ins)
@@ -798,8 +806,10 @@
             d2, x0, x1, hot, base,
         ],
         [pltpu.VMEM(full, F32)] * 3
-        + [pltpu.VMEM((2, 64, 128), F32), pltpu.VMEM(face, F32), pltpu.VMEM((512, 128), F32)],
+        + [pltpu.VMEM((2, 64, 128), F32), pltpu.VMEM(face, F32), pltpu.VMEM((512, 128), F32)]
+        + [pltpu.VMEM((2, 32, 8, 128), F32), pltpu.SemaphoreType.DMA((2,))],
         specs=[SMEM],
+        out_specs=[HBM, HBM],
     )
     sums = lax.all_gather(sums, "sub")
     (kernel,) = call(project_kernel, [(64, 128)], [sub, sums, stack], specs=[SMEM])

time: 53.7 us -> 53.8 us (level)
  no operation moved by 1% of the time
where the time goes in v7:
time: 53.8 us; the launch traced here: 53.6 us
  starting transfers between devices  19.4 us (36%)
  blocking collectives  18.2 us (34%)
  waiting for transfers between devices  7.7 us (14%)
  Pallas kernels  7.55 us (14%)
  between operations  0.72 us (1%)
    ppermute x2, starting transfers between devices, swap_rows(): lax.ppermute(far, 'dom', far_pairs)  15.6 us
    all_gather x1, blocking collectives, on_device(): sums = lax.all_gather(sums, 'sub')  10.3 us
    all_gather x1, blocking collectives, on_device(): edges = lax.all_gather(edges, 'sub')  7.8 us
    pallas_call x6, Pallas kernels, call(): pl.pallas_call(kernel, out_shape=outs, in_specs=specs, out_specs=list(out...  7.55 us
    ppermute x2, waiting for transfers between devices, swap_rows(): lax.ppermute(far, 'dom', far_pairs)  4.26 us
    ppermute x2, starting transfers between devices, swap_rows(): lax.ppermute(near, 'dom', near_pairs)  3.84 us
    ppermute x2, waiting for transfers between devices, swap_rows(): lax.ppermute(near, 'dom', near_pairs)  3.44 us
  transfers between devices with their start and end apart: 4, of which 4 were waited for; matrix products, arithmetic and copies ran while one was open for 0% of the time, Pallas kernels for 1%

profile of v7, /device:TPU:25, one launch (start us, length us, event | category | flops | bytes accessed | tf_op | source)
XLA Modules:
  0.0 53.6 jit_solution(13550589261811722448)
XLA Ops:
  0.6 0.0 copy-start
  0.6 1.9 %shard_map.94 = (f32[2,64,128]{2,1,0:T(8,128)S(1)}, f32[95,8,128]{2,1,0:T(8,128)S(1)}, f32[160,8,128]{2,1,0:T(8,128)S(1)}) custom-call(f32[256,128]{1,0:T(8,128)} %bitcast.50, f32[256,128]{1,0:T(8,128)} %bitcast.51, f32[768,128]{1,0:T(8,128)} %bitcast.42, f32[256,128]{1,0:T(8,128)} %bitcast.52, s32[4,128]{1,0:T(4,128)} %bitcast.53, ...), custom_call_target="tpu_custom_call" | custom-call | tf_op jit(solution)/shard_map/pallas_call | solution.py:727
  2.6 7.8 %all-gather = f32[8,64,128]{2,1,0:T(8,128)S(1)} all-gather(f32[2,64,128]{2,1,0:T(8,128)S(1)} %get-tuple-element.31), channel_id=2, replica_groups=mesh['dom'=128,'sub'=4] {'sub'}, dimensions={0}, use_global_device_ids=true | all-gather | bytes 327680 | tf_op jit(solution)/shard_map/all_gather | solution.py:772
  10.4 0.0 copy-done
  10.4 0.7 %shard_map.95 = (f32[38,8,128]{2,1,0:T(8,128)S(1)}, f32[38,8,128]{2,1,0:T(8,128)S(1)}, f32[64,8,128]{2,1,0:T(8,128)S(1)}, f32[64,8,128]{2,1,0:T(8,128)S(1)}, f32...) custom-call(s32[1]{0:T(128)} %bitcast.odd_ref, s32[1]{0:T(128)} %bitcast.1.sub_ref, ...), custom_call_target="tpu_custom_call" | custom-call | tf_op jit(solution)/shard_map/pallas_call | solution.py:727
  11.1 12.2 %collective-permute-start = (f32[38,8,128]{2,1,0:T(8,128)S(1)}, f32[38,8,128]{2,1,0:T(8,128)S(1)}, u32[]{:S(2)}, u32[]{:S(2)}) collective-permute-start(f32[38,8,128]{2,1,0:T(8,128)S(1)} %get-tuple-element.34), channel_id=1, source_target_pairs={{4,8},{8,4},{12,16},{16,12},{20,24},{24,20},{28,32},{32,28},{36,40... | collective-permute-start | bytes 466952 | tf_op jit(solution)/shard_map/ppermute | solution.py:759
  23.3 1.9 %collective-permute-start.1 = (f32[38,8,128]{2,1,0:T(8,128)S(1)}, f32[38,8,128]{2,1,0:T(8,128)S(1)}, u32[]{:S(2)}, u32[]{:S(2)}) collective-permute-start(f32[38,8,128]{2,1,0:T(8,128)S(1)} %get-tuple-element.35), channel_id=1, source_target_pairs={{0,4},{4,0},{8,12},{12,8},{16,20},{20,16},{24,28},{28,24},{32,36},... | collective-permute-start | bytes 466952 | tf_op jit(solution)/shard_map/ppermute | solution.py:759
  25.2 2.3 %collective-permute-done.far_in = f32[38,8,128]{2,1,0:T(8,128)S(1)} collective-permute-done((f32[38,8,128]{2,1,0:T(8,128)S(1)}, f32[38,8,128]{2,1,0:T(8,128)S(1)}, u32[]{:S(2)}, u32[]{:S(2)}) %collective-permute-start) | collective-permute-done | bytes 155680 | tf_op jit(solution)/shard_map/ppermute | solution.py:759
  27.5 2.8 %collective-permute-done.1.near_in = f32[38,8,128]{2,1,0:T(8,128)S(1)} collective-permute-done((f32[38,8,128]{2,1,0:T(8,128)S(1)}, f32[38,8,128]{2,1,0:T(8,128)S(1)}, u32[]{:S(2)}, u32[]{:S(2)}) %collective-permute-start.1) | collective-permute-done | bytes 155680 | tf_op jit(solution)/shard_map/ppermute | solution.py:759
  30.4 0.0 copy-start.1
  30.4 1.6 %shard_map.96 = (f32[18,8,128]{2,1,0:T(8,128)S(1)}, f32[18,8,128]{2,1,0:T(8,128)S(1)}, f32[64,8,128]{2,1,0:T(8,128)S(1)}, f32[64,8,128]{2,1,0:T(8,128)S(1)}, f32...) custom-call(s32[1]{0:T(128)} %bitcast.odd_ref, ...), custom_call_target="tpu_custom_call" | custom-call | tf_op jit(solution)/shard_map/pallas_call | solution.py:727
  31.9 3.3 %collective-permute-start.2 = (f32[18,8,128]{2,1,0:T(8,128)S(1)}, f32[18,8,128]{2,1,0:T(8,128)S(1)}, u32[]{:S(2)}, u32[]{:S(2)}) collective-permute-start(f32[18,8,128]{2,1,0:T(8,128)S(1)} %get-tuple-element.41), channel_id=1, source_target_pairs={{4,8},{8,4},{12,16},{16,12},{20,24},{24,20},{28,32},{32,28},{36,40... | collective-permute-start | bytes 221192 | tf_op jit(solution)/shard_map/ppermute | solution.py:759
  35.2 1.9 %collective-permute-start.3 = (f32[18,8,128]{2,1,0:T(8,128)S(1)}, f32[18,8,128]{2,1,0:T(8,128)S(1)}, u32[]{:S(2)}, u32[]{:S(2)}) collective-permute-start(f32[18,8,128]{2,1,0:T(8,128)S(1)} %get-tuple-element.42), channel_id=1, source_target_pairs={{0,4},{4,0},{8,12},{12,8},{16,20},{20,16},{24,28},{28,24},{32,36},... | collective-permute-start | bytes 221192 | tf_op jit(solution)/shard_map/ppermute | solution.py:759
  37.2 0.0 copy-done.1
  37.2 0.1 copy.23
  37.3 0.8 %shard_map.97 = (f32[64,8,128]{2,1,0:T(8,128)S(1)}, f32[192,8,128]{2,1,0:T(8,128)S(1)}, f32[192,8,128]{2,1,0:T(8,128)S(1)}, bf16[512,512]{1,0:T(8,128)(2,1)S(1)}, bf16[64,384]{1,0:T(8,128)(2,1)S(1)}) custom-call(f32[96,8,128]{2,1,0:T(8,128)S(1)} %bitcast.45, f32[95,8,128]{2,1,0:T(8,128)S(1)} %get-tuple-element.32.base_ref, ...), custom_call_target="tpu_custom_call" | custom-call | tf_op jit(solution)/shard_map/pallas_call | solution.py:727
  38.1 2.0 %collective-permute-done.2.far_in = f32[18,8,128]{2,1,0:T(8,128)S(1)} collective-permute-done((f32[18,8,128]{2,1,0:T(8,128)S(1)}, f32[18,8,128]{2,1,0:T(8,128)S(1)}, u32[]{:S(2)}, u32[]{:S(2)}) %collective-permute-start.2) | collective-permute-done | bytes 73760 | tf_op jit(solution)/shard_map/ppermute | solution.py:759
  40.0 0.6 %collective-permute-done.3.near_in = f32[18,8,128]{2,1,0:T(8,128)S(1)} collective-permute-done((f32[18,8,128]{2,1,0:T(8,128)S(1)}, f32[18,8,128]{2,1,0:T(8,128)S(1)}, u32[]{:S(2)}, u32[]{:S(2)}) %collective-permute-start.3) | collective-permute-done | bytes 73760 | tf_op jit(solution)/shard_map/ppermute | solution.py:759
  40.6 1.8 %shard_map.98 = (f32[32,8,128]{2,1,0:T(8,128)}, f32[32,8,128]{2,1,0:T(8,128)}, f32[4,64,128]{2,1,0:T(8,128)S(1)}) custom-call(s32[1]{0:T(128)} %bitcast.odd_ref, f32[18,8,128]{2,1,0:T(8,128)S(1)} %collective-permute-done.2.far_in, f32[18,8,128]{2,1,0:T(8,128)S(1)} %collective-permute-done.3.near_in, f32[96,8,128]{2,1,0:T(8,128)S(1)} %bitcast.46, ...), custom_call_target="tpu_custom_call" | custom-call | tf_op jit(solution)/shard_map/pallas_call | solution.py:727
  42.5 10.3 %all-gather.1 = f32[16,64,128]{2,1,0:T(8,128)S(1)} all-gather(f32[4,64,128]{2,1,0:T(8,128)S(1)} %get-tuple-element.57), channel_id=3, replica_groups=mesh['dom'=128,'sub'=4] {'sub'}, dimensions={0}, use_global_device_ids=true | all-gather | bytes 655360 | tf_op jit(solution)/shard_map/all_gather | solution.py:814
  52.8 0.8 %shard_map.99 = f32[64,128]{1,0:T(8,128)} custom-call(s32[1]{0:T(128)} %bitcast.1.sub_ref, f32[4,4,64,128]{3,2,1,0:T(8,128)S(1)} %bitcast.47, bf16[64,384]{1,0:T(8,128)(2,1)S(1)} %get-tuple-element.58.stack_ref), custom_call_target="tpu_custom_call" | custom-call | tf_op jit(solution)/shard_map/pallas_call | solution.py:727
Async XLA Ops:
  0.6 9.7 %copy-start = (f32[3,64,2,256]{3,2,1,0:T(2,128)S(1)}, f32[3,64,2,256]{3,2,1,0:T(2,128)}, u32[]{:S(2)}) copy-start(f32[3,64,2,256]{3,2,1,0:T(2,128)} %param.9) | copy-start | bytes 1179652
  11.1 16.5 %collective-permute-start = (f32[38,8,128]{2,1,0:T(8,128)S(1)}, f32[38,8,128]{2,1,0:T(8,128)S(1)}, u32[]{:S(2)}, u32[]{:S(2)}) collective-permute-start(f32[38,8,128]{2,1,0:T(8,128)S(1)} %get-tuple-element.34), channel_id=1, source_target_pairs={{4,8},{8,4},{12,16},{16,12},{20,24},{24,20},{28,32},{32,28},{36,40... | collective-permute-start | bytes 466952 | tf_op jit(solution)/shard_map/ppermute | solution.py:759
  23.3 7.0 %collective-permute-start.1 = (f32[38,8,128]{2,1,0:T(8,128)S(1)}, f32[38,8,128]{2,1,0:T(8,128)S(1)}, u32[]{:S(2)}, u32[]{:S(2)}) collective-permute-start(f32[38,8,128]{2,1,0:T(8,128)S(1)} %get-tuple-element.35), channel_id=1, source_target_pairs={{0,4},{4,0},{8,12},{12,8},{16,20},{20,16},{24,28},{28,24},{32,36},... | collective-permute-start | bytes 466952 | tf_op jit(solution)/shard_map/ppermute | solution.py:759
  30.4 6.8 %copy-start.1 = (f32[64,64]{1,0:T(8,128)S(1)}, f32[64,64]{1,0:T(8,128)}, u32[]{:S(2)}) copy-start(f32[64,64]{1,0:T(8,128)} %param.12) | copy-start | bytes 49156
  31.9 8.1 %collective-permute-start.2 = (f32[18,8,128]{2,1,0:T(8,128)S(1)}, f32[18,8,128]{2,1,0:T(8,128)S(1)}, u32[]{:S(2)}, u32[]{:S(2)}) collective-permute-start(f32[18,8,128]{2,1,0:T(8,128)S(1)} %get-tuple-element.41), channel_id=1, source_target_pairs={{4,8},{8,4},{12,16},{16,12},{20,24},{24,20},{28,32},{32,28},{36,40... | collective-permute-start | bytes 221192 | tf_op jit(solution)/shard_map/ppermute | solution.py:759
  35.2 5.4 %collective-permute-start.3 = (f32[18,8,128]{2,1,0:T(8,128)S(1)}, f32[18,8,128]{2,1,0:T(8,128)S(1)}, u32[]{:S(2)}, u32[]{:S(2)}) collective-permute-start(f32[18,8,128]{2,1,0:T(8,128)S(1)} %get-tuple-element.42), channel_id=1, source_target_pairs={{0,4},{4,0},{8,12},{12,8},{16,20},{20,16},{24,28},{28,24},{32,36},... | collective-permute-start | bytes 221192 | tf_op jit(solution)/shard_map/ppermute | solution.py:759
